TPU v7x, 32 devices: a whole 2x2x4 slice. The times are simulated.
32 devices in a mesh: dp: 8 (over z, x), narrow: 4 (over y, core).
Axes of the slice: x: 2, y: 2, z: 4, core: 2. Of those that a mesh axis runs over, the one named last changes fastest.
Arguments:
- inputs: bfloat16 [32768, 768], P(('dp', 'narrow')), may hold values from -6 to 6
- segments: int32 [128, 256], P('dp'), may hold values from 0 to 3, as said below
- row_kind: int32 [128, 256], P('dp'), may hold values from 0 to 1, as said below
- query_weight: bfloat16 [768, 768], P('dp', 'narrow'), may hold values from -0.21875 to 0.21875
- query_bias: bfloat16 [768], P('dp'), may hold values from -1.75 to 1.75
- key_weight: bfloat16 [768, 768], P('dp', 'narrow'), may hold values from -0.21875 to 0.21875
- value_weight: bfloat16 [768, 768], P('dp', 'narrow'), may hold values from -0.21875 to 0.21875
- value_bias: bfloat16 [768], P('dp'), may hold values from -1.75 to 1.75
- output_weight: bfloat16 [768, 768], P('dp', 'narrow'), may hold values from -1.75 to 1.75
- output_bias: bfloat16 [768], P('dp'), may hold values from -1.75 to 1.75
- first_gain: bfloat16 [768], P('dp'), may hold values from 0.5 to 1.5
- first_shift: bfloat16 [768], P('dp'), may hold values from -1.75 to 1.75
- up_weight: bfloat16 [768, 3072], P('dp', 'narrow'), may hold values from -0.21875 to 0.21875
- up_bias: bfloat16 [3072], P('dp'), may hold values from -1.75 to 1.75
- down_weight: bfloat16 [3072, 768], P('dp', 'narrow'), may hold values from -0.21875 to 0.21875
- down_bias: bfloat16 [768], P('dp'), may hold values from -1.75 to 1.75
- second_gain: bfloat16 [768], P('dp'), may hold values from 0.5 to 1.5
- second_shift: bfloat16 [768], P('dp'), may hold values from -1.75 to 1.75
- out_cotangent: bfloat16 [32768, 768], P(('dp', 'narrow')), may hold values from -6 to 6
- loss_cotangent: float32 [128], P('dp'), may hold values from -131072 to 131072
Outputs:
- mixed: bfloat16 [32768, 768], P('dp')
- transport: float32 [128], P('dp')
- grad_inputs: float32 [32768, 768], P(('dp', 'narrow'))
- grad_query_weight: float32 [768, 768], P('dp', 'narrow')
- grad_query_bias: float32 [768], P('dp')
- grad_key_weight: float32 [768, 768], P('dp', 'narrow')
- grad_value_weight: float32 [768, 768], P('dp', 'narrow')
- grad_value_bias: float32 [768], P('dp')
- grad_output_weight: float32 [768, 768], P('dp', 'narrow')
- grad_output_bias: float32 [768], P('dp')
- grad_first_gain: float32 [768], P('dp')
- grad_first_shift: float32 [768], P('dp')
- grad_up_weight: float32 [768, 3072], P('dp', 'narrow')
- grad_up_bias: float32 [3072], P('dp')
- grad_down_weight: float32 [3072, 768], P('dp', 'narrow')
- grad_down_bias: float32 [768], P('dp')
- grad_second_gain: float32 [768], P('dp')
- grad_second_shift: float32 [768], P('dp')
Inputs may be any that keep to these rules, and one draw needn't show every extreme that they name: `segments`: along each packed sequence the segment number never falls; each segment is a run of a multiple of 16 rows; in every aligned group of 4 packed sequences one, drawn from the seed, is a single segment. `row_kind`: the first row of every segment is a word and its last row a region.
All inputs are finite; a program needn't handle non-finite values.
Results may differ from a plain program's by a relative error of at most 0.018.
The roundings to bfloat16 on the way count: a program that leaves them out, or rounds other values in their place, can miss the bound.
Values may be sent and summed in bfloat16 or wider, within the bound.
A program may use at most 192 MiB of HBM per device.

v0:
```python
import jax
import jax.numpy as jnp
from jax import lax
from jax.sharding import PartitionSpec as P

D = 768
HEADS = 12
HEAD_DIM = 64
LEN = 256
ITERS = 20


EPS_NORM = 1e-06
BETA = 0.5
MASKED = -1e30


def product(left, right):
    return jnp.dot(left, right, preferred_element_type=jnp.float32)


def product_left(left, right):
    return lax.dot_general(
        left, right, (((0,), (0,)), ((), ())), preferred_element_type=jnp.float32
    )


def product_right(left, right):
    return lax.dot_general(
        left, right, (((1,), (1,)), ((), ())), preferred_element_type=jnp.float32
    )


def layer_norm(values, gain, shift):
    centre = values - jnp.mean(values, axis=-1, keepdims=True)
    spread = jnp.mean(centre * centre, axis=-1, keepdims=True)
    recip = lax.rsqrt(spread + EPS_NORM)
    normed = centre * recip
    return (normed * gain + shift, normed, recip)


def norm_back(grad_out, normed, recip, gain):
    scaled = grad_out * gain
    inner_mean = jnp.mean(scaled, axis=-1, keepdims=True)
    cross_mean = jnp.mean(scaled * normed, axis=-1, keepdims=True)
    grad_in = recip * (scaled - inner_mean - normed * cross_mean)
    return (grad_in, jnp.sum(grad_out * normed, axis=0), jnp.sum(grad_out, axis=0))


def gelu_slope(values):
    normal_cdf = 0.5 * (1.0 + lax.erf(values * 0.7071067811865476))
    density = jnp.exp(-0.5 * values * values) * 0.3989422804014327
    return normal_cdf + values * density


def fetch_weights(matrices, vectors):
    wide = (
        lax.all_gather(matrices[0], "narrow", axis=1, tiled=True),
        lax.all_gather(matrices[1], "narrow", axis=1, tiled=True),
        lax.all_gather(matrices[2], "narrow", axis=1, tiled=True),
        lax.all_gather(matrices[3], "narrow", axis=1, tiled=True),
        lax.all_gather(matrices[4], "narrow", axis=1, tiled=True),
        lax.all_gather(matrices[5], "narrow", axis=1, tiled=True),
    )
    return (
        lax.all_gather(wide[0], "dp", axis=0, tiled=True),
        lax.all_gather(wide[1], "dp", axis=0, tiled=True),
        lax.all_gather(wide[2], "dp", axis=0, tiled=True),
        lax.all_gather(wide[3], "dp", axis=0, tiled=True),
        lax.all_gather(wide[4], "dp", axis=0, tiled=True),
        lax.all_gather(wide[5], "dp", axis=0, tiled=True),
        lax.all_gather(vectors[0], "dp", axis=0, tiled=True),
        lax.all_gather(vectors[1], "dp", axis=0, tiled=True),
        lax.all_gather(vectors[2], "dp", axis=0, tiled=True),
        lax.all_gather(vectors[3], "dp", axis=0, tiled=True),
        lax.all_gather(vectors[4], "dp", axis=0, tiled=True),
        lax.all_gather(vectors[5], "dp", axis=0, tiled=True),
        lax.all_gather(vectors[6], "dp", axis=0, tiled=True),
        lax.all_gather(vectors[7], "dp", axis=0, tiled=True),
        lax.all_gather(vectors[8], "dp", axis=0, tiled=True),
    )


def fetch_again(matrices, vectors):
    wide = (
        lax.all_gather(matrices[0], "narrow", axis=1, tiled=True),
        lax.all_gather(matrices[1], "narrow", axis=1, tiled=True),
        lax.all_gather(matrices[2], "narrow", axis=1, tiled=True),
        lax.all_gather(matrices[3], "narrow", axis=1, tiled=True),
        lax.all_gather(matrices[4], "narrow", axis=1, tiled=True),
        lax.all_gather(matrices[5], "narrow", axis=1, tiled=True),
    )
    return (
        lax.all_gather(wide[0], "dp", axis=0, tiled=True),
        lax.all_gather(wide[1], "dp", axis=0, tiled=True),
        lax.all_gather(wide[2], "dp", axis=0, tiled=True),
        lax.all_gather(wide[3], "dp", axis=0, tiled=True),
        lax.all_gather(wide[4], "dp", axis=0, tiled=True),
        lax.all_gather(wide[5], "dp", axis=0, tiled=True),
        lax.all_gather(vectors[0], "dp", axis=0, tiled=True),
        lax.all_gather(vectors[1], "dp", axis=0, tiled=True),
        lax.all_gather(vectors[2], "dp", axis=0, tiled=True),
        lax.all_gather(vectors[3], "dp", axis=0, tiled=True),
        lax.all_gather(vectors[4], "dp", axis=0, tiled=True),
        lax.all_gather(vectors[5], "dp", axis=0, tiled=True),
        lax.all_gather(vectors[6], "dp", axis=0, tiled=True),
        lax.all_gather(vectors[7], "dp", axis=0, tiled=True),
        lax.all_gather(vectors[8], "dp", axis=0, tiled=True),
    )


def normalize(feats):
    feat_float = feats.astype(jnp.float32)
    recip = lax.rsqrt(jnp.sum(feat_float * feat_float, axis=-1, keepdims=True) + EPS_NORM)
    return (feat_float * recip, recip)


def transport(unit_low, seg_rows, kind_rows, weight, row_total, back_total):
    word_rows = (kind_rows == 0).astype(jnp.float32)
    region_rows = 1.0 - word_rows
    cosine = jnp.einsum("bjd,bid->bji", unit_low, unit_low, preferred_element_type=jnp.float32)
    costs = 1.0 - cosine
    paired = (seg_rows[:, :, None] == seg_rows[:, None, :]).astype(jnp.float32)
    word_count = jnp.sum(paired * word_rows[:, None, :], axis=2)
    same_segment = (seg_rows[:, :, None] == seg_rows[:, None, :]).astype(jnp.float32)
    region_count = jnp.sum(same_segment * region_rows[:, None, :], axis=2)
    kernel = jnp.exp(-costs / BETA) * same_segment * word_rows[:, None, :] * region_rows[:, :, None]
    sigma_start = region_rows / region_count

    def advance(carry, unused):
        coupling, sigma_cols = carry
        weighted = kernel * coupling
        row_sum = row_total(jnp.sum(weighted * sigma_cols[:, :, None], axis=1))
        delta_rows = word_rows / (word_count * row_sum + 1.0 - word_rows)
        col_sum = jnp.sum(weighted * delta_rows[:, None, :], axis=2)
        sigma_next = region_rows / (region_count * col_sum + 1.0 - region_rows)
        coupling_next = delta_rows[:, None, :] * weighted * sigma_next[:, :, None]
        return (
            (coupling_next, sigma_next),
            (coupling, weighted, sigma_cols, delta_rows, sigma_next, row_sum, col_sum),
        )

    (coupling, sigma_last), stored = lax.scan(
        advance, (jnp.ones_like(kernel), sigma_start), None, length=ITERS
    )
    partial_value = jnp.sum(coupling * costs, axis=(1, 2))

    def retreat(carry, saved):
        d_coupling, d_sigma, d_kernel = carry
        coupling_prev, weighted, sigma_prev, delta_rows, sigma_now, row_sum, col_sum = saved
        d_weighted = d_coupling * delta_rows[:, None, :] * sigma_now[:, :, None]
        d_delta = jnp.sum(d_coupling * weighted * sigma_now[:, :, None], axis=1)
        d_sigma = d_sigma + jnp.sum(d_coupling * weighted * delta_rows[:, None, :], axis=2)
        col_denom = region_count * col_sum + 1.0 - region_rows
        d_column = -d_sigma * region_rows * region_count / (col_denom * col_denom)
        d_weighted = d_weighted + delta_rows[:, None, :] * d_column[:, :, None]
        d_delta = back_total(d_delta + jnp.sum(weighted * d_column[:, :, None], axis=1))
        row_denom = word_count * row_sum + 1.0 - word_rows
        d_rowsum = -d_delta * word_rows * word_count / (row_denom * row_denom)
        d_weighted = d_weighted + d_rowsum[:, None, :] * sigma_prev[:, :, None]
        d_sigma_prev = jnp.sum(weighted * d_rowsum[:, None, :], axis=2)
        return ((d_weighted * kernel, d_sigma_prev, d_kernel + d_weighted * coupling_prev), None)

    start_carry = (
        weight[:, None, None] * costs,
        jnp.zeros_like(sigma_last),
        jnp.zeros_like(kernel),
    )
    (unused_coupling, unused_sigma, d_kernel), unused = lax.scan(
        retreat, start_carry, stored, reverse=True
    )
    d_cost = weight[:, None, None] * coupling - d_kernel * kernel / BETA
    d_cosine = (-d_cost).astype(jnp.bfloat16)
    d_rows = jnp.einsum("bji,bjd->bid", d_cosine, unit_low, preferred_element_type=jnp.float32)
    d_cols = jnp.einsum("bji,bid->bjd", d_cosine, unit_low, preferred_element_type=jnp.float32)
    return (partial_value, d_rows + d_cols)


def per_device(
    inputs,
    segments,
    row_kind,
    query_weight,
    query_bias,
    key_weight,
    value_weight,
    value_bias,
    output_weight,
    output_bias,
    first_gain,
    first_shift,
    up_weight,
    up_bias,
    down_weight,
    down_bias,
    second_gain,
    second_shift,
    out_cotangent,
    loss_cotangent,
):
    pack_count = inputs.shape[0] // LEN
    row_count = inputs.shape[0]
    position = lax.axis_index("narrow")
    own_seg = lax.dynamic_slice_in_dim(segments, position * pack_count, pack_count, 0)
    matrices = (query_weight, key_weight, value_weight, output_weight, up_weight, down_weight)
    vectors = (
        query_bias,
        value_bias,
        output_bias,
        first_gain,
        first_shift,
        up_bias,
        down_bias,
        second_gain,
        second_shift,
    )
    gathered = fetch_weights(matrices, vectors)
    w_query, w_key, w_value, w_output, w_up, w_down = gathered[0:6]
    b_query, b_value, b_output, g_first, s_first, b_up, b_down, g_second, s_second = [
        item.astype(jnp.float32) for item in gathered[6:15]
    ]
    shape_heads = (pack_count, LEN, HEADS, HEAD_DIM)
    scale = HEAD_DIM ** (-0.5)
    query_low = (product(inputs, w_query) + b_query).astype(jnp.bfloat16)
    key_low = product(inputs, w_key).astype(jnp.bfloat16)
    value_low = (product(inputs, w_value) + b_value).astype(jnp.bfloat16)
    query_heads = query_low.reshape(shape_heads)
    key_heads = key_low.reshape(shape_heads)
    value_heads = value_low.reshape(shape_heads)
    paired = own_seg[:, None, :, None] == own_seg[:, None, None, :]

    def attention_scores():
        raw = jnp.einsum(
            "plhe,pmhe->phlm", query_heads, key_heads, preferred_element_type=jnp.float32
        )
        return jnp.where(paired, raw * scale, MASKED)

    scores = attention_scores()
    highest = jnp.max(scores, axis=-1, keepdims=True)
    shifted = jnp.exp(scores - highest)
    denominator = jnp.sum(shifted, axis=-1, keepdims=True)
    probability_low = (shifted / denominator).astype(jnp.bfloat16)
    log_total = highest + jnp.log(denominator)
    context_low = (
        jnp.einsum(
            "phlm,pmhe->plhe", probability_low, value_heads, preferred_element_type=jnp.float32
        )
        .reshape(row_count, D)
        .astype(jnp.bfloat16)
    )
    rows_float = inputs.astype(jnp.float32)
    attended = product(context_low, w_output) + b_output
    first, normed_first, recip_first = layer_norm(rows_float + attended, g_first, s_first)
    first_low = first.astype(jnp.bfloat16)
    inner = product(first_low, w_up) + b_up
    active_low = jax.nn.gelu(inner, approximate=False).astype(jnp.bfloat16)
    branch = product(active_low, w_down) + b_down
    output, normed_second, recip_second = layer_norm(first + branch, g_second, s_second)
    output_low = output.astype(jnp.bfloat16)
    group_out = lax.all_gather(output_low, "narrow", axis=0, tiled=True)
    own_unit, own_recip = normalize(output_low.reshape(pack_count, LEN, D))
    own_kind = lax.dynamic_slice_in_dim(row_kind, position * pack_count, pack_count, 0)
    own_weight = lax.dynamic_slice_in_dim(loss_cotangent, position * pack_count, pack_count, 0)

    def row_total(values):
        return values

    partial_value, d_unit = transport(
        own_unit.astype(jnp.bfloat16), own_seg, own_kind, own_weight, row_total, row_total
    )
    transport_loss = lax.all_gather(partial_value, "narrow", axis=0, tiled=True)
    d_unit_own = d_unit.reshape(row_count, D)
    own_unit = own_unit.reshape(row_count, D)
    own_recip = own_recip.reshape(row_count, 1)
    d_output = out_cotangent.astype(jnp.float32) + own_recip * (
        d_unit_own - own_unit * jnp.sum(d_unit_own * own_unit, axis=-1, keepdims=True)
    )
    again = fetch_again(matrices, vectors)
    w_query, w_key, w_value, w_output, w_up, w_down = again[0:6]
    g_first = again[9].astype(jnp.float32)
    g_second = again[13].astype(jnp.float32)
    d_second, grad_second_gain, grad_second_shift = norm_back(
        d_output, normed_second, recip_second, g_second
    )
    d_branch = d_second.astype(jnp.bfloat16)
    grad_down_bias = jnp.sum(d_branch.astype(jnp.float32), axis=0)
    grad_down_weight = product_left(active_low, d_branch)
    d_inner = (product_right(d_branch, w_down) * gelu_slope(inner)).astype(jnp.bfloat16)
    grad_up_bias = jnp.sum(d_inner.astype(jnp.float32), axis=0)
    grad_up_weight = product_left(first_low, d_inner)
    d_first = d_second + product_right(d_inner, w_up)
    d_sum_first, grad_first_gain, grad_first_shift = norm_back(
        d_first, normed_first, recip_first, g_first
    )
    d_attended = d_sum_first.astype(jnp.bfloat16)
    grad_output_bias = jnp.sum(d_attended.astype(jnp.float32), axis=0)
    grad_output_weight = product_left(context_low, d_attended)
    d_context = product_right(d_attended, w_output).astype(jnp.bfloat16).reshape(shape_heads)
    probability = jnp.exp(attention_scores() - log_total)
    prob_again = probability.astype(jnp.bfloat16)
    d_values = (
        jnp.einsum("phlm,plhe->pmhe", prob_again, d_context, preferred_element_type=jnp.float32)
        .astype(jnp.bfloat16)
        .reshape(row_count, D)
    )
    d_probability = jnp.einsum(
        "plhe,pmhe->phlm", d_context, value_heads, preferred_element_type=jnp.float32
    )
    d_scores = (
        probability * (d_probability - jnp.sum(probability * d_probability, axis=-1, keepdims=True))
    ).astype(jnp.bfloat16)
    d_query = (
        (
            jnp.einsum("phlm,pmhe->plhe", d_scores, key_heads, preferred_element_type=jnp.float32)
            * scale
        )
        .astype(jnp.bfloat16)
        .reshape(row_count, D)
    )
    d_keys = (
        (
            jnp.einsum("phlm,plhe->pmhe", d_scores, query_heads, preferred_element_type=jnp.float32)
            * scale
        )
        .astype(jnp.bfloat16)
        .reshape(row_count, D)
    )
    grad_query_weight = product_left(inputs, d_query)
    grad_query_bias = jnp.sum(d_query.astype(jnp.float32), axis=0)
    grad_key_weight = product_left(inputs, d_keys)
    grad_value_weight = product_left(inputs, d_values)
    grad_value_bias = jnp.sum(d_values.astype(jnp.float32), axis=0)
    grad_inputs = (
        d_sum_first
        + product_right(d_query, w_query)
        + product_right(d_keys, w_key)
        + product_right(d_values, w_value)
    )
    reduced = (
        lax.psum_scatter(grad_query_weight, "dp", scatter_dimension=0, tiled=True),
        lax.psum_scatter(grad_key_weight, "dp", scatter_dimension=0, tiled=True),
        lax.psum_scatter(grad_value_weight, "dp", scatter_dimension=0, tiled=True),
        lax.psum_scatter(grad_output_weight, "dp", scatter_dimension=0, tiled=True),
        lax.psum_scatter(grad_up_weight, "dp", scatter_dimension=0, tiled=True),
        lax.psum_scatter(grad_down_weight, "dp", scatter_dimension=0, tiled=True),
        lax.psum_scatter(grad_query_bias, "dp", scatter_dimension=0, tiled=True),
        lax.psum_scatter(grad_value_bias, "dp", scatter_dimension=0, tiled=True),
        lax.psum_scatter(grad_output_bias, "dp", scatter_dimension=0, tiled=True),
        lax.psum_scatter(grad_first_gain, "dp", scatter_dimension=0, tiled=True),
        lax.psum_scatter(grad_first_shift, "dp", scatter_dimension=0, tiled=True),
        lax.psum_scatter(grad_up_bias, "dp", scatter_dimension=0, tiled=True),
        lax.psum_scatter(grad_down_bias, "dp", scatter_dimension=0, tiled=True),
        lax.psum_scatter(grad_second_gain, "dp", scatter_dimension=0, tiled=True),
        lax.psum_scatter(grad_second_shift, "dp", scatter_dimension=0, tiled=True),
    )
    mats = (
        lax.psum_scatter(
            reduced[0].astype(jnp.bfloat16), "narrow", scatter_dimension=1, tiled=True
        ).astype(jnp.float32),
        lax.psum_scatter(
            reduced[1].astype(jnp.bfloat16), "narrow", scatter_dimension=1, tiled=True
        ).astype(jnp.float32),
        lax.psum_scatter(
            reduced[2].astype(jnp.bfloat16), "narrow", scatter_dimension=1, tiled=True
        ).astype(jnp.float32),
        lax.psum_scatter(
            reduced[3].astype(jnp.bfloat16), "narrow", scatter_dimension=1, tiled=True
        ).astype(jnp.float32),
        lax.psum_scatter(
            reduced[4].astype(jnp.bfloat16), "narrow", scatter_dimension=1, tiled=True
        ).astype(jnp.float32),
        lax.psum_scatter(
            reduced[5].astype(jnp.bfloat16), "narrow", scatter_dimension=1, tiled=True
        ).astype(jnp.float32),
    )
    vecs = lax.psum(
        (
            reduced[6],
            reduced[7],
            reduced[8],
            reduced[9],
            reduced[10],
            reduced[11],
            reduced[12],
            reduced[13],
            reduced[14],
        ),
        "narrow",
    )
    return (
        group_out,
        transport_loss,
        grad_inputs,
        mats[0],
        vecs[0],
        mats[1],
        mats[2],
        vecs[1],
        mats[3],
        vecs[2],
        vecs[3],
        vecs[4],
        mats[4],
        vecs[5],
        mats[5],
        vecs[6],
        vecs[7],
        vecs[8],
    )


def solution(mesh):
    return jax.shard_map(
        per_device,
        mesh=mesh,
        in_specs=(
            P(("dp", "narrow"), None),
            P("dp", None),
            P("dp", None),
            P("dp", "narrow"),
            P("dp"),
            P("dp", "narrow"),
            P("dp", "narrow"),
            P("dp"),
            P("dp", "narrow"),
            P("dp"),
            P("dp"),
            P("dp"),
            P("dp", "narrow"),
            P("dp"),
            P("dp", "narrow"),
            P("dp"),
            P("dp"),
            P("dp"),
            P(("dp", "narrow"), None),
            P("dp"),
        ),
        out_specs=(
            P("dp", None),
            P("dp"),
            P(("dp", "narrow"), None),
            P("dp", "narrow"),
            P("dp"),
            P("dp", "narrow"),
            P("dp", "narrow"),
            P("dp"),
            P("dp", "narrow"),
            P("dp"),
            P("dp"),
            P("dp"),
            P("dp", "narrow"),
            P("dp"),
            P("dp", "narrow"),
            P("dp"),
            P("dp"),
            P("dp"),
        ),
        check_vma=False,
    )
```

profile of v0, /device:TPU:0, one launch (start us, length us, event | category | flops | bytes accessed | tf_op | source)
XLA Modules:
  0.0 1431.1 jit_solution(8593180012447737193)
XLA Ops:
  8.3 6.9 all_gather.86
  17.0 5.6 all_gather.89
  24.4 5.6 all_gather.83
  31.8 5.6 all_gather.91
  38.3 8.2 all_gather.96
  46.5 8.1 all_gather.99
  58.0 37.7 %all-reduce.20 = (bf16[768]{0:T(1024)(128)(2,1)S(1)}, bf16[768]{0:T(1024)(128)(2,1)S(1)}, bf16[768]{0:T(1024)(128)(2,1)S(1)}, bf16[768]{0:T(1024)(128)(2,1)S(1)}...) all-reduce(bf16[768]{0:T(1024)(128)(2,1)S(1)} %dynamic-update-slice, ...), channel_id=1, replica_groups=mesh['dp'=8,'narrow'=4] {'dp'}, use_global_device_ids=true, to_apply=%add.1 | all-reduce | flops 6144 | bytes 24576
  96.4 26.0 %all-gather = bf16[8,1,384]{2,1,0:T(2,128)(2,1)S(1)} all-gather(bf16[1,1,384]{2,1,0:T(2,128)(2,1)S(1)} %reshape.315), channel_id=1, replica_groups=mesh['dp'=8,'narrow'=4] {'dp'}, dimensions={0}, use_global_device_ids=true | all-gather | bytes 6912 | tf_op jit(solution)/shard_map/all_gather | solution.py:77
  123.3 4.3 add_convert_fusion.1
  132.1 4.3 convolution_convert_fusion.1
  140.5 3.6 all-gather.9.cloned.1.call-done
  151.8 4.9 fusion.38
  161.5 3.6 fusion.47
  166.7 19.3 %all-gather.15.cloned.1.call-done = bf16[768,768]{1,0:T(8,128)(2,1)} async-done(((bf16[96,768]{1,0:T(8,128)(2,1)}), bf16[768,768]{1,0:T(8,128)(2,1)}) %all-gather.15.cloned.1.call-update) | async-done | bytes 1179664 | tf_op jit(solution)/shard_map/all_gather | solution.py:69
  186.0 3.4 fusion.82
  191.7 75.1 %all-gather.17.cloned.1.call-done = bf16[768,3072]{1,0:T(8,128)(2,1)} async-done(((bf16[96,3072]{1,0:T(8,128)(2,1)}), bf16[768,3072]{1,0:T(8,128)(2,1)}) %all-gather.17.cloned.1.call-update) | async-done | bytes 4718608 | tf_op jit(solution)/shard_map/all_gather | solution.py:70
  266.7 37.2 %fusion.18 = (bf16[1024,3072]{1,0:T(8,128)(2,1)}, f32[1024,3072]{1,0:T(8,128)}) fusion(f32[3072]{0:T(1024)S(1)} %bitcast.208, bf16[768,3072]{1,0:T(8,128)(2,1)} %all-gather.17.cloned.1.call-done, f32[1024,768]{1,0:T(8,128)} %copy-done.7, f32[768]{0:T(1024)S(1)} %convert_element_type.187, f32[768]{0:T(1024)S(1)} %convert_element_type.186, ...), kind=kOutput, calls=%fused_computation.47 | convolution fusion | flops 5043388416 | bytes 26765312 | tf_op jit(solution)/shard_map/dot_general | solution.py:19
  303.9 43.9 %all-gather.19.cloned.1.call-done = bf16[3072,768]{0,1:T(8,128)(2,1)} async-done(((bf16[384,768]{0,1:T(8,128)(2,1)}), bf16[3072,768]{0,1:T(8,128)(2,1)}) %all-gather.19.cloned.1.call-update) | async-done | bytes 4718608 | tf_op jit(solution)/shard_map/all_gather | solution.py:71
  347.8 9.6 fusion.83
  360.1 4.2 broadcast_multiply_fusion
  364.3 71.2 %while.46 = (s32[]{:T(128)}, f32[4,256,256]{2,1,0:T(8,128)S(1)}, f32[4,256]{1,0:T(4,128)S(1)}, f32[20,4,256,256]{3,2,1,0:T(8,128)}, f32[20,4,256,256]{3,2,1,0:T(...) while((s32[]{:T(128)}, f32[4,256,256]{2,1,0:T(8,128)S(1)}, ...), condition=%wide.region_12.13_spmd.clone, body=%wide.region_9.12_spmd.clone.sunk | while | flops 2111491 | bytes 9545383 | solution.py:143
  435.5 145.2 %while.47 = (s32[]{:T(128)}, f32[4,256,256]{2,1,0:T(8,128)S(1)}, f32[4,256]{1,0:T(4,128)S(1)}, f32[4,256,256]{2,1,0:T(8,128)}, f32[20,4,256]{2,1,0:T(4,128)S(1)}...) while((s32[]{:T(128)}, f32[4,256,256]{2,1,0:T(8,128)S(1)}, ...), condition=%wide.region_19.20_spmd.clone, body=%wide.region_14.19_spmd.clone.sunk | while | flops 4995076 | bytes 10608863 | solution.py:169
  446.3 3.5 fusion.128
  453.6 3.5 fusion.128
  460.8 3.5 fusion.128
  468.1 3.5 fusion.128
  475.4 3.5 fusion.128
  482.6 3.5 fusion.128
  489.9 3.5 fusion.128
  497.2 3.5 fusion.128
  504.5 3.5 fusion.128
  511.8 3.5 fusion.128
  519.1 3.5 fusion.128
  526.3 3.5 fusion.128
  533.6 3.5 fusion.128
  540.9 3.5 fusion.128
  548.1 3.5 fusion.128
  555.4 3.5 fusion.128
  562.7 3.5 fusion.128
  569.9 3.5 fusion.128
  577.2 3.5 fusion.128
  590.9 13.8 convert_reduce_fusion
  604.7 6.0 multiply_reduce_fusion.6
  616.5 4.9 convolution_convert_fusion
  624.2 3.9 reshape.283
  628.1 9.9 multiply_reduce_fusion.4
  637.9 7.2 multiply_convert_fusion
  656.8 8.4 convert_reduce_fusion.3
  673.8 4.6 convert_reduce_fusion.4
  687.5 10.3 fusion.67
  697.9 10.7 fusion.75
  710.5 44.8 %reduce-scatter.39.cloned.1.call-done = f32[96,768]{1,0:T(8,128)} async-done(((f32[768,768]{1,0:T(8,128)}), f32[96,768]{1,0:T(8,128)}) %reduce-scatter.39.cloned.1.call-update) | async-done | bytes 294928
  757.2 69.6 %reduce-scatter.41.cloned.1.call-done = f32[96,768]{1,0:T(8,128)} async-done(((f32[768,768]{1,0:T(8,128)}), f32[96,768]{1,0:T(8,128)}) %reduce-scatter.41.cloned.1.call-update) | async-done | bytes 294928
  828.7 69.5 %reduce-scatter.37.cloned.1.call-done = f32[96,768]{1,0:T(8,128)} async-done(((f32[768,768]{1,0:T(8,128)}), f32[96,768]{1,0:T(8,128)}) %reduce-scatter.37.cloned.1.call-update) | async-done | bytes 294928
  900.6 163.7 %reduce-scatter.35.cloned.1.call-done = f32[384,768]{1,0:T(8,128)} async-done(((f32[3072,768]{1,0:T(8,128)}), f32[384,768]{1,0:T(8,128)}) %reduce-scatter.35.cloned.1.call-update) | async-done | bytes 1179664 | tf_op jit(solution)/shard_map/reduce_scatter | solution.py:345
  1069.3 161.0 %reduce-scatter.31.cloned.1.call-done = f32[96,3072]{1,0:T(8,128)} async-done(((f32[768,3072]{1,0:T(8,128)}), f32[96,3072]{1,0:T(8,128)}) %reduce-scatter.31.cloned.1.call-update) | async-done | bytes 1179664 | tf_op jit(solution)/shard_map/reduce_scatter | solution.py:344
  1235.8 35.6 %all-reduce.18 = (f32[768]{0:T(1024)S(1)}, f32[768]{0:T(1024)S(1)}, f32[768]{0:T(1024)S(1)}, f32[768]{0:T(1024)S(1)}, f32[768]{0:T(1024)S(1)}, /*index=5*/f32[30...) all-reduce(f32[768]{0:T(1024)S(1)} %reduce_sum.318, ...), channel_id=4, replica_groups=mesh['dp'=8,'narrow'=4] {'dp'}, use_global_device_ids=true, to_apply=%region_29.30.clone | all-reduce | flops 9216 | bytes 73728
  1272.3 6.6 all-reduce.19
  1288.7 7.7 reduce-scatter.27.cloned.1.call-done
  1298.0 21.1 %reduce-scatter.23.cloned.1.call-done = bf16[96,192]{0,1:T(8,128)(2,1)} async-done(((bf16[96,768]{0,1:T(8,128)(2,1)}), bf16[96,192]{0,1:T(8,128)(2,1)}) %reduce-scatter.23.cloned.1.call-update) | async-done | bytes 36880 | tf_op jit(solution)/shard_map/reduce_scatter | solution.py:357
  1320.6 46.3 %all-gather.21.cloned.1.call-done = bf16[4096,768]{1,0:T(8,128)(2,1)} async-done(((bf16[1024,768]{1,0:T(8,128)(2,1)}), bf16[4096,768]{1,0:T(8,128)(2,1)}) %all-gather.21.cloned.1.call-update) | async-done | bytes 6291472 | tf_op jit(solution)/shard_map/all_gather | solution.py:260
  1366.9 24.5 %reduce-scatter.45.cloned.1.call-done = bf16[192,384]{1,0:T(8,128)(2,1)} async-done(((bf16[768,384]{1,0:T(8,128)(2,1)}), bf16[192,384]{1,0:T(8,128)(2,1)}) %reduce-scatter.45.cloned.1.call-update) | async-done | bytes 147472
  1393.2 23.3 %reduce-scatter.33.cloned.1.call-done = bf16[96,768]{1,0:T(8,128)(2,1)} async-done(((bf16[96,3072]{1,0:T(8,128)(2,1)}), bf16[96,768]{1,0:T(8,128)(2,1)}) %reduce-scatter.33.cloned.1.call-update) | async-done | bytes 147472 | tf_op jit(solution)/shard_map/reduce_scatter | solution.py:369
  1418.2 5.9 copy.252
  (555 shorter events, 269.5 us)
Async XLA Ops:
  7.2 88.5 %copy-start = (s32[16,256]{1,0:T(8,128)S(1)}, s32[16,256]{1,0:T(8,128)}, u32[]{:S(2)}) copy-start(s32[16,256]{1,0:T(8,128)} %param.25) | copy-start | bytes 49156
  7.2 47.6 %copy-start.31 = (u32[32]{0:T(128)S(1)}, u32[32]{0:T(128)}, u32[]{:S(2)}) copy-start(u32[32]{0:T(128)} %constant.186) | copy-start | bytes 388
  7.2 31.0 %copy-start.29 = (bf16[96,768]{1,0:T(8,128)(2,1)S(1)}, bf16[96,768]{1,0:T(8,128)(2,1)}, u32[]{:S(2)}) copy-start(bf16[96,768]{1,0:T(8,128)(2,1)} %param.36) | copy-start | bytes 442372
  7.2 39.3 %copy-start.30 = (bf16[384,192]{0,1:T(8,128)(2,1)S(1)}, bf16[384,192]{0,1:T(8,128)(2,1)}, u32[]{:S(2)}) copy-start(bf16[384,192]{0,1:T(8,128)(2,1)} %param.38) | copy-start | bytes 442372
  7.2 48.9 %copy-start.36 = (bf16[96]{0:T(256)(128)(2,1)S(1)}, bf16[96]{0:T(256)(128)(2,1)}, u32[]{:S(2)}) copy-start(bf16[96]{0:T(256)(128)(2,1)} %param.31) | copy-start | bytes 580
  7.3 49.1 %copy-start.37 = (bf16[96]{0:T(256)(128)(2,1)S(1)}, bf16[96]{0:T(256)(128)(2,1)}, u32[]{:S(2)}) copy-start(bf16[96]{0:T(256)(128)(2,1)} %param.28) | copy-start | bytes 580
  7.3 49.3 %copy-start.38 = (bf16[96]{0:T(256)(128)(2,1)S(1)}, bf16[96]{0:T(256)(128)(2,1)}, u32[]{:S(2)}) copy-start(bf16[96]{0:T(256)(128)(2,1)} %param.33) | copy-start | bytes 580
  7.3 49.5 %copy-start.39 = (bf16[96]{0:T(256)(128)(2,1)S(1)}, bf16[96]{0:T(256)(128)(2,1)}, u32[]{:S(2)}) copy-start(bf16[96]{0:T(256)(128)(2,1)} %param.34) | copy-start | bytes 580
  7.3 49.8 %copy-start.40 = (bf16[96]{0:T(256)(128)(2,1)S(1)}, bf16[96]{0:T(256)(128)(2,1)}, u32[]{:S(2)}) copy-start(bf16[96]{0:T(256)(128)(2,1)} %param.35) | copy-start | bytes 580
  7.3 50.0 %copy-start.41 = (bf16[96]{0:T(256)(128)(2,1)S(1)}, bf16[96]{0:T(256)(128)(2,1)}, u32[]{:S(2)}) copy-start(bf16[96]{0:T(256)(128)(2,1)} %param.39) | copy-start | bytes 580
  7.3 50.2 %copy-start.42 = (bf16[96]{0:T(256)(128)(2,1)S(1)}, bf16[96]{0:T(256)(128)(2,1)}, u32[]{:S(2)}) copy-start(bf16[96]{0:T(256)(128)(2,1)} %param.40) | copy-start | bytes 580
  7.3 50.4 %copy-start.43 = (bf16[96]{0:T(256)(128)(2,1)S(1)}, bf16[96]{0:T(256)(128)(2,1)}, u32[]{:S(2)}) copy-start(bf16[96]{0:T(256)(128)(2,1)} %param.41) | copy-start | bytes 580
  7.3 116.0 %all-gather.11.cloned.1.call-start = ((), (), s32[]{:S(2)}) async-start(), calls=%async_computation.13 | async-start | bytes 1327104 | tf_op jit(solution)/shard_map/all_gather | solution.py:66
  16.0 80.5 %copy-start.32 = (bf16[384]{0:T(512)(128)(2,1)S(1)}, bf16[384]{0:T(512)(128)(2,1)}, u32[]{:S(2)}) copy-start(bf16[384]{0:T(512)(128)(2,1)} %param.37) | copy-start | bytes 2308
  16.0 107.2 %copy-start.44 = (f32[16]{0:T(128)S(1)}, f32[16]{0:T(128)}, u32[]{:S(2)}) copy-start(f32[16]{0:T(128)} %param.43) | copy-start | bytes 196
  16.0 116.1 %all-gather.13.cloned.1.call-start = ((), (), s32[]{:S(2)}) async-start(), calls=%async_computation.14 | async-start | bytes 1327104 | tf_op jit(solution)/shard_map/all_gather | solution.py:67
  23.4 120.7 %all-gather.9.cloned.1.call-start = ((), (), s32[]{:S(2)}) async-start(), calls=%async_computation.12 | async-start | bytes 1327104 | tf_op jit(solution)/shard_map/all_gather | solution.py:68
  30.8 155.2 %all-gather.15.cloned.1.call-start = ((), (), s32[]{:S(2)}) async-start(), calls=%async_computation.15 | async-start | bytes 1327104 | tf_op jit(solution)/shard_map/all_gather | solution.py:69
  38.2 228.6 %all-gather.17.cloned.1.call-start = ((), (), s32[]{:S(2)}) async-start(), calls=%async_computation.16 | async-start | bytes 5308416 | tf_op jit(solution)/shard_map/all_gather | solution.py:70
  46.5 301.4 %all-gather.19.cloned.1.call-start = ((), (), s32[]{:S(2)}) async-start(), calls=%async_computation.17 | async-start | bytes 5308416 | tf_op jit(solution)/shard_map/all_gather | solution.py:71
  54.7 654.0 %reduce-scatter.29.cloned.1.call-start = ((), (), s32[]{:S(2)}) async-start(), calls=%async_computation.22 | async-start | bytes 2654208 | tf_op jit(solution)/shard_map/reduce_scatter | solution.py:343
  96.4 63.6 %copy-start.16 = (pred[4,256,256]{1,2,0:T(8,128)(4,1)}, pred[4,256,256]{1,2,0:T(8,128)(4,1)S(1)}, u32[]{:S(2)}) copy-start(pred[4,256,256]{1,2,0:T(8,128)(4,1)S(1)} %copy.115) | copy-start | bytes 786436
  151.8 8.2 copy-start.11
  156.7 4.5 copy-start.2
  156.7 4.8 copy-start.25
  161.5 3.6 copy-start.27
  166.7 22.8 %copy-start.19 = (bf16[96,8,4,256]{3,1,2,0:T(8,128)(2,1)}, bf16[96,8,4,256]{3,1,2,0:T(8,128)(2,1)S(1)}, u32[]{:S(2)}) copy-start(bf16[96,8,4,256]{3,1,2,0:T(8,128)(2,1)S(1)} %copy.161) | copy-start | bytes 4718596
  357.5 2.6 copy-start.5
  580.7 2.0 copy-start.4
  584.3 1.9 copy-start.6
  584.3 2.3 copy-start.23
  584.3 6.5 slice-start.2
  586.6 4.2 slice-start.3
  589.7 15.0 %slice-start = ((s8[4718592]{0:T(1024)(128)(4,1)}), s8[4194304]{0:T(1024)(128)(4,1)S(1)}, s32[]{:S(2)}) async-start(s8[4718592]{0:T(1024)(128)(4,1)} %bitcast.210), calls=%async_computation.31 | async-start | bytes 8388608
  590.8 13.9 copy-start.18
  590.9 13.8 copy-start.8
  590.9 13.8 slice-start.1
  604.7 6.1 copy-start.13
  610.8 2.8 copy-start.20
  613.6 2.9 copy-start.26
  613.6 2.9 copy-start.28
  616.4 138.9 %reduce-scatter.39.cloned.1.call-start = ((), (), s32[]{:S(2)}) async-start(), calls=%async_computation.27 | async-start | bytes 2654208
  621.4 6.6 copy-start.17
  637.9 7.2 copy-start.12
  645.1 2.7 copy-start.3
  647.8 2.7 copy-start.33
  656.5 170.4 %reduce-scatter.41.cloned.1.call-start = ((), (), s32[]{:S(2)}) async-start(), calls=%async_computation.28 | async-start | bytes 2654208
  665.1 2.7 copy-start.34
  673.8 224.4 %reduce-scatter.37.cloned.1.call-start = ((), (), s32[]{:S(2)}) async-start(), calls=%async_computation.26 | async-start | bytes 2654208
  678.4 2.7 copy-start.35
  687.2 377.1 %reduce-scatter.35.cloned.1.call-start = ((), (), s32[]{:S(2)}) async-start(), calls=%async_computation.25 | async-start | bytes 10616832 | tf_op jit(solution)/shard_map/reduce_scatter | solution.py:345
  697.8 532.5 %reduce-scatter.31.cloned.1.call-start = ((), (), s32[]{:S(2)}) async-start(), calls=%async_computation.23 | async-start | bytes 10616832 | tf_op jit(solution)/shard_map/reduce_scatter | solution.py:344
  708.6 577.1 %reduce-scatter.43.cloned.1.call-start = ((), (), s32[]{:S(2)}) async-start(), calls=%async_computation.29 | async-start | bytes 245760
  710.5 576.7 %reduce-scatter.25.cloned.1.call-start = ((), (), s32[]{:S(2)}) async-start(), calls=%async_computation.20 | async-start | bytes 245760 | tf_op jit(solution)/shard_map/reduce_scatter | solution.py:360
  757.2 310.9 %copy-start.45 = (u32[32]{0:T(128)S(1)}, u32[32]{0:T(128)}, u32[]{:S(2)}) copy-start(u32[32]{0:T(128)} %constant.226) | copy-start | bytes 388
  757.2 539.2 %reduce-scatter.27.cloned.1.call-start = ((), (), s32[]{:S(2)}) async-start(), calls=%async_computation.21 | async-start | bytes 245760 | tf_op jit(solution)/shard_map/reduce_scatter | solution.py:363
  828.6 490.4 %reduce-scatter.23.cloned.1.call-start = ((), (), s32[]{:S(2)}) async-start(), calls=%async_computation.19 | async-start | bytes 245760 | tf_op jit(solution)/shard_map/reduce_scatter | solution.py:357
  900.0 466.9 %all-gather.21.cloned.1.call-start = ((), (), s32[]{:S(2)}) async-start(), calls=%async_computation.18 | async-start | bytes 7864320 | tf_op jit(solution)/shard_map/all_gather | solution.py:260
  900.6 490.7 %reduce-scatter.45.cloned.1.call-start = ((), (), s32[]{:S(2)}) async-start(), calls=%async_computation.30 | async-start | bytes 737280
  1066.7 349.8 %reduce-scatter.33.cloned.1.call-start = ((), (), s32[]{:S(2)}) async-start(), calls=%async_computation.24 | async-start | bytes 737280 | tf_op jit(solution)/shard_map/reduce_scatter | solution.py:369
  1278.9 3.4 copy-start.10
  1278.9 3.4 copy-start.15
  1278.9 3.5 copy-start.24
  1418.2 5.9 copy-start.1
  (5 other events, 6.8 us)
Sparse Core Ops, SparseCore 0:
  16.1 42.4 all-gather.10
  61.4 40.0 all-gather.12
  104.2 39.8 all-gather.8
  146.2 39.8 all-gather.14
  188.1 78.6 all-gather.16
  268.7 79.1 all-gather.18
  616.6 67.1 reduce-scatter.28
  687.2 68.0 reduce-scatter.38
  758.9 67.9 reduce-scatter.40
  830.2 67.9 reduce-scatter.36
  901.8 162.4 reduce-scatter.34
  1067.7 162.5 reduce-scatter.30
  1232.7 18.8 reduce-scatter.42
  1254.5 19.7 reduce-scatter.24
  1276.5 19.8 reduce-scatter.26
  1299.3 19.7 reduce-scatter.22
  1320.5 46.3 all-gather.20
  1369.2 22.0 reduce-scatter.44
  1394.4 22.0 reduce-scatter.32
where the time goes:
time: 1440 us; the launch traced here: 1430 us
  waiting for transfers between devices  774 us (54%)
  other arithmetic  219 us (15%)
  matrix products  168 us (12%)
  blocking collectives  146 us (10%)
  local copies, waits for them, and re-layouts  104 us (7%)
  between operations  18.2 us (1%)
    unnamed x24, waiting for transfers between devices  209 us
    reduce_scatter x1, waiting for transfers between devices, per_device(): lax.psum_scatter(grad_down_weight, 'dp', scatter_dimension=0, tiled=True)  164 us
    reduce_scatter x1, waiting for transfers between devices, per_device(): lax.psum_scatter(grad_up_weight, 'dp', scatter_dimension=0, tiled=True)  161 us
    unnamed x3, blocking collectives  79.9 us
    all_gather x1, waiting for transfers between devices, fetch_weights(): lax.all_gather(wide[4], 'dp', axis=0, tiled=True)  75.1 us
    add x20, other arithmetic, retreat(): d_kernel + d_weighted * coupling_prev  69.1 us
    dot_general x6, matrix products, product(): return jnp.dot(left, right, preferred_element_type=jnp.float32)  61.9 us
    unnamed x153, local copies, waits for them, and re-layouts  49.5 us
  transfers between devices with their start and end apart: 19, of which 14 were waited for; matrix products, arithmetic and copies ran while one was open for 14% of the time, Pallas kernels for 0%

commit v1 on v0

v1 whole, which is shorter than its diff:
```python
import functools

import jax
import jax.numpy as jnp
from jax import lax
from jax.experimental import pallas as pl
from jax.experimental.pallas import tpu as pltpu
from jax.sharding import PartitionSpec as P

D = 768
HEADS = 12
HEAD_DIM = 64
LEN = 256
ITERS = 20
ROWS = 32
VMEM_LIMIT = 60 * 1024 * 1024


EPS_NORM = 1e-06
BETA = 0.5
MASKED = -1e30


def product(left, right):
    return jnp.dot(left, right, preferred_element_type=jnp.float32)


def product_left(left, right):
    return lax.dot_general(
        left, right, (((0,), (0,)), ((), ())), preferred_element_type=jnp.float32
    )


def product_right(left, right):
    return lax.dot_general(
        left, right, (((1,), (1,)), ((), ())), preferred_element_type=jnp.float32
    )


def layer_norm(values, gain, shift):
    centre = values - jnp.mean(values, axis=-1, keepdims=True)
    spread = jnp.mean(centre * centre, axis=-1, keepdims=True)
    recip = lax.rsqrt(spread + EPS_NORM)
    normed = centre * recip
    return (normed * gain + shift, normed, recip)


def norm_back(grad_out, normed, recip, gain):
    scaled = grad_out * gain
    inner_mean = jnp.mean(scaled, axis=-1, keepdims=True)
    cross_mean = jnp.mean(scaled * normed, axis=-1, keepdims=True)
    grad_in = recip * (scaled - inner_mean - normed * cross_mean)
    return (grad_in, jnp.sum(grad_out * normed, axis=0), jnp.sum(grad_out, axis=0))


def gelu_slope(values):
    normal_cdf = 0.5 * (1.0 + lax.erf(values * 0.7071067811865476))
    density = jnp.exp(-0.5 * values * values) * 0.3989422804014327
    return normal_cdf + values * density


def fetch_weights(matrices, vectors):
    wide = [lax.all_gather(item, "narrow", axis=1, tiled=True) for item in matrices]
    return (
        [lax.all_gather(item, "dp", axis=0, tiled=True) for item in wide],
        [lax.all_gather(item, "dp", axis=0, tiled=True).astype(jnp.float32) for item in vectors],
    )


def reduce_grads(matrices, vectors):
    reduced = [lax.psum_scatter(item, "dp", scatter_dimension=0, tiled=True) for item in matrices]
    sums = [lax.psum_scatter(item, "dp", scatter_dimension=0, tiled=True) for item in vectors]
    return (
        [
            lax.psum_scatter(
                item.astype(jnp.bfloat16), "narrow", scatter_dimension=1, tiled=True
            ).astype(jnp.float32)
            for item in reduced
        ],
        lax.psum(sums, "narrow"),
    )


MESH = pl.DeviceIdType.MESH


def hops():
    dp, narrow = lax.axis_index("dp"), lax.axis_index("narrow")
    return (dp // 2, lax.rem(dp, 2), narrow // 2, lax.rem(narrow, 2))


def place(me, depth, item, order):
    s, a, b, c = item
    z, x, y, core = me
    dx, dy = (a, b) if order == "x" else (b, a)
    z = z if isinstance(s, int) and s == 0 else lax.rem(z + s + depth, depth)
    x = 1 - x if dx else x
    y = 1 - y if dy else y
    core = 1 - core if c else core
    return (2 * z + x, 2 * y + core)


def greet(me, depth):
    peers = [place(me, depth, (s, 0, 0, 0), "x") for s in range(1, depth)]
    peers += [place(me, depth, (0, *bits), "x") for bits in ((1, 0, 0), (0, 1, 0), (0, 0, 1))]
    barrier = pltpu.get_barrier_semaphore()
    for peer in peers:
        pl.semaphore_signal(barrier, inc=1, device_id=peer, device_id_type=MESH)
    pl.semaphore_wait(barrier, len(peers))


def number(item):
    s, a, b, c = item
    return ((s * 2 + a) * 2 + b) * 2 + c


class Gather:
    def __init__(self, land, send_sem, recv_sem, chunks):
        self.land, self.send_sem, self.recv_sem, self.chunks = land, send_sem, recv_sem, chunks
        self.me = hops()
        self.depth = land.shape[0] // 2
        self.sent = []

    def copy(self, k, item, target):
        first, rows, order = self.chunks[k]
        s, a, b, c = item
        source = place(self.me, self.depth, (-s, a, b, c), order)
        block = self.land.at[source[0], source[1], pl.ds(first, rows), :]
        kind, amount = target
        there = {"z": (amount, 0, 0, 0), "p": (0, 1, 0, 0), "q": (0, 0, 1, 0), "c": (0, 0, 0, 1)}[kind]
        at = {"z": (amount, a, b, c), "p": (s, 1, b, c), "q": (s, a, 1, c), "c": (s, a, b, 1)}[kind]
        mark = number(at)
        return pltpu.make_async_remote_copy(
            src_ref=block,
            dst_ref=block,
            send_sem=self.send_sem.at[k, mark],
            recv_sem=self.recv_sem.at[k, mark],
            device_id=place(self.me, self.depth, there, order),
            device_id_type=MESH,
        )

    def send(self, k, item, kinds):
        for kind in kinds:
            for amount in range(1, self.depth) if kind == "z" else (1,):
                copy = self.copy(k, item, (kind, amount))
                copy.start()
                self.sent.append(copy)

    def wait(self, k, item):
        first, rows, order = self.chunks[k]
        s, a, b, c = item
        source = place(self.me, self.depth, (-s, a, b, c), order)
        block = self.land.at[source[0], source[1], pl.ds(first, rows), :]
        mark = number(item)
        pltpu.make_async_remote_copy(
            src_ref=block,
            dst_ref=block,
            send_sem=self.send_sem.at[k, mark],
            recv_sem=self.recv_sem.at[k, mark],
            device_id=place(self.me, self.depth, (0, 0, 0, 1), order),
            device_id_type=MESH,
        ).wait_recv()

    def start(self, k):
        self.send(k, (0, 0, 0, 0), "zpqc")

    def after_z(self, k):
        for s in range(1, self.depth):
            self.wait(k, (s, 0, 0, 0))
            self.send(k, (s, 0, 0, 0), "pqc")

    def after_p(self, k):
        for s in range(self.depth):
            self.wait(k, (s, 1, 0, 0))
            self.send(k, (s, 1, 0, 0), "qc")

    def after_q(self, k):
        for s in range(self.depth):
            for a in range(2):
                self.wait(k, (s, a, 1, 0))
                self.send(k, (s, a, 1, 0), "c")

    def after_c(self, k):
        for s in range(self.depth):
            for a in range(2):
                for b in range(2):
                    self.wait(k, (s, a, b, 1))

    def drain(self):
        for copy in self.sent:
            copy.wait_send()
        self.sent = []


def swap(half):
    return pltpu.roll(half, 64, 1)


def left_half(shape):
    return lax.broadcasted_iota(jnp.int32, shape, 1) < 64


def pack_block(block, odd):
    rows = block.shape[0]
    wide = jnp.concatenate([block, jnp.zeros((rows, 64), jnp.float32)], axis=1)
    turned = pltpu.roll(wide, 192, 1)
    main = jnp.where(odd, turned[:, :128], wide[:, :128])
    rest = jnp.where(left_half((rows, 128)), jnp.where(odd, wide[:, :128], wide[:, 128:]), 0.0)
    top, low = rest[: rows // 2], rest[rows // 2 :]
    return main, jnp.where(odd, swap(top) + low, top + swap(low))


def middle_of(even, odd):
    left = left_half(even.shape)
    return jnp.where(left, even, odd), swap(jnp.where(left, odd, even))


def fold_middle(top, low):
    left = left_half(top.shape)
    return jnp.where(left, top, swap(low)), jnp.where(left, swap(low), top)


VEC, SQUARE, UP, DOWN, TOTAL = 0, 16, 592, 1168, 1744


def gather_chunks():
    return (
        (0, 160, "x"), (160, 144, "y"),
        (304, 144, "x"), (448, 144, "y"),
        (592, 144, "x"), (736, 144, "y"), (880, 144, "x"), (1024, 144, "y"),
        (1168, 144, "x"), (1312, 144, "y"), (1456, 144, "x"), (1600, 144, "y"),
    )


def gather_kernel(
    q_ref, k_ref, v_ref, o_ref, up_ref, down_ref, vec_ref,
    fq_ref, fk_ref, fv_ref, fo_ref, fup_ref, fdown_ref, fvec_ref,
    land, send_sem, recv_sem,
):
    me = hops()
    depth = land.shape[0] // 2
    dp, narrow = lax.axis_index("dp"), lax.axis_index("narrow")
    odd = lax.rem(narrow, 2) == 1
    own = land.at[dp, narrow]
    half = q_ref.shape[0]
    own[0:16, :] = vec_ref[...]
    for i, ref in enumerate((q_ref, k_ref, v_ref, o_ref)):
        main, rest = pack_block(ref[...].astype(jnp.float32), odd)
        at = SQUARE + 144 * i
        own[at : at + 96, :] = main.astype(jnp.bfloat16)
        own[at + 96 : at + 144, :] = rest.astype(jnp.bfloat16)
    greet(me, depth)
    g = Gather(land, send_sem, recv_sem, gather_chunks())
    for k in range(4):
        g.start(k)
    for t in range(6):
        own[UP + 96 * t : UP + 96 * (t + 1), :] = up_ref[:, 128 * t : 128 * (t + 1)]
    main, rest = pack_block(down_ref[...].astype(jnp.float32), odd)
    own[DOWN : DOWN + 384, :] = main.astype(jnp.bfloat16)
    own[DOWN + 384 : DOWN + 576, :] = rest.astype(jnp.bfloat16)

    def put_square(ref, at, rows):
        for d in range(2 * depth):
            for pair in range(land.shape[1] // 2):
                even, other = land.at[d, 2 * pair], land.at[d, 2 * pair + 1]
                here = pl.ds(d * rows, rows)
                ref[here, pl.ds(384 * pair, 128)] = even[at : at + rows, :]
                ref[here, pl.ds(384 * pair + 256, 128)] = other[at : at + rows, :]
                top, low = middle_of(
                    even[at + rows : at + rows * 3 // 2, :].astype(jnp.float32),
                    other[at + rows : at + rows * 3 // 2, :].astype(jnp.float32),
                )
                ref[pl.ds(d * rows, rows // 2), pl.ds(384 * pair + 128, 128)] = top.astype(jnp.bfloat16)
                ref[pl.ds(d * rows + rows // 2, rows // 2), pl.ds(384 * pair + 128, 128)] = low.astype(jnp.bfloat16)

    steps = len(g.chunks) // 2
    for j in range(steps + 4):
        for stage, lag in ((g.after_z, 0), (g.after_p, 1), (g.after_q, 2), (g.after_c, 3)):
            if 0 <= j - lag < steps:
                stage(2 * (j - lag))
                stage(2 * (j - lag) + 1)
            if lag == 0 and j + 2 < steps:
                g.start(2 * j + 4)
                g.start(2 * j + 5)
        if j == 4:
            for i, ref in enumerate((fq_ref, fk_ref, fv_ref, fo_ref)):
                put_square(ref, SQUARE + 144 * i, 96)
    for d in range(2 * depth):
        for n in range(land.shape[1]):
            for t in range(6):
                fup_ref[pl.ds(96 * d, 96), pl.ds(768 * n + 128 * t, 128)] = land[d, n, UP + 96 * t : UP + 96 * (t + 1), :]
    put_square(fdown_ref, DOWN, 384)
    for d in range(2 * depth):
        fvec_ref[d] = land[d, 0, 0:16, :].astype(jnp.float32)
    g.drain()


def gather_weights(matrices, vectors, dp, narrow):
    packed = jnp.stack([jnp.pad(item, (0, 32)) for item in vectors[:8]])
    packed = jnp.concatenate([packed, vectors[8].reshape(3, 128), jnp.zeros((5, 128), jnp.bfloat16)])
    vmem = pl.BlockSpec(memory_space=pltpu.VMEM)
    square = jax.ShapeDtypeStruct((D, D), jnp.bfloat16)
    count = len(gather_chunks())
    out = pl.pallas_call(
        gather_kernel,
        name="gather",
        out_shape=(
            square, square, square, square,
            jax.ShapeDtypeStruct((D, 4 * D), jnp.bfloat16),
            jax.ShapeDtypeStruct((4 * D, D), jnp.bfloat16),
            jax.ShapeDtypeStruct((dp, 16, 128), jnp.float32),
        ),
        in_specs=[vmem] * 7,
        out_specs=(vmem,) * 7,
        scratch_shapes=[
            pltpu.VMEM((dp, narrow, TOTAL, 128), jnp.bfloat16),
            pltpu.SemaphoreType.DMA((count, dp * narrow)),
            pltpu.SemaphoreType.DMA((count, dp * narrow)),
        ],
        compiler_params=pltpu.CompilerParams(
            collective_id=0, has_side_effects=True, vmem_limit_bytes=VMEM_LIMIT
        ),
    )(*matrices, packed)
    vec = out[6]
    flat = [vec[:, i, :96].reshape(D) for i in range(8)] + [vec[:, 8:11, :].reshape(4 * D)]
    return out[:6], flat


class Scatter:
    def __init__(self, part, lands, send_sem, recv_sem, chunks):
        self.part, self.lands, self.send_sem, self.recv_sem, self.chunks = part, lands, send_sem, recv_sem, chunks
        self.me = hops()
        self.depth = part.shape[0] // 2
        self.sent = []

    def block(self, k, item):
        first, rows, order = self.chunks[k]
        owner = place(self.me, self.depth, item, order)
        return self.part.at[owner[0], owner[1], pl.ds(first, rows), :]

    def landing(self, k, item):
        first, rows, order = self.chunks[k]
        s, a, b, c = item
        rows = pl.ds(first, rows)
        if c:
            return self.lands[0].at[(s * 2 + a) * 2 + b, rows, :]
        if b:
            return self.lands[1].at[s * 2 + a, rows, :]
        if a:
            return self.lands[2].at[s, rows, :]
        return self.lands[3].at[s - 1, rows, :]

    def copy(self, k, item):
        s, a, b, c = item
        hop = (0, 0, 0, 1) if c else (0, 0, 1, 0) if b else (0, 1, 0, 0) if a else (s, 0, 0, 0)
        mark = number(item)
        return pltpu.make_async_remote_copy(
            src_ref=self.block(k, item),
            dst_ref=self.landing(k, item),
            send_sem=self.send_sem.at[k, mark],
            recv_sem=self.recv_sem.at[k, mark],
            device_id=place(self.me, self.depth, hop, self.chunks[k][2]),
            device_id_type=MESH,
        )

    def send(self, k, item):
        copy = self.copy(k, item)
        copy.start()
        self.sent.append(copy)

    def take(self, k, item, into):
        self.copy(k, item).wait_recv()
        ref = self.block(k, into)
        ref[...] = (ref[...].astype(jnp.float32) + self.landing(k, item)[...].astype(jnp.float32)).astype(jnp.bfloat16)

    def start(self, k):
        for s in range(self.depth):
            for a in range(2):
                for b in range(2):
                    self.send(k, (s, a, b, 1))

    def after_c(self, k):
        for b in (1, 0):
            for s in range(self.depth):
                for a in range(2):
                    self.take(k, (s, a, b, 1), (s, a, b, 0))
                    if b:
                        self.send(k, (s, a, 1, 0))

    def after_q(self, k):
        for a in (1, 0):
            for s in range(self.depth):
                self.take(k, (s, a, 1, 0), (s, a, 0, 0))
                if a:
                    self.send(k, (s, 1, 0, 0))

    def after_p(self, k):
        for s in [*range(1, self.depth), 0]:
            self.take(k, (s, 1, 0, 0), (s, 0, 0, 0))
            if s:
                self.send(k, (s, 0, 0, 0))

    def total(self, k):
        for s in range(1, self.depth):
            self.copy(k, (s, 0, 0, 0)).wait_recv()
        first, rows, order = self.chunks[k]
        value = self.block(k, (0, 0, 0, 0))[...].astype(jnp.float32)
        for s in range(1, self.depth):
            value = value + self.landing(k, (s, 0, 0, 0))[...].astype(jnp.float32)
        return value

    def drain(self):
        for copy in self.sent:
            copy.wait_send()
        self.sent = []


def scatter_lands(depth):
    shape = lambda count: pltpu.VMEM((count, TOTAL, 128), jnp.bfloat16)
    return [shape(depth * 4), shape(depth * 2), shape(depth), shape(max(depth - 1, 1))]


def scatter_kernel(
    q_ref, k_ref, v_ref, o_ref, up_ref, down_ref, vec_ref,
    gq_ref, gk_ref, gv_ref, go_ref, gup_ref, gdown_ref, gvec_ref,
    part, land_c, land_q, land_p, land_z, total, send_sem, recv_sem,
):
    me = hops()
    depth = part.shape[0] // 2
    narrow = lax.axis_index("narrow")
    odd = lax.rem(narrow, 2) == 1
    greet(me, depth)
    g = Scatter(part, (land_c, land_q, land_p, land_z), send_sem, recv_sem, scatter_chunks())

    def take_square(ref, at, rows):
        for d in range(2 * depth):
            for pair in range(part.shape[1] // 2):
                even, other = part.at[d, 2 * pair], part.at[d, 2 * pair + 1]
                here = pl.ds(d * rows, rows)
                even[at : at + rows, :] = ref[here, pl.ds(384 * pair, 128)]
                other[at : at + rows, :] = ref[here, pl.ds(384 * pair + 256, 128)]
                middle = ref[here, pl.ds(384 * pair + 128, 128)].astype(jnp.float32)
                one, two = fold_middle(middle[: rows // 2], middle[rows // 2 :])
                even[at + rows : at + rows * 3 // 2, :] = one.astype(jnp.bfloat16)
                other[at + rows : at + rows * 3 // 2, :] = two.astype(jnp.bfloat16)

    take_square(down_ref, DOWN, 384)
    for d in range(2 * depth):
        for n in range(part.shape[1]):
            for t in range(6):
                part[d, n, UP + 96 * t : UP + 96 * (t + 1), :] = up_ref[pl.ds(96 * d, 96), pl.ds(768 * n + 128 * t, 128)]
    for i, ref in enumerate((q_ref, k_ref, v_ref, o_ref)):
        take_square(ref, SQUARE + 144 * i, 96)
    for d in range(2 * depth):
        for n in range(part.shape[1]):
            part[d, n, 0:16, :] = vec_ref[d]
    count = len(g.chunks)
    for j in range(count + 4):
        if j < count:
            g.start(j)
        if 0 <= j - 1 < count:
            g.after_c(j - 1)
        if 0 <= j - 2 < count:
            g.after_q(j - 2)
        if 0 <= j - 3 < count:
            g.after_p(j - 3)
        if 0 <= j - 4 < count:
            first, rows, order = g.chunks[j - 4]
            total[pl.ds(first, rows), :] = g.total(j - 4)
    gvec_ref[...] = total[0:16, :]
    for t in range(6):
        gup_ref[:, 128 * t : 128 * (t + 1)] = total[UP + 96 * t : UP + 96 * (t + 1), :]
    for ref, at in ((gq_ref, SQUARE), (gk_ref, SQUARE + 144), (gv_ref, SQUARE + 288), (go_ref, SQUARE + 432), (gdown_ref, DOWN)):
        rows = ref.shape[0]
        ref[...] = unpack_block(total[at : at + rows, :], total[at + rows : at + rows * 3 // 2, :], odd)
    g.drain()


def unpack_block(main, rest, odd):
    left = left_half(rest.shape)
    other = swap(rest)
    top, low = jnp.where(odd, other, rest), jnp.where(odd, rest, other)
    piece = jnp.concatenate([top, low], axis=0)
    piece = jnp.where(left_half(piece.shape), piece, 0.0)
    swapped = swap(main)
    first = jnp.where(odd, jnp.where(left_half(piece.shape), piece, swapped), main)
    second = jnp.where(odd, swapped, piece)
    return jnp.concatenate([first, second[:, :64]], axis=1)


def scatter_chunks():
    return (
        (1168, 144, "x"), (1312, 144, "y"), (1456, 144, "x"), (1600, 144, "y"),
        (592, 144, "x"), (736, 144, "y"), (880, 144, "x"), (1024, 144, "y"),
        (448, 144, "x"), (304, 144, "y"), (160, 144, "x"), (0, 160, "y"),
    )


def scatter_grads(matrices, packed, dp, narrow):
    vmem = pl.BlockSpec(memory_space=pltpu.VMEM)
    square = jax.ShapeDtypeStruct((D // dp, D // narrow), jnp.float32)
    count = len(scatter_chunks())
    return pl.pallas_call(
        scatter_kernel,
        name="scatter",
        out_shape=(
            square, square, square, square,
            jax.ShapeDtypeStruct((D // dp, 4 * D // narrow), jnp.float32),
            jax.ShapeDtypeStruct((4 * D // dp, D // narrow), jnp.float32),
            jax.ShapeDtypeStruct((16, 128), jnp.float32),
        ),
        in_specs=[vmem] * 7,
        out_specs=(vmem,) * 7,
        scratch_shapes=[
            pltpu.VMEM((dp, narrow, TOTAL, 128), jnp.bfloat16),
            *scatter_lands(dp // 2),
            pltpu.VMEM((TOTAL, 128), jnp.float32),
            pltpu.SemaphoreType.DMA((count, dp * narrow)),
            pltpu.SemaphoreType.DMA((count, dp * narrow)),
        ],
        compiler_params=pltpu.CompilerParams(
            collective_id=1, has_side_effects=True, vmem_limit_bytes=VMEM_LIMIT
        ),
    )(*matrices, packed)


def transport_kernel(
    mixed_ref, seg_ref, kind_ref, weight_ref, cot_ref, normed_ref, recip_ref, gain_ref,
    value_ref, second_ref, branch_ref, sums_ref,
    kern_ref, prod_ref, flow_ref, acc_ref, left_ref, sigma_ref,
):
    packs = mixed_ref.shape[0] // LEN
    base = lax.axis_index("narrow") * packs
    blocks = LEN // ROWS
    lanes = lambda col: jnp.concatenate([col, col], axis=1)
    fold = lambda wide: wide[:, :128] + wide[:, 128:]
    eight = lambda wide: jnp.sum(wide.reshape(ROWS // 8, 8, LEN), axis=0)
    replicate = lambda col: jnp.broadcast_to(col, (ROWS, 128))

    def turned(row):
        return jnp.transpose(jnp.broadcast_to(row, (128, LEN)))

    for p in range(packs):
        rows = pl.ds(p * LEN, LEN)
        feats = mixed_ref[rows, :].astype(jnp.float32)
        recip = lax.rsqrt(jnp.sum(feats * feats, axis=1, keepdims=True) + EPS_NORM)
        unit = (feats * recip).astype(jnp.bfloat16)
        cosine = product_right(unit, unit)
        seg_row = seg_ref[pl.ds(base + p, 1), :].astype(jnp.float32)
        region_row = jnp.where(kind_ref[pl.ds(base + p, 1), :] == 0, 0.0, 1.0)
        seg_col = turned(seg_row)
        word_col = 1.0 - turned(region_row)
        same = jnp.where(lanes(seg_col) == seg_row, 1.0, 0.0)
        word_count = jnp.sum(same * (1.0 - region_row), axis=1, keepdims=True)
        region_count = jnp.sum(same * lanes(1.0 - word_col), axis=0, keepdims=True)
        kern_ref[p] = jnp.exp((cosine - 1.0) * (1.0 / BETA)) * same * lanes(word_col) * region_row
        left_ref[p, 0] = word_col
        left_ref[p, 1] = jnp.broadcast_to(word_count, (LEN, 128))
        prod_ref[0, p] = jnp.ones((LEN, LEN), jnp.float32)
        sigma_ref[0, p, 0:1] = region_row / region_count
        sigma_ref[0, p, 1:2] = region_row
        sigma_ref[0, p, 2:3] = region_count

    def advance(t, carry):
        for p in range(packs):
            sigma = sigma_ref[t, p, 0:1]
            scale = jnp.where(t == 0, 1.0, sigma)
            region = sigma_ref[0, p, 1:2]
            count = sigma_ref[0, p, 2:3]
            total = jnp.zeros((8, LEN), jnp.float32)
            for b in range(blocks):
                rows = pl.ds(b * ROWS, ROWS)
                weighted = kern_ref[p, rows, :] * (prod_ref[t, p, rows, :] * scale)
                row_sum = jnp.sum(fold(weighted * sigma), axis=1, keepdims=True)
                word = left_ref[p, 0, rows, :]
                delta = word / (left_ref[p, 1, rows, :] * replicate(row_sum) + 1.0 - word)
                scaled = weighted * lanes(delta)
                prod_ref[t + 1, p, rows, :] = scaled
                total = total + eight(scaled)
            col_sum = jnp.sum(total, axis=0, keepdims=True)
            sigma_ref[t + 1, p, 0:1] = region / (count * col_sum + 1.0 - region)
        return carry

    lax.fori_loop(0, ITERS, advance, 0)

    starts = []
    for p in range(packs):
        rows = pl.ds(p * LEN, LEN)
        weight = weight_ref[base + p]
        feats = mixed_ref[rows, :].astype(jnp.float32)
        recip = lax.rsqrt(jnp.sum(feats * feats, axis=1, keepdims=True) + EPS_NORM)
        unit = (feats * recip).astype(jnp.bfloat16)
        cosine = product_right(unit, unit)
        moved = (prod_ref[ITERS, p] * sigma_ref[ITERS, p, 0:1]) * (1.0 - cosine)
        value_ref[p : p + 1, :] = jnp.broadcast_to(jnp.sum(moved), (1, 128))
        moved = moved * weight
        flow_ref[p] = moved
        acc_ref[p] = jnp.zeros((LEN, LEN), jnp.float32)
        starts += [jnp.sum(moved, axis=0, keepdims=True), jnp.zeros((1, LEN), jnp.float32)]

    def retreat(step, carry):
        t = ITERS - 1 - step
        out = []
        for p in range(packs):
            flow_sum, spread = carry[2 * p : 2 * p + 2]
            before = sigma_ref[t, p, 0:1]
            d_col = -sigma_ref[0, p, 2:3] * sigma_ref[t + 1, p, 0:1] * (spread + flow_sum)
            total = jnp.zeros((8, LEN), jnp.float32)
            shift = jnp.zeros((8, LEN), jnp.float32)
            for b in range(blocks):
                rows = pl.ds(b * ROWS, ROWS)
                scaled = prod_ref[t + 1, p, rows, :]
                flow = flow_ref[p, rows, :] + scaled * d_col
                d_row = replicate(jnp.sum(fold(flow), axis=1, keepdims=True))
                d_row = -left_ref[p, 1, rows, :] * d_row
                moved = scaled * lanes(d_row)
                flow = flow + moved * before
                flow_ref[p, rows, :] = flow
                acc_ref[p, rows, :] = acc_ref[p, rows, :] + flow
                total = total + eight(flow)
                shift = shift + eight(moved)
            out += [
                jnp.sum(total, axis=0, keepdims=True),
                before * jnp.sum(shift, axis=0, keepdims=True),
            ]
        return tuple(out)

    lax.fori_loop(0, ITERS, retreat, tuple(starts))

    sums = [jnp.zeros((1, D), jnp.float32)] * 3
    for p in range(packs):
        rows = pl.ds(p * LEN, LEN)
        coupling = prod_ref[ITERS, p] * sigma_ref[ITERS, p, 0:1]
        d_cost = weight_ref[base + p] * coupling - acc_ref[p] * (1.0 / BETA)
        d_cosine = (-d_cost).astype(jnp.bfloat16)
        feats = mixed_ref[rows, :].astype(jnp.float32)
        recip = lax.rsqrt(jnp.sum(feats * feats, axis=1, keepdims=True) + EPS_NORM)
        unit = feats * recip
        unit_low = unit.astype(jnp.bfloat16)
        d_unit = product(d_cosine, unit_low) + product_left(d_cosine, unit_low)
        d_mixed = cot_ref[rows, :].astype(jnp.float32) + recip * (
            d_unit - unit * jnp.sum(d_unit * unit, axis=1, keepdims=True)
        )
        normed = normed_ref[rows, :]
        scaled = d_mixed * gain_ref[...]
        inner_mean = jnp.mean(scaled, axis=1, keepdims=True)
        cross_mean = jnp.mean(scaled * normed, axis=1, keepdims=True)
        d_second = recip_ref[rows, 0:1] * (scaled - inner_mean - normed * cross_mean)
        d_branch = d_second.astype(jnp.bfloat16)
        second_ref[rows, :] = d_second
        branch_ref[rows, :] = d_branch
        sums[0] = sums[0] + jnp.sum(d_mixed * normed, axis=0, keepdims=True)
        sums[1] = sums[1] + jnp.sum(d_mixed, axis=0, keepdims=True)
        sums[2] = sums[2] + jnp.sum(d_branch.astype(jnp.float32), axis=0, keepdims=True)
    for k in range(3):
        sums_ref[k : k + 1, :] = sums[k]


def transport_step(mixed, segments, row_kind, weight, cotangent, normed, recip, gain):
    rows = mixed.shape[0]
    packs = rows // LEN
    vmem = pl.BlockSpec(memory_space=pltpu.VMEM)
    square = (packs, LEN, LEN)
    return pl.pallas_call(
        transport_kernel,
        name="transport",
        out_shape=(
            jax.ShapeDtypeStruct((packs, 128), jnp.float32),
            jax.ShapeDtypeStruct((rows, D), jnp.float32),
            jax.ShapeDtypeStruct((rows, D), jnp.bfloat16),
            jax.ShapeDtypeStruct((8, D), jnp.float32),
        ),
        in_specs=[vmem, vmem, vmem, pl.BlockSpec(memory_space=pltpu.SMEM), vmem, vmem, vmem, vmem],
        out_specs=(vmem, vmem, vmem, vmem),
        scratch_shapes=[
            pltpu.VMEM(square, jnp.float32),
            pltpu.VMEM((ITERS + 1, *square), jnp.float32),
            pltpu.VMEM(square, jnp.float32),
            pltpu.VMEM(square, jnp.float32),
            pltpu.VMEM((packs, 2, LEN, 128), jnp.float32),
            pltpu.VMEM((ITERS + 1, packs, 8, LEN), jnp.float32),
        ],
        compiler_params=pltpu.CompilerParams(vmem_limit_bytes=VMEM_LIMIT),
    )(mixed, segments, row_kind, weight, cotangent, normed, recip, gain)


def per_device(
    inputs,
    segments,
    row_kind,
    query_weight,
    query_bias,
    key_weight,
    value_weight,
    value_bias,
    output_weight,
    output_bias,
    first_gain,
    first_shift,
    up_weight,
    up_bias,
    down_weight,
    down_bias,
    second_gain,
    second_shift,
    out_cotangent,
    loss_cotangent,
):
    pack_count = inputs.shape[0] // LEN
    row_count = inputs.shape[0]
    position = lax.axis_index("narrow")
    own_seg = lax.dynamic_slice_in_dim(segments, position * pack_count, pack_count, 0)
    matrices = (query_weight, key_weight, value_weight, output_weight, up_weight, down_weight)
    vectors = (
        query_bias,
        value_bias,
        output_bias,
        first_gain,
        first_shift,
        down_bias,
        second_gain,
        second_shift,
        up_bias,
    )
    dp, narrow = lax.axis_size("dp"), lax.axis_size("narrow")
    direct = D // dp == 96 and D // narrow == 192
    fetch = functools.partial(gather_weights, dp=dp, narrow=narrow) if direct else fetch_weights
    (w_query, w_key, w_value, w_output, w_up, w_down), gathered = fetch(matrices, vectors)
    b_query, b_value, b_output, g_first, s_first, b_down, g_second, s_second, b_up = gathered
    shape_heads = (pack_count, LEN, HEADS, HEAD_DIM)
    scale = HEAD_DIM ** (-0.5)
    query_low = (product(inputs, w_query) + b_query).astype(jnp.bfloat16)
    key_low = product(inputs, w_key).astype(jnp.bfloat16)
    value_low = (product(inputs, w_value) + b_value).astype(jnp.bfloat16)
    query_heads = query_low.reshape(shape_heads)
    key_heads = key_low.reshape(shape_heads)
    value_heads = value_low.reshape(shape_heads)
    paired = own_seg[:, None, :, None] == own_seg[:, None, None, :]

    def attention_scores():
        raw = jnp.einsum(
            "plhe,pmhe->phlm", query_heads, key_heads, preferred_element_type=jnp.float32
        )
        return jnp.where(paired, raw * scale, MASKED)

    scores = attention_scores()
    highest = jnp.max(scores, axis=-1, keepdims=True)
    shifted = jnp.exp(scores - highest)
    denominator = jnp.sum(shifted, axis=-1, keepdims=True)
    probability_low = (shifted / denominator).astype(jnp.bfloat16)
    log_total = highest + jnp.log(denominator)
    context_low = (
        jnp.einsum(
            "phlm,pmhe->plhe", probability_low, value_heads, preferred_element_type=jnp.float32
        )
        .reshape(row_count, D)
        .astype(jnp.bfloat16)
    )
    rows_float = inputs.astype(jnp.float32)
    attended = product(context_low, w_output) + b_output
    first, normed_first, recip_first = layer_norm(rows_float + attended, g_first, s_first)
    first_low = first.astype(jnp.bfloat16)
    inner = product(first_low, w_up) + b_up
    active_low = jax.nn.gelu(inner, approximate=False).astype(jnp.bfloat16)
    branch = product(active_low, w_down) + b_down
    output, normed_second, recip_second = layer_norm(first + branch, g_second, s_second)
    output_low = output.astype(jnp.bfloat16)
    group_out = lax.all_gather(output_low, "narrow", axis=0, tiled=True)
    partial_value, d_second, d_branch, sums_second = transport_step(
        output_low,
        segments,
        row_kind,
        loss_cotangent,
        out_cotangent,
        normed_second,
        jnp.broadcast_to(recip_second, (row_count, 128)),
        g_second.reshape(1, D),
    )
    transport_loss = lax.all_gather(partial_value[:, 0], "narrow", axis=0, tiled=True)
    grad_second_gain, grad_second_shift, grad_down_bias = sums_second[0], sums_second[1], sums_second[2]
    grad_down_weight = product_left(active_low, d_branch)
    d_inner = (product_right(d_branch, w_down) * gelu_slope(inner)).astype(jnp.bfloat16)
    grad_up_bias = jnp.sum(d_inner.astype(jnp.float32), axis=0)
    grad_up_weight = product_left(first_low, d_inner)
    d_first = d_second + product_right(d_inner, w_up)
    d_sum_first, grad_first_gain, grad_first_shift = norm_back(
        d_first, normed_first, recip_first, g_first
    )
    d_attended = d_sum_first.astype(jnp.bfloat16)
    grad_output_bias = jnp.sum(d_attended.astype(jnp.float32), axis=0)
    grad_output_weight = product_left(context_low, d_attended)
    d_context = product_right(d_attended, w_output).astype(jnp.bfloat16).reshape(shape_heads)
    probability = jnp.exp(attention_scores() - log_total)
    prob_again = probability.astype(jnp.bfloat16)
    d_values = (
        jnp.einsum("phlm,plhe->pmhe", prob_again, d_context, preferred_element_type=jnp.float32)
        .astype(jnp.bfloat16)
        .reshape(row_count, D)
    )
    d_probability = jnp.einsum(
        "plhe,pmhe->phlm", d_context, value_heads, preferred_element_type=jnp.float32
    )
    d_scores = (
        probability * (d_probability - jnp.sum(probability * d_probability, axis=-1, keepdims=True))
    ).astype(jnp.bfloat16)
    d_query = (
        (
            jnp.einsum("phlm,pmhe->plhe", d_scores, key_heads, preferred_element_type=jnp.float32)
            * scale
        )
        .astype(jnp.bfloat16)
        .reshape(row_count, D)
    )
    d_keys = (
        (
            jnp.einsum("phlm,plhe->pmhe", d_scores, query_heads, preferred_element_type=jnp.float32)
            * scale
        )
        .astype(jnp.bfloat16)
        .reshape(row_count, D)
    )
    grad_query_weight = product_left(inputs, d_query)
    grad_query_bias = jnp.sum(d_query.astype(jnp.float32), axis=0)
    grad_key_weight = product_left(inputs, d_keys)
    grad_value_weight = product_left(inputs, d_values)
    grad_value_bias = jnp.sum(d_values.astype(jnp.float32), axis=0)
    grad_inputs = (
        d_sum_first
        + product_right(d_query, w_query)
        + product_right(d_keys, w_key)
        + product_right(d_values, w_value)
    )
    grads = (grad_query_weight, grad_key_weight, grad_value_weight, grad_output_weight, grad_up_weight, grad_down_weight)
    sums = (
        grad_query_bias,
        grad_value_bias,
        grad_output_bias,
        grad_first_gain,
        grad_first_shift,
        grad_down_bias,
        grad_second_gain,
        grad_second_shift,
        grad_up_bias,
    )
    if direct:
        small = jnp.stack([jnp.pad(item.reshape(dp, D // dp), ((0, 0), (0, 128 - D // dp))) for item in sums[:8]], axis=1)
        packed = jnp.concatenate([small, sums[8].reshape(dp, 3, 128), jnp.zeros((dp, 5, 128), jnp.float32)], axis=1)
        out = scatter_grads([item.astype(jnp.bfloat16) for item in grads], packed.astype(jnp.bfloat16), dp, narrow)
        mats, vec = out[:6], out[6]
        vecs = [vec[i, : D // dp] for i in range(8)] + [vec[8:11].reshape(4 * D // dp)]
    else:
        mats, vecs = reduce_grads(grads, sums)
    return (
        group_out,
        transport_loss,
        grad_inputs,
        mats[0],
        vecs[0],
        mats[1],
        mats[2],
        vecs[1],
        mats[3],
        vecs[2],
        vecs[3],
        vecs[4],
        mats[4],
        vecs[8],
        mats[5],
        vecs[5],
        vecs[6],
        vecs[7],
    )


def solution(mesh):
    return jax.shard_map(
        per_device,
        mesh=mesh,
        in_specs=(
            P(("dp", "narrow"), None),
            P("dp", None),
            P("dp", None),
            P("dp", "narrow"),
            P("dp"),
            P("dp", "narrow"),
            P("dp", "narrow"),
            P("dp"),
            P("dp", "narrow"),
            P("dp"),
            P("dp"),
            P("dp"),
            P("dp", "narrow"),
            P("dp"),
            P("dp", "narrow"),
            P("dp"),
            P("dp"),
            P("dp"),
            P(("dp", "narrow"), None),
            P("dp"),
        ),
        out_specs=(
            P("dp", None),
            P("dp"),
            P(("dp", "narrow"), None),
            P("dp", "narrow"),
            P("dp"),
            P("dp", "narrow"),
            P("dp", "narrow"),
            P("dp"),
            P("dp", "narrow"),
            P("dp"),
            P("dp"),
            P("dp"),
            P("dp", "narrow"),
            P("dp"),
            P("dp", "narrow"),
            P("dp"),
            P("dp"),
            P("dp"),
        ),
        check_vma=False,
    )
```

time: 1440 us -> 464 us (0.32)
  waiting for transfers between devices: 774 us -> 0.02 us
  Pallas kernels: 0 us -> 198 us
  other arithmetic: 219 us -> 23.9 us
  blocking collectives: 146 us -> 6.39 us
  local copies, waits for them, and re-layouts: 104 us -> 59.2 us
  matrix products: 168 us -> 152 us
    reduce_scatter x7 -> x0, waiting for transfers between devices: 377 us -> none  [the longest x1 164 us: per_device(): lax.psum_scatter(grad_down_weight, 'dp', scatter_dimension=0, tiled=True)]
    unnamed x24 -> x1, waiting for transfers between devices: 209 us -> 0.02 us
    pallas_call x0 -> x3, Pallas kernels: none -> 198 us  [the longest x1 90.7 us: scatter_grads(): pl.pallas_call(scatter_kernel, name='scatter', out_shape=(square, square,...]
    all_gather x6 -> x0, waiting for transfers between devices: 142 us -> none  [the longest x1 75.1 us: fetch_weights(): lax.all_gather(wide[4], 'dp', axis=0, tiled=True)]
    unnamed x3 -> x0, blocking collectives: 79.9 us -> none
    reduce_sum x84 -> x0, other arithmetic: 76.5 us -> none  [the longest x20 31.9 us: retreat(): jnp.sum(d_coupling * weighted * delta_rows[:, None, :], axis=2)]
    add x20 -> x0, other arithmetic: 69.1 us -> none  [retreat(): d_kernel + d_weighted * coupling_prev]
    all_gather x7 -> x1, blocking collectives: 66 us -> 6.39 us  [per_device(): lax.all_gather(partial_value[:, 0], 'narrow', axis=0, tiled=True)]
  transfers between devices with their start and end apart: 19 -> 1, of which waited for: 14 -> 0; matrix products, arithmetic and copies ran while one was open for 14% -> 26% of each run, Pallas kernels for 0% -> 25%
where the time goes in v1:
time: 464 us; the launch traced here: 456 us
  Pallas kernels  198 us (43%)
  matrix products  152 us (33%)
  local copies, waits for them, and re-layouts  59.2 us (13%)
  other arithmetic  23.9 us (5%)
  between operations  16 us (3%)
  blocking collectives  6.39 us (1%)
    pallas_call x1, Pallas kernels, scatter_grads(): pl.pallas_call(scatter_kernel, name='scatter', out_shape=(square, square,...  90.7 us
    pallas_call x1, Pallas kernels, gather_weights(): pl.pallas_call(gather_kernel, name='gather', out_shape=(square, square, s...  82.2 us
    dot_general x6, matrix products, product(): return jnp.dot(left, right, preferred_element_type=jnp.float32)  61.9 us
    dot_general x6, matrix products, product_right(): lax.dot_general(left, right, (((1,), (1,)), ((), ())), preferred_element_...  32.7 us
    dot_general x6, matrix products, product_left(): lax.dot_general(left, right, (((0,), (0,)), ((), ())), preferred_element_...  26.6 us
    unnamed x135, local copies, waits for them, and re-layouts  25.7 us
    pallas_call x1, Pallas kernels, transport_step(): pl.pallas_call(transport_kernel, name='transport', out_shape=(jax.ShapeDt...  25.4 us
    convert_element_type x1, other arithmetic, per_device(): d_scores = (probability * (d_probability - jnp.sum(probability * d_probab...  12.7 us
  transfers between devices with their start and end apart: 1, of which 0 were waited for; matrix products, arithmetic and copies ran while one was open for 26% of the time, Pallas kernels for 25%

profile of v1, /device:TPU:0, one launch (start us, length us, event | category | flops | bytes accessed | tf_op | source)
XLA Modules:
  0.0 455.8 jit_solution(244782770185669837)
XLA Ops:
  7.2 1.7 copy.57.down_ref
  10.3 0.7 pad_bitcast_fusion.12
  11.0 0.7 pad_bitcast_fusion.14
  11.7 1.9 concatenate.7.vec_ref
  13.5 82.2 %gather.1 = (bf16[768,768]{1,0:T(8,128)(2,1)}, bf16[768,768]{1,0:T(8,128)(2,1)}, bf16[768,768]{1,0:T(8,128)(2,1)}, bf16[768,768]{1,0:T(8,128)(2,1)}, bf16[768,30...) custom-call(bf16[96,192]{1,0:T(8,128)(2,1)} %q_ref.1, bf16[96,192]{1,0:T(8,128)(2,1)} %k_ref.1, ...), custom_call_target="tpu_custom_call" | custom-call | tf_op jit(solution)/shard_map/gather/pallas_call | solution.py:304
  95.8 2.5 slice_reduce_fusion.11
  98.2 0.8 slice.74
  99.1 3.3 fusion.31
  102.3 1.4 reshape.155
  103.7 3.8 fusion.29
  107.5 2.4 reshape.156
  109.9 0.7 constant_dynamic-slice_fusion
  110.9 4.4 fusion.30
  115.3 2.9 reshape.154
  118.3 4.4 fusion.22
  122.6 3.2 fusion.16
  125.9 1.3 copy-done
  127.2 3.9 fusion.28
  131.1 1.2 copy.62
  132.3 1.5 copy.98
  133.9 3.8 fusion.59
  138.7 36.7 %fusion.2 = (bf16[1024,3072]{1,0:T(8,128)(2,1)S(1)}, f32[1024,3072]{1,0:T(8,128)}) fusion(f32[3072]{0:T(1024)S(1)} %add.170, bf16[768,3072]{1,0:T(8,128)(2,1)} %get-tuple-element.41, f32[1024,768]{1,0:T(8,128)S(1)} %get-tuple-element.121, f32[768]{0:T(1024)S(1)} %add.167, f32[768]{0:T(1024)S(1)} %mul.130, f32[1024]{0:T(1024)S(1)} %add_rsqrt_fusion.1, ...), kind=kOutput, calls=%fused_computation.4 | convolution fusion | flops 5043388416 | bytes 26765312 | tf_op jit(solution)/shard_map/dot_general | solution.py:25
  175.5 10.0 %fusion.60 = (f32[1024]{0:T(1024)S(1)}, f32[1024,768]{1,0:T(8,128)S(1)}) fusion(f32[768]{0:T(1024)S(1)} %add.173, bf16[1024,3072]{1,0:T(8,128)(2,1)S(1)} %get-tuple-element.122, bf16[3072,768]{1,0:T(8,128)(2,1)} %get-tuple-element.42, f32[768]{0:T(1024)S(1)} %add.167, f32[768]{0:T(1024)S(1)} %mul.130, f32[1024]{0:T(1024)S(1)} %add_rsqrt_fusion.1, ...), kind=kOutput, calls=%fused_computation.142 | convolution fusion | flops 4837342208 | bytes 17323008 | tf_op jit(solution)/shard_map/dot_general | solution.py:25
  185.5 1.6 copy-done.3
  187.8 4.7 %add_convert_fusion = (bf16[1024,768]{1,0:T(8,128)(2,1)}, f32[1024,768]{1,0:T(8,128)}) fusion(f32[768]{0:T(1024)S(1)} %add.178, f32[768]{0:T(1024)S(1)} %mul.139, f32[1024]{0:T(1024)S(1)} %add_rsqrt_fusion, f32[1024,768]{1,0:T(8,128)} %copy-done.3, f32[1024]{0:T(1024)S(1)} %broadcast_multiply_fusion.2), kind=kLoop, calls=%fused_computation.46 | loop fusion | flops 3932160 | bytes 7878656 | tf_op jit(solution)/shard_map/convert_element_type | solution.py:767
  192.5 0.9 log_add_fusion
  194.0 1.0 broadcast_in_dim.41.recip_ref
  195.0 25.4 %transport.1 = (f32[4,128]{1,0:T(4,128)}, f32[1024,768]{1,0:T(8,128)}, bf16[1024,768]{1,0:T(8,128)(2,1)}, f32[8,768]{1,0:T(8,128)}) custom-call(bf16[1024,768]{1,0:T(8,128)(2,1)} %get-tuple-element.107.mixed_ref, s32[16,256]{1,0:T(8,128)} %seg_ref.1, s32[16,256]{1,0:T(8,128)} %kind_ref.1, f32[16]{0:T(128)} %weight_ref.1, bf16[1024,768]{1,0:T(8,128)(2,1)} %cot_ref.1, ...), custom_call_target="tpu_custom_call" | custom-call | tf_op jit(solution)/shard_map/transport/pallas_call | solution.py:664
  220.5 12.8 %fusion.63 = (bf16[3072]{0:T(1024)(128)(2,1)S(1)}, bf16[1024,3072]{1,0:T(8,128)(2,1)S(1)}) fusion(f32[1024,3072]{1,0:T(8,128)} %get-tuple-element.123, f32[3072]{0:T(1024)S(1)} %copy-done.39, bf16[1024,768]{1,0:T(8,128)(2,1)} %get-tuple-element.45, bf16[3072,768]{1,0:T(8,128)(2,1)} %get-tuple-element.42), kind=kOutput, calls=%fused_computation.145 | convolution fusion | flops 4869583872 | bytes 25184256 | tf_op jit(solution)/shard_map/dot_general | solution.py:35
  233.4 10.5 %multiply_reduce_fusion.1 = (bf16[768]{0:T(1024)(128)(2,1)S(1)}, f32[1024]{0:T(1024)S(1)}, f32[1024]{0:T(1024)S(1)}, bf16[768]{0:T(1024)(128)(2,1)S(1)}, f32[1024,768]{1,0:T(8,128)S(1)}) fusion(f32[1024,768]{1,0:T(8,128)S(1)} %get-tuple-element.121, f32[1024]{0:T(1024)S(1)} %copy-done.28, f32[1024]{0:T(1024)S(1)} %copy-done.25, f32[768]{0:T(1024)S(1)} %copy-done.30, ...), kind=kOutput, calls=%fused_computation.40 | convolution fusion | flops 4839698432 | bytes 20469760 | tf_op jit(solution)/shard_map/dot_general | solution.py:35
  243.9 1.1 convert_reduce_fusion
  245.0 1.7 copy-done.4
  246.7 1.4 convolution_convert_fusion.2
  248.2 1.6 copy.65
  249.8 2.9 reshape.157
  252.7 10.3 %multiply_reduce_fusion = (f32[4,12,256]{2,1,0:T(8,128)S(1)}, f32[4,12,256,256]{2,3,1,0:T(8,128)}) fusion(f32[4,12,256]{2,1,0:T(8,128)S(1)} %log_add_fusion, f32[4,12,256,256]{2,3,1,0:T(8,128)} %copy-done, pred[4,256,256]{1,2,0:T(8,128)(4,1)S(1)} %broadcast_compare_fusion, bf16[4,256,12,64]{1,0,3,2:T(4,128)(2,1)S(1)} %copy-done.7, ...), kind=kOutput, calls=%fused_computation.12 | convolution fusion | flops 418369536 | bytes 28672000 | tf_op jit(solution)/shard_map/plhe,pmhe->phlm/dot_general | solution.py:800
  263.0 12.7 %multiply_convert_fusion = bf16[4,12,256,256]{2,3,1,0:T(8,128)(2,1)} fusion(f32[4,12,256,256]{2,3,1,0:T(8,128)} %get-tuple-element.128, f32[4,12,256]{2,1,0:T(8,128)S(1)} %get-tuple-element.127, f32[4,12,256]{2,1,0:T(8,128)S(1)} %log_add_fusion, f32[4,12,256,256]{2,3,1,0:T(8,128)} %copy-done, pred[4,256,256]{1,2,0:T(8,128)(4,1)S(1)} %broadcast_compare_fusion), kind=kLoop, calls=%fused_computation.11 | loop fusion | flops 18874368 | bytes 31817728 | tf_op jit(solution)/shard_map/convert_element_type | solution.py:805
  275.7 4.5 fusion.62
  280.4 5.8 %fusion.61 = (bf16[12,64]{1,0:T(8,128)(2,1)S(1)}, bf16[4,256,12,64]{1,3,2,0:T(8,128)(2,1)}) fusion(bf16[4,12,256,256]{2,3,1,0:T(8,128)(2,1)} %multiply_convert_fusion, bf16[4,256,12,64]{1,0,3,2:T(4,128)(2,1)} %reshape.156), kind=kOutput, calls=%fused_computation.143 | convolution fusion | flops 405011712 | bytes 9438720 | tf_op jit(solution)/shard_map/phlm,pmhe->plhe/dot_general | solution.py:808
  287.0 2.8 copy.76
  289.8 1.5 copy.101
  291.2 1.2 copy.70
  292.5 1.5 copy.99
  294.0 2.0 fusion.33
  296.0 1.2 copy.73
  297.2 1.5 copy.100
  298.7 1.3 concatenate.8.vec_ref
  300.0 4.0 fusion.39.v_ref
  304.1 2.6 fusion.37.q_ref
  306.7 2.5 fusion.38.k_ref
  309.3 2.7 convolution_convert_fusion.4.o_ref
  311.9 0.9 slice-done.6
  312.8 7.8 %convolution_convert_fusion.1.up_ref = bf16[768,3072]{1,0:T(8,128)(2,1)} fusion(bf16[1024,3072]{1,0:T(8,128)(2,1)S(1)} %bitcast.154, f32[1024,768]{1,0:T(8,128)S(1)} %copy-done.2, f32[768]{0:T(1024)S(1)} %copy-done.41, f32[768]{0:T(1024)S(1)} %copy-done.30, f32[1024]{0:T(1024)S(1)} %copy-done.28, f32[1024]{0:T(1024)S(1)} %copy-done.25), kind=kOutput, calls=%fused_computation.38 | convolution fusion | flops 4838129664 | bytes 14170112 | tf_op jit(solution)/shard_map/dot_general | solution.py:29
  320.6 7.0 %convolution_convert_fusion.down_ref = bf16[3072,768]{1,0:T(8,128)(2,1)} fusion(bf16[1024,3072]{1,0:T(8,128)(2,1)S(1)} %bitcast.156, bf16[1024,768]{1,0:T(8,128)(2,1)S(1)} %copy-done.45), kind=kOutput, calls=%fused_computation.37 | convolution fusion | flops 4834197504 | bytes 12582912 | tf_op jit(solution)/shard_map/dot_general | solution.py:29
  327.6 90.7 %scatter.1 = (f32[96,192]{1,0:T(8,128)}, f32[96,192]{1,0:T(8,128)}, f32[96,192]{1,0:T(8,128)}, f32[96,192]{1,0:T(8,128)}, f32[96,768]{1,0:T(8,128)}, /*index=5*/f32[384,192]{1,0:T(8,128)}, f32[16,128]{1,0:T(8,128)}) custom-call(bf16[768,768]{1,0:T(8,128)(2,1)} %fusion.37.q_ref, bf16[768,768]{1,0:T(8,128)(2,1)} %fusion.38.k_ref, ...), custom_call_target="tpu_custom_call" | custom-call | tf_op jit(solution)/shard_map/scatter/pallas_call | solution.py:503
  418.3 1.9 copy.88
  421.8 6.4 %all-reduce.16 = f32[16]{0:T(128)} all-reduce(f32[16]{0:T(128)S(1)} %dynamic-update-slice), channel_id=2, replica_groups=mesh['dp'=8,'narrow'=4] {'narrow'}, use_global_device_ids=true, to_apply=%add.16 | all-reduce | flops 16 | bytes 128 | tf_op jit(solution)/shard_map/all_gather | solution.py:779
  428.2 1.2 slice_bitcast_fusion
  429.4 1.5 slice_bitcast_fusion.1
  430.9 3.3 fusion.64
  434.3 1.5 fusion.65
  436.0 3.2 add_add_fusion
  439.2 6.0 %copy.137 = bf16[4096,768]{1,0:T(8,128)(2,1)} copy(bf16[4096,768]{1,0:T(8,128)(2,1)} %all-gather.3.cloned.1.call-done) | data formatting | bytes 12582912
  447.8 0.7 copy.142
  (181 shorter events, 8.9 us)
Async XLA Ops:
  7.2 432.0 %all-gather.3.cloned.1.call-start = ((), (), s32[]{:S(2)}) async-start(), calls=%async_computation | async-start | bytes 7864320 | tf_op jit(solution)/shard_map/all_gather | solution.py:768
  103.7 14.5 %copy-start.8 = (bf16[4,256,12,64]{1,0,3,2:T(4,128)(2,1)}, bf16[4,256,12,64]{1,0,3,2:T(4,128)(2,1)S(1)}, u32[]{:S(2)}) copy-start(bf16[4,256,12,64]{1,0,3,2:T(4,128)(2,1)S(1)} %reshape.155) | copy-start | bytes 4718596
  118.3 7.6 %copy-start.6 = (bf16[4,256,12,64]{1,0,3,2:T(4,128)(2,1)}, bf16[4,256,12,64]{1,0,3,2:T(4,128)(2,1)S(1)}, u32[]{:S(2)}) copy-start(bf16[4,256,12,64]{1,0,3,2:T(4,128)(2,1)S(1)} %reshape.154) | copy-start | bytes 4718596
  122.6 4.5 copy-start
  127.2 3.9 copy-start.19
  131.0 2.8 copy-start.37
  137.8 106.1 %copy-start.1 = (f32[1024,768]{1,0:T(8,128)}, f32[1024,768]{1,0:T(8,128)S(1)}, u32[]{:S(2)}) copy-start(f32[1024,768]{1,0:T(8,128)S(1)} %get-tuple-element.121) | copy-start | bytes 9437188
  137.8 0.7 copy-start.36
  137.8 0.8 copy-start.35
  137.8 0.9 copy-start.34
  137.8 37.6 %copy-start.24 = (f32[1024]{0:T(1024)}, f32[1024]{0:T(1024)S(1)}, u32[]{:S(2)}) copy-start(f32[1024]{0:T(1024)S(1)} %broadcast_multiply_fusion.3) | copy-start | bytes 12292
  138.3 37.1 %copy-start.27 = (f32[1024]{0:T(1024)}, f32[1024]{0:T(1024)S(1)}, u32[]{:S(2)}) copy-start(f32[1024]{0:T(1024)S(1)} %add_rsqrt_fusion.1) | copy-start | bytes 12292
  138.5 36.9 %copy-start.29 = (f32[768]{0:T(1024)}, f32[768]{0:T(1024)S(1)}, u32[]{:S(2)}) copy-start(f32[768]{0:T(1024)S(1)} %mul.130) | copy-start | bytes 9220
  138.6 36.9 %copy-start.40 = (f32[768]{0:T(1024)}, f32[768]{0:T(1024)S(1)}, u32[]{:S(2)}) copy-start(f32[768]{0:T(1024)S(1)} %add.167) | copy-start | bytes 9220
  138.6 36.8 %copy-start.38 = (f32[3072]{0:T(1024)}, f32[3072]{0:T(1024)S(1)}, u32[]{:S(2)}) copy-start(f32[3072]{0:T(1024)S(1)} %add.170) | copy-start | bytes 36868
  175.4 10.0 %copy-start.50 = (bf16[1024,3072]{1,0:T(8,128)(2,1)}, bf16[1024,3072]{1,0:T(8,128)(2,1)S(1)}, u32[]{:S(2)}) copy-start(bf16[1024,3072]{1,0:T(8,128)(2,1)S(1)} %get-tuple-element.122) | copy-start | bytes 18874372
  185.5 1.7 copy-start.3
  185.5 2.2 copy-start.33
  185.5 2.3 copy-start.32
  187.8 5.5 %copy-start.31 = (f32[8,1,96]{2,1,0:T(1,128)S(1)}, f32[8,1,96]{2,1,0:T(1,128)}, u32[]{:S(2)}) copy-start(f32[8,1,96]{2,1,0:T(1,128)} %get-tuple-element.109) | copy-start | bytes 9220
  195.0 25.4 %copy-start.39 = (f32[3072]{0:T(1024)S(1)}, f32[3072]{0:T(1024)}, u32[]{:S(2)}) copy-start(f32[3072]{0:T(1024)} %copy-done.38) | copy-start | bytes 36868
  220.4 12.9 %copy-start.25 = (f32[1024]{0:T(1024)S(1)}, f32[1024]{0:T(1024)}, u32[]{:S(2)}) copy-start(f32[1024]{0:T(1024)} %copy-done.24) | copy-start | bytes 12292
  220.4 12.9 %copy-start.28 = (f32[1024]{0:T(1024)S(1)}, f32[1024]{0:T(1024)}, u32[]{:S(2)}) copy-start(f32[1024]{0:T(1024)} %copy-done.27) | copy-start | bytes 12292
  220.4 12.9 %copy-start.30 = (f32[768]{0:T(1024)S(1)}, f32[768]{0:T(1024)}, u32[]{:S(2)}) copy-start(f32[768]{0:T(1024)} %copy-done.29) | copy-start | bytes 9220
  220.4 12.9 %copy-start.43 = (f32[1024,768]{1,0:T(8,128)S(1)}, f32[1024,768]{1,0:T(8,128)}, u32[]{:S(2)}) copy-start(f32[1024,768]{1,0:T(8,128)} %get-tuple-element.44) | copy-start | bytes 9437188
  233.3 10.5 %copy-start.49 = (bf16[1024,3072]{1,0:T(8,128)(2,1)}, bf16[1024,3072]{1,0:T(8,128)(2,1)S(1)}, u32[]{:S(2)}) copy-start(bf16[1024,3072]{1,0:T(8,128)(2,1)S(1)} %get-tuple-element.134) | copy-start | bytes 18874372
  243.9 2.8 copy-start.47
  245.0 1.7 copy-start.4
  248.1 4.5 copy-start.7
  252.7 23.0 %slice-start = ((s8[12582912]{0:T(1024)(128)(4,1)}), s8[4194304]{0:T(1024)(128)(4,1)S(1)}, s32[]{:S(2)}) async-start(s8[12582912]{0:T(1024)(128)(4,1)} %bitcast.135), calls=%async_computation.1 | async-start | bytes 8388608
  252.7 23.0 %slice-start.1 = ((s8[12582912]{0:T(1024)(128)(4,1)}), s8[4194304]{0:T(1024)(128)(4,1)S(1)}, s32[]{:S(2)}) async-start(s8[12582912]{0:T(1024)(128)(4,1)} %bitcast.135), calls=%async_computation.2 | async-start | bytes 8388608
  263.0 12.7 %slice-start.2 = ((s8[12582912]{0:T(1024)(128)(4,1)}), s8[4194304]{0:T(1024)(128)(4,1)S(1)}, s32[]{:S(2)}) async-start(s8[12582912]{0:T(1024)(128)(4,1)} %bitcast.135), calls=%async_computation.3 | async-start | bytes 8388608
  280.3 6.2 %copy-start.26 = (f32[8,768]{1,0:T(8,128)S(1)}, f32[8,768]{1,0:T(8,128)}, u32[]{:S(2)}) copy-start(f32[8,768]{1,0:T(8,128)} %get-tuple-element.46) | copy-start | bytes 73732
  280.3 13.6 %slice-start.3 = ((s8[6291456]{0:T(1024)(128)(4,1)}), s8[2097152]{0:T(1024)(128)(4,1)S(1)}, s32[]{:S(2)}) async-start(s8[6291456]{0:T(1024)(128)(4,1)} %bitcast.137), calls=%async_computation.4 | async-start | bytes 4194304
  287.0 4.3 copy-start.12
  287.0 7.0 %slice-start.4 = ((s8[6291456]{0:T(1024)(128)(4,1)}), s8[4194304]{0:T(1024)(128)(4,1)S(1)}, s32[]{:S(2)}) async-start(s8[6291456]{0:T(1024)(128)(4,1)} %bitcast.137), calls=%async_computation.5 | async-start | bytes 8388608
  291.2 2.7 copy-start.9
  296.0 4.0 copy-start.10
  300.0 4.1 copy-start.14
  300.0 4.1 copy-start.44
  304.1 2.6 copy-start.15
  306.7 2.6 copy-start.5
  306.7 2.6 copy-start.13
  306.7 5.2 %slice-start.5 = ((s8[6291456]{0:T(1024)(128)(4,1)}), s8[4194304]{0:T(1024)(128)(4,1)S(1)}, s32[]{:S(2)}) async-start(s8[6291456]{0:T(1024)(128)(4,1)} %bitcast.153), calls=%async_computation.6 | async-start | bytes 8388608
  309.2 2.7 copy-start.2
  309.2 2.7 copy-start.41
  309.3 3.6 slice-start.6
  309.3 11.3 %slice-start.7 = ((s8[6291456]{0:T(1024)(128)(4,1)}), s8[4194304]{0:T(1024)(128)(4,1)S(1)}, s32[]{:S(2)}) async-start(s8[6291456]{0:T(1024)(128)(4,1)} %bitcast.155), calls=%async_computation.8 | async-start | bytes 8388608
  312.8 7.8 %copy-start.45 = (bf16[1024,768]{1,0:T(8,128)(2,1)S(1)}, bf16[1024,768]{1,0:T(8,128)(2,1)}, u32[]{:S(2)}) copy-start(bf16[1024,768]{1,0:T(8,128)(2,1)} %get-tuple-element.45) | copy-start | bytes 4718596
  312.8 7.8 %slice-start.8 = ((s8[6291456]{0:T(1024)(128)(4,1)}), s8[2097152]{0:T(1024)(128)(4,1)S(1)}, s32[]{:S(2)}) async-start(s8[6291456]{0:T(1024)(128)(4,1)} %bitcast.155), calls=%async_computation.9 | async-start | bytes 4194304
  327.6 92.6 %copy-start.48 = (u32[32]{0:T(128)S(1)}, u32[32]{0:T(128)}, u32[]{:S(2)}) copy-start(u32[32]{0:T(128)} %constant.136) | copy-start | bytes 388
  327.6 93.8 %copy-start.42 = (f32[4,128]{1,0:T(4,128)S(1)}, f32[4,128]{1,0:T(4,128)}, u32[]{:S(2)}) copy-start(f32[4,128]{1,0:T(4,128)} %get-tuple-element.43) | copy-start | bytes 6148
  430.9 3.4 copy-start.16
  430.9 3.4 copy-start.46
  434.3 1.5 copy-start.11
  434.3 1.7 copy-start.17
  439.2 6.0 %copy-start.23 = (f32[96,192]{1,0:T(8,128)S(1)}, f32[96,192]{1,0:T(8,128)}, u32[]{:S(2)}) copy-start(f32[96,192]{1,0:T(8,128)} %get-tuple-element.164) | copy-start | bytes 221188
  439.2 6.6 %copy-start.22 = (f32[96,192]{1,0:T(8,128)S(1)}, f32[96,192]{1,0:T(8,128)}, u32[]{:S(2)}) copy-start(f32[96,192]{1,0:T(8,128)} %get-tuple-element.166) | copy-start | bytes 221188
  439.2 7.3 %copy-start.21 = (f32[96,192]{1,0:T(8,128)S(1)}, f32[96,192]{1,0:T(8,128)}, u32[]{:S(2)}) copy-start(f32[96,192]{1,0:T(8,128)} %get-tuple-element.167) | copy-start | bytes 221188
  439.2 7.9 %copy-start.20 = (f32[96,192]{1,0:T(8,128)S(1)}, f32[96,192]{1,0:T(8,128)}, u32[]{:S(2)}) copy-start(f32[96,192]{1,0:T(8,128)} %get-tuple-element.169) | copy-start | bytes 221188
  439.2 8.5 %copy-start.18 = (f32[96,768]{1,0:T(8,128)S(1)}, f32[96,768]{1,0:T(8,128)}, u32[]{:S(2)}) copy-start(f32[96,768]{1,0:T(8,128)} %get-tuple-element.173) | copy-start | bytes 884740
Sparse Core Ops, SparseCore 0:
  192.6 48.7 all-gather.2

commit v2 on v1

v2 whole, which is shorter than its diff:
```python
import functools

import jax
import jax.numpy as jnp
from jax import lax
from jax.experimental import pallas as pl
from jax.experimental.pallas import tpu as pltpu
from jax.sharding import PartitionSpec as P

D = 768
HEADS = 12
HEAD_DIM = 64
LEN = 256
ITERS = 20
ROWS = 32
VMEM_LIMIT = 62 * 1024 * 1024

EPS_NORM = 1e-06
BETA = 0.5
MASKED = -1e30


def product(left, right):
    return jnp.dot(left, right, preferred_element_type=jnp.float32)


def product_left(left, right):
    return lax.dot_general(
        left, right, (((0,), (0,)), ((), ())), preferred_element_type=jnp.float32
    )


def product_right(left, right):
    return lax.dot_general(
        left, right, (((1,), (1,)), ((), ())), preferred_element_type=jnp.float32
    )


def fetch_weights(matrices, vectors):
    wide = [lax.all_gather(item, "narrow", axis=1, tiled=True) for item in matrices]
    query, keys, values, output, up, down = [lax.all_gather(item, "dp", axis=0, tiled=True) for item in wide]
    vecs = [lax.all_gather(item, "dp", axis=0, tiled=True).astype(jnp.float32) for item in vectors]
    up = up.reshape(GRID[0], BLOCK, GRID[1], 6, 128).transpose(0, 2, 3, 1, 4).reshape(*GRID, 6 * BLOCK, 128)
    small = jnp.pad(jnp.stack(vecs[:8]), ((0, 8), (0, 128)))
    tiles = jnp.pad(vecs[8].reshape(24, 128), ((0, 8), (0, 0)))
    return (jnp.concatenate([query, keys, values, output]), up, down, small, tiles)


def reduce_grads(matrices, vectors):
    reduced = [lax.psum_scatter(item, "dp", scatter_dimension=0, tiled=True) for item in matrices]
    sums = [lax.psum_scatter(item, "dp", scatter_dimension=0, tiled=True) for item in vectors]
    return (
        [
            lax.psum_scatter(
                item.astype(jnp.bfloat16), "narrow", scatter_dimension=1, tiled=True
            ).astype(jnp.float32)
            for item in reduced
        ],
        lax.psum(sums, "narrow"),
    )


MESH = pl.DeviceIdType.MESH
FF = 4 * D
VEC, SQUARE, UP, DOWN, TOTAL = 0, 16, 592, 1168, 1744
STEP, PART, STEPS = 288, 144, 6
GRID = (8, 4)
BLOCK = D // GRID[0]


def hops():
    dp, narrow = lax.axis_index("dp"), lax.axis_index("narrow")
    return (dp // 2, lax.rem(dp, 2), narrow // 2, lax.rem(narrow, 2))


def place(me, depth, item, order):
    s, a, b, c = item
    z, x, y, core = me
    dx, dy = (a, b) if order == "x" else (b, a)
    z = z if s == 0 else lax.rem(z + s + depth, depth)
    x = 1 - x if dx else x
    y = 1 - y if dy else y
    core = 1 - core if c else core
    return (2 * z + x, 2 * y + core)


def greet(me, depth):
    peers = [place(me, depth, (s, 0, 0, 0), "x") for s in range(1, depth)]
    peers += [place(me, depth, (0, *bits), "x") for bits in ((1, 0, 0), (0, 1, 0), (0, 0, 1))]
    barrier = pltpu.get_barrier_semaphore()
    for peer in peers:
        pl.semaphore_signal(barrier, inc=1, device_id=peer, device_id_type=MESH)
    pl.semaphore_wait(barrier, len(peers))


def number(item):
    s, a, b, c = item
    return ((s * 2 + a) * 2 + b) * 2 + c


def chunks_of(step):
    first = SQUARE + step * STEP
    return ((2 * step, first, PART, "x"), (2 * step + 1, first + PART, STEP - PART, "y"))


VEC_CHUNK = (2 * STEPS, 0, SQUARE, "x")


class Gather:
    def __init__(self, land, send_sem, recv_sem):
        self.land, self.send_sem, self.recv_sem = land, send_sem, recv_sem
        self.me = hops()
        self.depth = land.shape[0] // 2

    def copy(self, chunk, item, hop, at):
        row, first, rows, order = chunk
        s, a, b, c = item
        source = place(self.me, self.depth, (-s, a, b, c), order)
        block = self.land.at[source[0], source[1], pl.ds(first, rows), :]
        return pltpu.make_async_remote_copy(
            src_ref=block,
            dst_ref=block,
            send_sem=self.send_sem.at[row, number(at)],
            recv_sem=self.recv_sem.at[row, number(at)],
            device_id=place(self.me, self.depth, hop, order),
            device_id_type=MESH,
        )

    def send(self, chunk, item, kinds):
        s, a, b, c = item
        if "z" in kinds:
            for far in range(1, self.depth):
                self.copy(chunk, item, (far, 0, 0, 0), (far, 0, 0, 0)).start()
        if "p" in kinds:
            self.copy(chunk, item, (0, 1, 0, 0), (s, 1, b, c)).start()
        if "q" in kinds:
            self.copy(chunk, item, (0, 0, 1, 0), (s, a, 1, c)).start()
        if "c" in kinds:
            self.copy(chunk, item, (0, 0, 0, 1), (s, a, b, 1)).start()

    def take(self, chunk, item, kinds):
        self.copy(chunk, item, (0, 0, 0, 1), item).wait_recv()
        self.send(chunk, item, kinds)

    def start(self, chunk):
        self.send(chunk, (0, 0, 0, 0), "zpqc")

    def after_z(self, chunk):
        for s in range(1, self.depth):
            self.take(chunk, (s, 0, 0, 0), "pqc")

    def after_p(self, chunk):
        for s in range(self.depth):
            self.take(chunk, (s, 1, 0, 0), "qc")

    def after_q(self, chunk):
        for s in range(self.depth):
            for a in range(2):
                self.take(chunk, (s, a, 1, 0), "c")

    def after_c(self, chunk):
        for s in range(self.depth):
            for a in range(2):
                for b in range(2):
                    self.take(chunk, (s, a, b, 1), "")

    def drain(self, chunk):
        for s in range(self.depth):
            for a in range(2):
                for b in range(2):
                    for c in range(2):
                        if s + a + b + c:
                            self.copy(chunk, (0, 0, 0, 0), (0, 0, 0, 1), (s, a, b, c)).wait_send()

    def each(self, stage, step):
        if 0 <= step < STEPS:
            for chunk in chunks_of(step):
                getattr(self, stage)(chunk)

    def slot(self, i):
        for stage, step in (("after_z", i), ("start", i + 2), ("after_p", i - 1), ("after_q", i - 2), ("after_c", i - 3)):
            self.each(stage, step)


def swap(half):
    return pltpu.roll(half, 64, 1)


def left_half(shape):
    return lax.broadcasted_iota(jnp.int32, shape, 1) < 64


def pack_block(block, odd):
    rows = block.shape[0]
    wide = jnp.concatenate([block, jnp.zeros((rows, 64), jnp.float32)], axis=1)
    turned = pltpu.roll(wide, 192, 1)
    main = jnp.where(odd, turned[:, :128], wide[:, :128])
    rest = jnp.where(left_half((rows, 128)), jnp.where(odd, wide[:, :128], wide[:, 128:]), 0.0)
    top, low = rest[: rows // 2], rest[rows // 2 :]
    return main, jnp.where(odd, swap(top) + low, top + swap(low))


def middle_of(even, odd):
    left = left_half(even.shape)
    return jnp.where(left, even, odd), swap(jnp.where(left, odd, even))


def put_block(land, d, at, rows, ref, row):
    half = rows // 2
    for pair in range(GRID[1] // 2):
        even, other = land.at[d, 2 * pair], land.at[d, 2 * pair + 1]
        left = 384 * pair
        ref[pl.ds(row, rows), left : left + 128] = even[at : at + rows, :]
        ref[pl.ds(row, rows), left + 256 : left + 384] = other[at : at + rows, :]
        top, low = middle_of(
            even[at + rows : at + rows + half, :].astype(jnp.float32),
            other[at + rows : at + rows + half, :].astype(jnp.float32),
        )
        ref[pl.ds(row, half), left + 128 : left + 256] = top.astype(jnp.bfloat16)
        ref[pl.ds(row + half, half), left + 128 : left + 256] = low.astype(jnp.bfloat16)


def norm_parts(values):
    centre = values - jnp.mean(values, axis=1, keepdims=True)
    spread = jnp.mean(centre * centre, axis=1, keepdims=True)
    recip = lax.rsqrt(spread + EPS_NORM)
    return centre * recip, recip


def gelu_parts(z):
    size = jnp.abs(z)
    base = 1.0 + 0.2316419 * size
    t = pl.reciprocal(base, approx=True)
    t = t * (2.0 - base * t)
    density = jnp.exp(z * z * -0.5) * 0.3989422804014327
    poly = t * (0.319381530 + t * (-0.356563782 + t * (1.781477937 + t * (-1.821255978 + t * 1.330274429))))
    tail = poly * density
    cdf = jnp.where(z < 0.0, tail, 1.0 - tail)
    return z * cdf, cdf + z * density


def forward_kernel(direct, *refs):
    if direct:
        q_ref, k_ref, v_ref, o_ref, upw_ref, downw_ref, small_ref = refs[:7]
        refs = refs[7:]
    else:
        square_in, up_in, down_in, vec_in, bup_in = refs[:5]
        refs = refs[5:]
    in_ref, seg_ref = refs[:2]
    (square_out, up_out, down_out, vec_ref, qkv_out, prob_out, turned_out, norm1_out, recip1_out,
     act_out, slope_out, mixed_out, norm2_out, recip2_out) = refs[2:16]
    (land, square, down, bup, qkv, prob, turned, ctx, first, flow, norm, recip, act, slope, act_turned, mixed,
     out_sem, pack_sem, tile_sem) = refs[16:35]
    packs = in_ref.shape[0] // LEN
    base = lax.axis_index("narrow") * packs
    pending = {}

    def save(name, src, dst):
        pending[name] = pltpu.make_async_copy(src, dst, out_sem.at[len(pending)])
        pending[name].start()

    if direct:
        send_sem, recv_sem = refs[35:37]
        dp, narrow = lax.axis_index("dp"), lax.axis_index("narrow")
        odd = lax.rem(narrow, 2) == 1
        own = land.at[dp, narrow]
        own[0:16, :] = small_ref[...]
        for i, ref in enumerate((q_ref, k_ref, v_ref, o_ref)):
            main, rest = pack_block(ref[...].astype(jnp.float32), odd)
            at = SQUARE + PART * i
            own[at : at + BLOCK, :] = main.astype(jnp.bfloat16)
            own[at + BLOCK : at + PART, :] = rest.astype(jnp.bfloat16)
        g = Gather(land, send_sem, recv_sem)
        greet(g.me, g.depth)
        g.start(VEC_CHUNK)
        g.each("start", 0)
        g.each("start", 1)
        for t in range(6):
            own[UP + BLOCK * t : UP + BLOCK * (t + 1), :] = upw_ref[:, 128 * t : 128 * (t + 1)]
        main, rest = pack_block(downw_ref[...].astype(jnp.float32), odd)
        own[DOWN : DOWN + 384, :] = main.astype(jnp.bfloat16)
        own[DOWN + 384 : DOWN + 576, :] = rest.astype(jnp.bfloat16)
        g.after_z(VEC_CHUNK)
        g.slot(0)
        g.after_p(VEC_CHUNK)
        g.slot(1)
        g.after_q(VEC_CHUNK)
        g.slot(2)
        g.after_c(VEC_CHUNK)
        g.slot(3)
        vec_ref[...] = jnp.zeros_like(vec_ref)
        for d in range(GRID[0]):
            tile = land[d, 0, 0:16, :].astype(jnp.float32)
            wide = jnp.concatenate([tile, jnp.zeros((16, 128), jnp.float32)], axis=1)
            at, shift = divmod(BLOCK * d, 128)
            wide = pltpu.roll(wide, shift, 1) if shift else wide
            vec_ref[:, 128 * at : 128 * at + 256] += wide
            bup[3 * d : 3 * d + 3, :] = tile[8:11]
            for i in range(2):
                put_block(land, d, SQUARE + PART * i, BLOCK, square, D * i + BLOCK * d)
        g.slot(4)
        for d in range(GRID[0]):
            for i in range(2, 4):
                put_block(land, d, SQUARE + PART * i, BLOCK, square, D * i + BLOCK * d)

        def tick(loop, index, pieces):
            for when, stage, step in pieces:
                pl.when(index == when)(lambda: g.each(stage, step))
    else:
        fills = [
            pltpu.make_async_copy(src, dst, out_sem.at[i])
            for i, (src, dst) in enumerate(
                ((square_in, square), (down_in, down), (up_in, land.at[:, :, pl.ds(UP, DOWN - UP), :]))
            )
        ]
        for copy in fills:
            copy.start()
        vec_ref[...] = vec_in[...]
        bup[...] = bup_in[...]
        for copy in fills:
            copy.wait()
        tick = lambda loop, index, pieces: None
    save("square", square, square_out)

    def pack_copies(p):
        k = p % 2
        at = pl.ds(pl.multiple_of(p * LEN, LEN), LEN)
        return [
            pltpu.make_async_copy(prob.at[k], prob_out.at[p], pack_sem.at[0, k]),
            pltpu.make_async_copy(qkv.at[k], qkv_out.at[at, :], pack_sem.at[1, k]),
            pltpu.make_async_copy(turned.at[k], turned_out.at[:, :, at], pack_sem.at[2, k]),
        ]

    def attend(p, carry):
        rows = pl.ds(pl.multiple_of(p * LEN, LEN), LEN)
        k = p % 2

        @pl.when(p >= 2)
        def _():
            for copy in pack_copies(p - 2):
                copy.wait()

        x = in_ref[rows, :]
        turned[k, 0] = jnp.transpose(x)
        for i in range(3):
            part = product(x, square[D * i : D * (i + 1), :])
            if i != 1:
                part = part + vec_ref[i // 2 : i // 2 + 1, :D]
            qkv[k, :, D * i : D * (i + 1)] = part.astype(jnp.bfloat16)
        tick("attend", p, ((0, "after_z", 5), (1, "after_q", 3), (2, "after_p", 5)))
        seg_row = seg_ref[pl.ds(base + p, 1), :].astype(jnp.float32)
        seg_col = jnp.transpose(jnp.broadcast_to(seg_row, (128, LEN)))
        same = jnp.concatenate([seg_col, seg_col], axis=1) == seg_row
        left = left_half((LEN, 128))
        for h in range(HEADS // 2):
            columns = slice(128 * h, 128 * (h + 1))
            query = qkv[k, :, columns] * jnp.asarray(HEAD_DIM**-0.5, jnp.bfloat16)
            keys = qkv[k, :, D + 128 * h : D + 128 * (h + 1)]
            values = qkv[k, :, 2 * D + 128 * h : 2 * D + 128 * (h + 1)]
            mixes = []
            for side in range(2):
                mine = left if side == 0 else jnp.logical_not(left)
                scores = product_right(jnp.where(mine, query, jnp.zeros_like(query)), keys)
                scores = jnp.where(same, scores, MASKED)
                shifted = jnp.exp(scores - jnp.max(scores, axis=1, keepdims=True))
                total = jnp.sum(shifted, axis=1, keepdims=True)
                low = (shifted * (1.0 / total)).astype(jnp.bfloat16)
                prob[k, 2 * h + side] = low
                mixes.append(product(low, values))
            ctx[:, columns] = jnp.where(left, mixes[0], mixes[1]).astype(jnp.bfloat16)
            if h == 3:
                tick("attend", p, ((0, "after_p", 4), (1, "after_c", 2), (2, "after_q", 4), (3, "after_c", 3)))
        turned[k, 1] = jnp.transpose(ctx[...])
        total = x.astype(jnp.float32) + (product(ctx[...], square[3 * D :, :]) + vec_ref[2:3, :D])
        normed, scale = norm_parts(total)
        value = normed * vec_ref[3:4, :D] + vec_ref[4:5, :D]
        first[rows, :] = value
        low = value.astype(jnp.bfloat16)
        flow[rows, :] = low
        turned[k, 2] = jnp.transpose(low)
        norm[rows, :] = normed
        recip[0, rows, :] = jnp.broadcast_to(scale, (LEN, 128))
        for copy in pack_copies(p):
            copy.start()
        return carry

    lax.fori_loop(0, packs, attend, 0)
    save("norm", norm, norm1_out)
    save("recip", recip.at[0], recip1_out)
    for p in (packs - 2, packs - 1):
        for copy in pack_copies(p):
            copy.wait()

    def tile_copies(t):
        k = t % 2
        copies = []
        for n in range(GRID[1]):
            columns = pl.ds(pl.multiple_of(D * n + 128 * t, 128), 128)
            first_row = pl.multiple_of(UP + BLOCK * t, 16)
            copies += [
                pltpu.make_async_copy(slope.at[k, n], slope_out.at[:, columns], tile_sem.at[0, k, n]),
                pltpu.make_async_copy(act_turned.at[k, n], act_out.at[columns, :], tile_sem.at[1, k, n]),
                pltpu.make_async_copy(
                    land.at[:, n, pl.ds(first_row, BLOCK), :], up_out.at[:, :, columns], tile_sem.at[2, k, n]
                ),
            ]
        return copies

    def widen(t, carry):
        k = t % 2

        @pl.when(t >= 2)
        def _():
            for copy in tile_copies(t - 2):
                copy.wait()

        first_row = pl.multiple_of(UP + BLOCK * t, 16)
        for pair in range(2):
            weight = jnp.concatenate(
                [land[:, 2 * pair + i, pl.ds(first_row, BLOCK), :].reshape(D, 128) for i in range(2)], axis=1
            )
            bias = jnp.concatenate([bup[pl.ds(6 * (2 * pair + i) + t, 1), :] for i in range(2)], axis=1)
            for r in range(packs):
                rows = slice(LEN * r, LEN * (r + 1))
                value, turn = gelu_parts(product(flow[rows, :], weight) + bias)
                value, turn = value.astype(jnp.bfloat16), turn.astype(jnp.bfloat16)
                back = jnp.transpose(value)
                for i in range(2):
                    n = 2 * pair + i
                    columns = pl.ds(pl.multiple_of(D * n + 128 * t, 128), 128)
                    act[rows, columns] = value[:, 128 * i : 128 * (i + 1)]
                    act_turned[k, n, :, rows] = back[128 * i : 128 * (i + 1), :]
                    slope[k, n, rows, :] = turn[:, 128 * i : 128 * (i + 1)]
        tick("widen", t, ((0, "after_q", 5), (1, "after_c", 4)))
        for copy in tile_copies(t):
            copy.start()
        return carry

    lax.fori_loop(0, 6, widen, 0)
    if direct:
        g.each("after_c", 5)
        for d in range(GRID[0]):
            put_block(land, d, DOWN, 384, down, 384 * d)
    save("down", down, down_out)
    pending["norm"].wait()

    def finish(p, carry):
        rows = pl.ds(pl.multiple_of(p * LEN, LEN), LEN)
        total = first[rows, :] + (product(act[rows, :], down[...]) + vec_ref[5:6, :D])
        normed, scale = norm_parts(total)
        norm[rows, :] = normed
        recip[1, rows, :] = jnp.broadcast_to(scale, (LEN, 128))
        mixed[rows, :] = (normed * vec_ref[6:7, :D] + vec_ref[7:8, :D]).astype(jnp.bfloat16)
        return carry

    lax.fori_loop(0, packs, finish, 0)
    save("mixed", mixed, mixed_out)
    save("norm2", norm, norm2_out)
    save("recip2", recip.at[1], recip2_out)
    for t in (4, 5):
        for copy in tile_copies(t):
            copy.wait()
    if direct:
        for chunk in [VEC_CHUNK] + [chunk for step in range(STEPS) for chunk in chunks_of(step)]:
            g.drain(chunk)
    for name, copy in pending.items():
        if name != "norm":
            copy.wait()


def forward_step(direct, weights, inputs, segments, dp, narrow):
    rows = inputs.shape[0]
    packs = rows // LEN
    vmem = pl.BlockSpec(memory_space=pltpu.VMEM)
    anywhere = pl.BlockSpec(memory_space=pl.ANY)
    low = lambda *shape: jax.ShapeDtypeStruct(shape, jnp.bfloat16)
    full = lambda *shape: jax.ShapeDtypeStruct(shape, jnp.float32)
    room = lambda *shape: pltpu.VMEM(shape, jnp.bfloat16)
    wide = lambda *shape: pltpu.VMEM(shape, jnp.float32)
    sems = [pltpu.SemaphoreType.DMA((2 * STEPS + 1, 32))] * 2 if direct else []
    return pl.pallas_call(
        functools.partial(forward_kernel, direct),
        name="forward",
        out_shape=(
            low(FF, D), low(GRID[0], BLOCK, FF), low(FF, D), full(16, 896),
            low(rows, 3 * D), low(packs, HEADS, LEN, LEN), low(3, D, rows), full(rows, D), full(rows, 128),
            low(FF, rows), low(rows, FF), low(rows, D), full(rows, D), full(rows, 128),
        ),
        in_specs=([vmem] * 7 if direct else [anywhere] * 3 + [vmem] * 2) + [vmem] * 2,
        out_specs=(anywhere,) * 3 + (vmem,) + (anywhere,) * 10,
        scratch_shapes=[
            room(*GRID, TOTAL, 128), room(FF, D), room(FF, D), wide(32, 128),
            room(2, LEN, 3 * D), room(2, HEADS, LEN, LEN), room(2, 3, D, LEN), room(LEN, D), wide(rows, D), room(rows, D),
            wide(rows, D), wide(2, rows, 128), room(rows, FF), room(2, 4, rows, 128), room(2, 4, 128, rows), room(rows, D),
            pltpu.SemaphoreType.DMA((12,)), pltpu.SemaphoreType.DMA((3, 2)), pltpu.SemaphoreType.DMA((3, 2, 4)),
            *sems,
        ],
        compiler_params=pltpu.CompilerParams(
            vmem_limit_bytes=VMEM_LIMIT, **(dict(collective_id=0, has_side_effects=True) if direct else {})
        ),
    )(*weights, inputs, segments)


def transport_kernel(
    mixed_ref, seg_ref, kind_ref, weight_ref, cot_ref, normed_ref, recip_ref, gain_ref,
    value_ref, second_ref, branch_ref, sums_ref,
    kern_ref, prod_ref, flow_ref, acc_ref, left_ref, sigma_ref,
):
    packs = mixed_ref.shape[0] // LEN
    base = lax.axis_index("narrow") * packs
    blocks = LEN // ROWS
    lanes = lambda col: jnp.concatenate([col, col], axis=1)
    fold = lambda wide: wide[:, :128] + wide[:, 128:]
    eight = lambda wide: jnp.sum(wide.reshape(ROWS // 8, 8, LEN), axis=0)
    replicate = lambda col: jnp.broadcast_to(col, (ROWS, 128))

    def turned(row):
        return jnp.transpose(jnp.broadcast_to(row, (128, LEN)))

    for p in range(packs):
        rows = pl.ds(p * LEN, LEN)
        feats = mixed_ref[rows, :].astype(jnp.float32)
        recip = lax.rsqrt(jnp.sum(feats * feats, axis=1, keepdims=True) + EPS_NORM)
        unit = (feats * recip).astype(jnp.bfloat16)
        cosine = product_right(unit, unit)
        seg_row = seg_ref[pl.ds(base + p, 1), :].astype(jnp.float32)
        region_row = jnp.where(kind_ref[pl.ds(base + p, 1), :] == 0, 0.0, 1.0)
        seg_col = turned(seg_row)
        word_col = 1.0 - turned(region_row)
        same = jnp.where(lanes(seg_col) == seg_row, 1.0, 0.0)
        word_count = jnp.sum(same * (1.0 - region_row), axis=1, keepdims=True)
        region_count = jnp.sum(same * lanes(1.0 - word_col), axis=0, keepdims=True)
        kern_ref[p] = jnp.exp((cosine - 1.0) * (1.0 / BETA)) * same * lanes(word_col) * region_row
        left_ref[p, 0] = word_col
        left_ref[p, 1] = jnp.broadcast_to(word_count, (LEN, 128))
        prod_ref[0, p] = jnp.ones((LEN, LEN), jnp.float32)
        sigma_ref[0, p, 0:1] = region_row / region_count
        sigma_ref[0, p, 1:2] = region_row
        sigma_ref[0, p, 2:3] = region_count

    def advance(t, carry):
        for p in range(packs):
            sigma = sigma_ref[t, p, 0:1]
            scale = jnp.where(t == 0, 1.0, sigma)
            region = sigma_ref[0, p, 1:2]
            count = sigma_ref[0, p, 2:3]
            total = jnp.zeros((8, LEN), jnp.float32)
            for b in range(blocks):
                rows = pl.ds(b * ROWS, ROWS)
                weighted = kern_ref[p, rows, :] * (prod_ref[t, p, rows, :] * scale)
                row_sum = jnp.sum(fold(weighted * sigma), axis=1, keepdims=True)
                word = left_ref[p, 0, rows, :]
                delta = word / (left_ref[p, 1, rows, :] * replicate(row_sum) + 1.0 - word)
                scaled = weighted * lanes(delta)
                prod_ref[t + 1, p, rows, :] = scaled
                total = total + eight(scaled)
            col_sum = jnp.sum(total, axis=0, keepdims=True)
            sigma_ref[t + 1, p, 0:1] = region / (count * col_sum + 1.0 - region)
        return carry

    lax.fori_loop(0, ITERS, advance, 0)

    starts = []
    for p in range(packs):
        rows = pl.ds(p * LEN, LEN)
        weight = weight_ref[base + p]
        feats = mixed_ref[rows, :].astype(jnp.float32)
        recip = lax.rsqrt(jnp.sum(feats * feats, axis=1, keepdims=True) + EPS_NORM)
        unit = (feats * recip).astype(jnp.bfloat16)
        cosine = product_right(unit, unit)
        moved = (prod_ref[ITERS, p] * sigma_ref[ITERS, p, 0:1]) * (1.0 - cosine)
        value_ref[p : p + 1, :] = jnp.broadcast_to(jnp.sum(moved), (1, 128))
        moved = moved * weight
        flow_ref[p] = moved
        acc_ref[p] = jnp.zeros((LEN, LEN), jnp.float32)
        starts += [jnp.sum(moved, axis=0, keepdims=True), jnp.zeros((1, LEN), jnp.float32)]

    def retreat(step, carry):
        t = ITERS - 1 - step
        out = []
        for p in range(packs):
            flow_sum, spread = carry[2 * p : 2 * p + 2]
            before = sigma_ref[t, p, 0:1]
            d_col = -sigma_ref[0, p, 2:3] * sigma_ref[t + 1, p, 0:1] * (spread + flow_sum)
            total = jnp.zeros((8, LEN), jnp.float32)
            shift = jnp.zeros((8, LEN), jnp.float32)
            for b in range(blocks):
                rows = pl.ds(b * ROWS, ROWS)
                scaled = prod_ref[t + 1, p, rows, :]
                flow = flow_ref[p, rows, :] + scaled * d_col
                d_row = replicate(jnp.sum(fold(flow), axis=1, keepdims=True))
                d_row = -left_ref[p, 1, rows, :] * d_row
                moved = scaled * lanes(d_row)
                flow = flow + moved * before
                flow_ref[p, rows, :] = flow
                acc_ref[p, rows, :] = acc_ref[p, rows, :] + flow
                total = total + eight(flow)
                shift = shift + eight(moved)
            out += [
                jnp.sum(total, axis=0, keepdims=True),
                before * jnp.sum(shift, axis=0, keepdims=True),
            ]
        return tuple(out)

    lax.fori_loop(0, ITERS, retreat, tuple(starts))

    sums = [jnp.zeros((1, D), jnp.float32)] * 3
    for p in range(packs):
        rows = pl.ds(p * LEN, LEN)
        coupling = prod_ref[ITERS, p] * sigma_ref[ITERS, p, 0:1]
        d_cost = weight_ref[base + p] * coupling - acc_ref[p] * (1.0 / BETA)
        d_cosine = (-d_cost).astype(jnp.bfloat16)
        feats = mixed_ref[rows, :].astype(jnp.float32)
        recip = lax.rsqrt(jnp.sum(feats * feats, axis=1, keepdims=True) + EPS_NORM)
        unit = feats * recip
        unit_low = unit.astype(jnp.bfloat16)
        d_unit = product(d_cosine, unit_low) + product_left(d_cosine, unit_low)
        d_mixed = cot_ref[rows, :].astype(jnp.float32) + recip * (
            d_unit - unit * jnp.sum(d_unit * unit, axis=1, keepdims=True)
        )
        normed = normed_ref[rows, :]
        scaled = d_mixed * gain_ref[...]
        inner_mean = jnp.mean(scaled, axis=1, keepdims=True)
        cross_mean = jnp.mean(scaled * normed, axis=1, keepdims=True)
        d_second = recip_ref[rows, 0:1] * (scaled - inner_mean - normed * cross_mean)
        d_branch = d_second.astype(jnp.bfloat16)
        second_ref[rows, :] = d_second
        branch_ref[rows, :] = d_branch
        sums[0] = sums[0] + jnp.sum(d_mixed * normed, axis=0, keepdims=True)
        sums[1] = sums[1] + jnp.sum(d_mixed, axis=0, keepdims=True)
        sums[2] = sums[2] + jnp.sum(d_branch.astype(jnp.float32), axis=0, keepdims=True)
    for k in range(3):
        sums_ref[k : k + 1, :] = sums[k]


def transport_step(mixed, segments, row_kind, weight, cotangent, normed, recip, gain):
    rows = mixed.shape[0]
    packs = rows // LEN
    vmem = pl.BlockSpec(memory_space=pltpu.VMEM)
    square = (packs, LEN, LEN)
    return pl.pallas_call(
        transport_kernel,
        name="transport",
        out_shape=(
            jax.ShapeDtypeStruct((packs, 128), jnp.float32),
            jax.ShapeDtypeStruct((rows, D), jnp.float32),
            jax.ShapeDtypeStruct((rows, D), jnp.bfloat16),
            jax.ShapeDtypeStruct((8, D), jnp.float32),
        ),
        in_specs=[vmem, vmem, vmem, pl.BlockSpec(memory_space=pltpu.SMEM), vmem, vmem, vmem, vmem],
        out_specs=(vmem, vmem, vmem, vmem),
        scratch_shapes=[
            pltpu.VMEM(square, jnp.float32),
            pltpu.VMEM((ITERS + 1, *square), jnp.float32),
            pltpu.VMEM(square, jnp.float32),
            pltpu.VMEM(square, jnp.float32),
            pltpu.VMEM((packs, 2, LEN, 128), jnp.float32),
            pltpu.VMEM((ITERS + 1, packs, 8, LEN), jnp.float32),
        ],
        compiler_params=pltpu.CompilerParams(vmem_limit_bytes=VMEM_LIMIT),
    )(mixed, segments, row_kind, weight, cotangent, normed, recip, gain)


class Scatter:
    def __init__(self, part, lands, send_sem, recv_sem, credit):
        self.part, self.lands, self.send_sem, self.recv_sem, self.credit = part, lands, send_sem, recv_sem, credit
        self.me = hops()
        self.depth = part.shape[0] // 2

    def block(self, chunk, item):
        row, first, rows, order = chunk
        owner = place(self.me, self.depth, item, order)
        return self.part.at[owner[0], owner[1], pl.ds(first, rows), :]

    def landing(self, chunk, item):
        row, first, rows, order = chunk
        s, a, b, c = item
        span = pl.ds(first, rows)
        if c:
            step, at = divmod(first - SQUARE, STEP) if first else (2, 0)
            slot = (step % 2) * STEP + at if first else 2 * STEP
            return self.lands[0].at[(s * 2 + a) * 2 + b, pl.ds(slot, rows), :]
        if b:
            return self.lands[1].at[s * 2 + a, span, :]
        if a:
            return self.lands[2].at[s, span, :]
        return self.lands[3].at[s - 1, span, :]

    def copy(self, chunk, item):
        s, a, b, c = item
        hop = (0, 0, 0, 1) if c else (0, 0, 1, 0) if b else (0, 1, 0, 0) if a else (s, 0, 0, 0)
        return pltpu.make_async_remote_copy(
            src_ref=self.block(chunk, item),
            dst_ref=self.landing(chunk, item),
            send_sem=self.send_sem.at[chunk[0], number(item)],
            recv_sem=self.recv_sem.at[chunk[0], number(item)],
            device_id=place(self.me, self.depth, hop, chunk[3]),
            device_id_type=MESH,
        )

    def take(self, chunk, item, into):
        self.copy(chunk, item).wait_recv()
        ref = self.block(chunk, into)
        ref[...] = (
            ref[...].astype(jnp.float32) + self.landing(chunk, item)[...].astype(jnp.float32)
        ).astype(jnp.bfloat16)

    def start(self, chunk):
        for s in range(self.depth):
            for a in range(2):
                for b in (1, 0):
                    self.copy(chunk, (s, a, b, 1)).start()

    def after_c(self, chunk):
        for b in (1, 0):
            for s in range(self.depth):
                for a in range(2):
                    self.take(chunk, (s, a, b, 1), (s, a, b, 0))
                    if b:
                        self.copy(chunk, (s, a, 1, 0)).start()

    def after_q(self, chunk):
        for a in (1, 0):
            for s in range(self.depth):
                self.take(chunk, (s, a, 1, 0), (s, a, 0, 0))
                if a:
                    self.copy(chunk, (s, 1, 0, 0)).start()

    def after_p(self, chunk):
        for s in [*range(1, self.depth), 0]:
            self.take(chunk, (s, 1, 0, 0), (s, 0, 0, 0))
            if s:
                self.copy(chunk, (s, 0, 0, 0)).start()

    def finish(self, chunk, total):
        for s in range(1, self.depth):
            self.copy(chunk, (s, 0, 0, 0)).wait_recv()
        value = self.block(chunk, (0, 0, 0, 0))[...].astype(jnp.float32)
        for s in range(1, self.depth):
            value = value + self.landing(chunk, (s, 0, 0, 0))[...].astype(jnp.float32)
        total[pl.ds(chunk[1], chunk[2]), :] = value

    def drain(self, chunk):
        for s in range(self.depth):
            for a in range(2):
                for b in range(2):
                    for c in range(2):
                        if s + a + b + c:
                            self.copy(chunk, (s, a, b, c)).wait_send()

    def tick(self, stage, step, total):
        if stage == "start" and step < STEPS - 2:
            pl.semaphore_wait(self.credit, 1)
        for chunk in chunks_of(step):
            if stage == "finish":
                self.finish(chunk, total)
            else:
                getattr(self, stage)(chunk)
        if stage == "after_c" and step >= 2:
            other = place(self.me, self.depth, (0, 0, 0, 1), "x")
            pl.semaphore_signal(self.credit, inc=1, device_id=other, device_id_type=MESH)


def fold_middle(top, low):
    left = left_half(top.shape)
    return jnp.where(left, top, swap(low)), jnp.where(left, swap(low), top)


def take_block(part, d, at, rows, block, pair):
    even, other = part.at[d, 2 * pair], part.at[d, 2 * pair + 1]
    half = rows // 2
    even[at : at + rows, :] = block[:, :128].astype(jnp.bfloat16)
    other[at : at + rows, :] = block[:, 256:].astype(jnp.bfloat16)
    one, two = fold_middle(block[:half, 128:256], block[half:, 128:256])
    even[at + rows : at + rows + half, :] = one.astype(jnp.bfloat16)
    other[at + rows : at + rows + half, :] = two.astype(jnp.bfloat16)


def unpack_block(main, rest, odd):
    other = swap(rest)
    top, low = jnp.where(odd, other, rest), jnp.where(odd, rest, other)
    piece = jnp.concatenate([top, low], axis=0)
    left = left_half(piece.shape)
    swapped = swap(main)
    first = jnp.where(odd, jnp.where(left, piece, swapped), main)
    second = jnp.where(odd, swapped, piece)
    return jnp.concatenate([first, second[:, :64]], axis=1)


def backward_kernel(direct, *refs):
    (act_in, slope_in, branch_in, second_in, sums_in, turned_in, norm_in, recip_in, qkv_in, prob_in,
     square_in, up_in, down_in, vec_ref) = refs[:14]
    refs = refs[14:]
    if direct:
        grad_in_out, gq_ref, gk_ref, gv_ref, go_ref, gup_ref, gdown_ref, gvec_ref = refs[:8]
        refs = refs[8:]
    else:
        grad_in_out, gsquare_ref, gup_ref, gdown_ref, gvec_ref, gbup_ref = refs[:6]
        refs = refs[6:]
    turned, slope, square, up, flow, norm, recip, branch, prob, sums, bup, load_sem, prob_sem, out_sem = refs[:14]
    rows_all = slope.shape[0]
    packs = rows_all // LEN
    if direct:
        part, land_c, land_q, land_p, land_z, total, send_sem, recv_sem, credit = refs[14:23]
        g = Scatter(part, (land_c, land_q, land_p, land_z), send_sem, recv_sem, credit)
        odd = lax.rem(lax.axis_index("narrow"), 2) == 1
    else:
        (stage,) = refs[14:15]

    loads = {}

    def load(name, src, dst):
        loads[name] = pltpu.make_async_copy(src, dst, load_sem.at[len(loads)])
        loads[name].start()

    load("branch", branch_in, branch)
    load("act", act_in, turned)
    load("down", down_in, square)
    load("slope", slope_in, slope)
    load("up", up_in, up)
    load("flow", second_in, flow)
    load("norm", norm_in, norm)
    load("recip", recip_in, recip)
    if direct:
        greet(g.me, g.depth)

    def tick(index, pieces):
        if direct:
            for when, name, step in pieces:
                if isinstance(index, int):
                    if index == when:
                        g.tick(name, step, total)
                else:
                    pl.when(index == when)(lambda: g.tick(name, step, total))

    sums[...] = jnp.zeros_like(sums)
    bup[...] = jnp.zeros_like(bup)
    sums[5:6, :D] = sums_in[2:3, :]
    sums[6:7, :D] = sums_in[0:1, :]
    sums[7:8, :D] = sums_in[1:2, :]
    loads["branch"].wait()
    loads["act"].wait()

    def put_down(d, carry):
        at = pl.multiple_of(384 * d, 128)
        grad = product(turned[pl.ds(at, 384), :], branch[...])
        if direct:
            for pair in range(2):
                take_block(part, d, DOWN, 384, grad[:, 384 * pair : 384 * (pair + 1)], pair)
        else:
            stage[0, 0:384, :] = grad
            copy = pltpu.make_async_copy(stage.at[0, pl.ds(0, 384), :], gdown_ref.at[pl.ds(at, 384), :], out_sem.at[0])
            copy.start()
            copy.wait()
        return carry

    lax.fori_loop(0, 8, put_down, 0)
    tick(0, ((0, "start", 5), (0, "start", 4)))
    load("turned", turned_in, turned.at[pl.ds(0, 3 * D), :])
    loads["down"].wait()
    loads["slope"].wait()

    def narrow_down(c, carry):
        at = pl.multiple_of(256 * c, 128)
        columns = pl.ds(at, 256)
        weight = square[pl.ds(at, 256), :]
        column_sum = jnp.zeros((1, 256), jnp.float32)
        for r in range(packs):
            rows = slice(LEN * r, LEN * (r + 1))
            value = product_right(branch[rows, :], weight) * slope[rows, columns].astype(jnp.float32)
            low = value.astype(jnp.bfloat16)
            slope[rows, columns] = low
            column_sum = column_sum + jnp.sum(low.astype(jnp.float32), axis=0, keepdims=True)
        bup[pl.ds(2 * c, 1), :] = column_sum[:, :128]
        bup[pl.ds(2 * c + 1, 1), :] = column_sum[:, 128:]
        tick(c, ((3, "after_c", 5), (6, "after_c", 4)))
        return carry

    lax.fori_loop(0, 12, narrow_down, 0)
    load("square", square_in, square)
    loads["turned"].wait()

    def put_up(i, carry):
        t, pair = i // 2, i % 2
        first_row = pl.multiple_of(UP + BLOCK * t, 16)
        at = [pl.multiple_of(D * (2 * pair + j) + 128 * t, 128) for j in range(2)]
        columns = jnp.concatenate([slope[:, pl.ds(at[j], 128)] for j in range(2)], axis=1)
        grad = product(turned[2 * D : 3 * D, :], columns)
        for j in range(2):
            block = grad[:, 128 * j : 128 * (j + 1)]
            if direct:
                part[:, 2 * pair + j, pl.ds(first_row, BLOCK), :] = block.astype(jnp.bfloat16).reshape(GRID[0], BLOCK, 128)
            else:
                stage[j, :, :128] = block
                copy = pltpu.make_async_copy(stage.at[j, :, pl.ds(0, 128)], gup_ref.at[:, pl.ds(at[j], 128)], out_sem.at[j])
                copy.start()
                copy.wait()
        tick(i, ((6, "after_q", 5),))
        return carry

    lax.fori_loop(0, 12, put_up, 0)
    tick(0, ((0, "start", 3), (0, "start", 2)))
    for name in ("up", "flow", "norm", "recip"):
        loads[name].wait()

    def norm_back(r, carry):
        rows = pl.ds(pl.multiple_of(r * LEN, LEN), LEN)
        d_first = flow[rows, :] + product_right(slope[rows, :], up[...])
        normed = norm[rows, :]
        scaled = d_first * vec_ref[3:4, :D]
        inner_mean = jnp.mean(scaled, axis=1, keepdims=True)
        cross_mean = jnp.mean(scaled * normed, axis=1, keepdims=True)
        d_sum = recip[rows, 0:1] * (scaled - inner_mean - normed * cross_mean)
        flow[rows, :] = d_sum
        low = d_sum.astype(jnp.bfloat16)
        branch[rows, :] = low
        sums[3:4, :D] += jnp.sum(d_first * normed, axis=0, keepdims=True)
        sums[4:5, :D] += jnp.sum(d_first, axis=0, keepdims=True)
        sums[2:3, :D] += jnp.sum(low.astype(jnp.float32), axis=0, keepdims=True)
        tick(r, ((0, "after_c", 3), (2, "after_c", 2), (3, "after_q", 4)))
        return carry

    lax.fori_loop(0, packs, norm_back, 0)
    load("qkv", qkv_in, slope.at[:, pl.ds(0, 3 * D)])

    def put_square(i, left, right):
        for pair in range(2):
            grad = product(left, right[:, 384 * pair : 384 * (pair + 1)])
            if direct:
                for d in range(GRID[0]):
                    take_block(part, d, SQUARE + PART * i, BLOCK, grad[BLOCK * d : BLOCK * (d + 1)], pair)
            else:
                stage[0, :, :384] = grad
                copy = pltpu.make_async_copy(
                    stage.at[0, :, pl.ds(0, 384)], gsquare_ref.at[pl.ds(D * i, D), pl.ds(384 * pair, 384)], out_sem.at[0]
                )
                copy.start()
                copy.wait()

    put_square(3, turned[D : 2 * D, :], branch)
    loads["square"].wait()
    loads["qkv"].wait()
    for r in range(packs):
        rows = slice(LEN * r, LEN * (r + 1))
        slope[rows, 3 * D :] = product_right(branch[rows, :], square[3 * D :, :]).astype(jnp.bfloat16)
    tick(0, ((0, "after_q", 3),))

    def prob_copy(p):
        return pltpu.make_async_copy(prob_in.at[p], prob.at[p % 2], prob_sem.at[p % 2])

    prob_copy(0).start()

    def attend(p, carry):
        rows = pl.ds(pl.multiple_of(p * LEN, LEN), LEN)
        k = p % 2
        pl.when(p + 1 < packs)(lambda: prob_copy(p + 1).start())
        prob_copy(p).wait()
        left = left_half((LEN, 128))
        for h in range(HEADS // 2):
            columns = slice(128 * h, 128 * (h + 1))
            key_columns = slice(D + 128 * h, D + 128 * (h + 1))
            value_columns = slice(2 * D + 128 * h, 2 * D + 128 * (h + 1))
            query, keys, values = slope[rows, columns], slope[rows, key_columns], slope[rows, value_columns]
            d_context = slope[rows, 3 * D + 128 * h : 3 * D + 128 * (h + 1)]
            d_values, d_query, d_keys = [], [], []
            for side in range(2):
                mine = left if side == 0 else jnp.logical_not(left)
                low = prob[k, 2 * h + side]
                d_values.append(product_left(low, d_context))
                d_prob = product_right(jnp.where(mine, d_context, jnp.zeros_like(d_context)), values)
                share = low.astype(jnp.float32)
                moved = share * d_prob
                d_scores = (moved - share * jnp.sum(moved, axis=1, keepdims=True)).astype(jnp.bfloat16)
                d_query.append(product(d_scores, keys))
                d_keys.append(product_left(d_scores, query))
            scale = HEAD_DIM**-0.5
            low_query = (jnp.where(left, *d_query) * scale).astype(jnp.bfloat16)
            low_values = jnp.where(left, *d_values).astype(jnp.bfloat16)
            slope[rows, columns] = low_query
            slope[rows, key_columns] = (jnp.where(left, *d_keys) * scale).astype(jnp.bfloat16)
            slope[rows, value_columns] = low_values
            sums[0:1, columns] += jnp.sum(low_query.astype(jnp.float32), axis=0, keepdims=True)
            sums[1:2, columns] += jnp.sum(low_values.astype(jnp.float32), axis=0, keepdims=True)
        tick(p, ((0, "after_p", 5), (1, "after_q", 2), (2, "after_p", 4)))
        return carry

    lax.fori_loop(0, packs, attend, 0)
    for i in range(3):
        put_square(i, turned[0:D, :], slope[:, D * i : D * (i + 1)])
    if direct:
        for d in range(GRID[0]):
            at, shift = divmod(BLOCK * d, 128)
            wide = sums[:, 128 * at : 128 * at + 256]
            wide = pltpu.roll(wide, 256 - shift, 1) if shift else wide
            mine = lax.broadcasted_iota(jnp.int32, (8, 128), 1) < BLOCK
            tile = jnp.concatenate([jnp.where(mine, wide[:8, :128], 0.0), bup[3 * d : 3 * d + 8, :]], axis=0)
            for n in range(GRID[1]):
                part[d, n, 0:16, :] = tile.astype(jnp.bfloat16)
        tick(0, ((0, "start", 1), (0, "start", 0)))
        g.start(VEC_CHUNK)
    tick(0, ((0, "after_p", 3), (0, "after_c", 1), (0, "after_c", 0)))
    if direct:
        g.after_c(VEC_CHUNK)

    def widen_back(r, carry):
        rows = pl.ds(pl.multiple_of(r * LEN, LEN), LEN)
        value = flow[rows, :]
        for i in range(3):
            value = value + product_right(slope[rows, D * i : D * (i + 1)], square[D * i : D * (i + 1), :])
        norm[rows, :] = value
        tick(r, ((1, "after_p", 2),))
        return carry

    lax.fori_loop(0, packs, widen_back, 0)
    result = pltpu.make_async_copy(norm, grad_in_out, out_sem.at[0])
    result.start()
    if direct:
        tick(0, ((0, "finish", 5), (0, "finish", 4), (0, "after_q", 1), (0, "after_q", 0)))
        g.after_q(VEC_CHUNK)
        tick(0, ((0, "finish", 3), (0, "finish", 2), (0, "after_p", 1), (0, "after_p", 0)))
        g.after_p(VEC_CHUNK)
        for t in range(6):
            gup_ref[:, 128 * t : 128 * (t + 1)] = total[UP + BLOCK * t : UP + BLOCK * (t + 1), :]
        gdown_ref[...] = unpack_block(total[DOWN : DOWN + 384, :], total[DOWN + 384 : DOWN + 576, :], odd)
        tick(0, ((0, "finish", 1), (0, "finish", 0)))
        g.finish(VEC_CHUNK, total)
        gvec_ref[...] = total[0:16, :]
        for i, ref in enumerate((gq_ref, gk_ref, gv_ref, go_ref)):
            at = SQUARE + PART * i
            ref[...] = unpack_block(total[at : at + BLOCK, :], total[at + BLOCK : at + PART, :], odd)
        for chunk in [VEC_CHUNK] + [chunk for step in range(STEPS) for chunk in chunks_of(step)]:
            g.drain(chunk)
    else:
        gvec_ref[...] = sums[...]
        gbup_ref[...] = bup[...]
    result.wait()


def backward_step(direct, operands, dp, narrow):
    rows = operands[1].shape[0]
    vmem = pl.BlockSpec(memory_space=pltpu.VMEM)
    anywhere = pl.BlockSpec(memory_space=pl.ANY)
    full = lambda *shape: jax.ShapeDtypeStruct(shape, jnp.float32)
    room = lambda *shape: pltpu.VMEM(shape, jnp.bfloat16)
    wide = lambda *shape: pltpu.VMEM(shape, jnp.float32)
    if direct:
        outs = [full(D // dp, D // narrow)] * 4 + [full(D // dp, FF // narrow), full(FF // dp, D // narrow), full(16, 128)]
        places = [vmem] * 7
        depth = dp // 2
        extra = [
            room(*GRID, TOTAL, 128), room(4 * depth, 2 * STEP + SQUARE, 128), room(2 * depth, TOTAL, 128),
            room(depth, TOTAL, 128), room(depth - 1, TOTAL, 128), wide(TOTAL, 128),
            pltpu.SemaphoreType.DMA((2 * STEPS + 1, 32)), pltpu.SemaphoreType.DMA((2 * STEPS + 1, 32)),
            pltpu.SemaphoreType.REGULAR,
        ]
    else:
        outs = [full(FF, D), full(D, FF), full(FF, D), full(16, 896), full(32, 128)]
        places = [anywhere] * 3 + [vmem] * 2
        extra = [wide(2, D, D)]
    return pl.pallas_call(
        functools.partial(backward_kernel, direct),
        name="backward",
        out_shape=(full(rows, D), *outs),
        in_specs=[anywhere] * 4 + [vmem] + [anywhere] * 8 + [vmem],
        out_specs=(anywhere, *places),
        scratch_shapes=[
            room(FF, rows), room(rows, FF), room(FF, D), room(D, FF), wide(rows, D), wide(rows, D), wide(rows, 128),
            room(rows, D), room(2, HEADS, LEN, LEN), wide(16, 896), wide(32, 128),
            pltpu.SemaphoreType.DMA((12,)), pltpu.SemaphoreType.DMA((2,)), pltpu.SemaphoreType.DMA((2,)),
            *extra,
        ],
        compiler_params=pltpu.CompilerParams(
            vmem_limit_bytes=VMEM_LIMIT, **(dict(collective_id=1, has_side_effects=True) if direct else {})
        ),
    )(*operands)


def per_device(
    inputs,
    segments,
    row_kind,
    query_weight,
    query_bias,
    key_weight,
    value_weight,
    value_bias,
    output_weight,
    output_bias,
    first_gain,
    first_shift,
    up_weight,
    up_bias,
    down_weight,
    down_bias,
    second_gain,
    second_shift,
    out_cotangent,
    loss_cotangent,
):
    row_count = inputs.shape[0]
    matrices = (query_weight, key_weight, value_weight, output_weight, up_weight, down_weight)
    vectors = (
        query_bias,
        value_bias,
        output_bias,
        first_gain,
        first_shift,
        down_bias,
        second_gain,
        second_shift,
        up_bias,
    )
    dp, narrow = lax.axis_size("dp"), lax.axis_size("narrow")
    direct = (dp, narrow, row_count) == (*GRID, 4 * LEN)
    if direct:
        small = jnp.stack([jnp.pad(item, (0, 128 - BLOCK)) for item in vectors[:8]])
        small = jnp.concatenate([small, vectors[8].reshape(3, 128), jnp.zeros((5, 128), jnp.bfloat16)])
        weights = (*matrices, small)
    else:
        weights = fetch_weights(matrices, vectors)
    (square, up, down, vecs, qkv, prob, turned, norm_first, recip_first, active, slope, output_low, norm_second,
     recip_second) = forward_step(direct, weights, inputs, segments, dp, narrow)
    group_out = lax.all_gather(output_low, "narrow", axis=0, tiled=True)
    partial_value, d_second, d_branch, sums_second = transport_step(
        output_low, segments, row_kind, loss_cotangent, out_cotangent, norm_second, recip_second, vecs[6:7, :D]
    )
    transport_loss = lax.all_gather(partial_value[:, 0], "narrow", axis=0, tiled=True)
    grad_inputs, *grads = backward_step(
        direct,
        (active, slope, d_branch, d_second, sums_second, turned.reshape(3 * D, row_count), norm_first, recip_first, qkv, prob, square,
         up.reshape(D, FF), down, vecs),
        dp,
        narrow,
    )
    if direct:
        mats, vec = grads[:6], grads[6]
        vecs = [vec[i, :BLOCK] for i in range(8)] + [vec[8:11].reshape(FF // dp)]
    else:
        squares, g_up, g_down, small, tiles = grads
        mats, vecs = reduce_grads(
            [*squares.reshape(4, D, D), g_up, g_down], [*small[:8, :D], tiles[:24].reshape(FF)]
        )
    return (
        group_out,
        transport_loss,
        grad_inputs,
        mats[0],
        vecs[0],
        mats[1],
        mats[2],
        vecs[1],
        mats[3],
        vecs[2],
        vecs[3],
        vecs[4],
        mats[4],
        vecs[8],
        mats[5],
        vecs[5],
        vecs[6],
        vecs[7],
    )


def solution(mesh):
    return jax.shard_map(
        per_device,
        mesh=mesh,
        in_specs=(
            P(("dp", "narrow"), None),
            P("dp", None),
            P("dp", None),
            P("dp", "narrow"),
            P("dp"),
            P("dp", "narrow"),
            P("dp", "narrow"),
            P("dp"),
            P("dp", "narrow"),
            P("dp"),
            P("dp"),
            P("dp"),
            P("dp", "narrow"),
            P("dp"),
            P("dp", "narrow"),
            P("dp"),
            P("dp"),
            P("dp"),
            P(("dp", "narrow"), None),
            P("dp"),
        ),
        out_specs=(
            P("dp", None),
            P("dp"),
            P(("dp", "narrow"), None),
            P("dp", "narrow"),
            P("dp"),
            P("dp", "narrow"),
            P("dp", "narrow"),
            P("dp"),
            P("dp", "narrow"),
            P("dp"),
            P("dp"),
            P("dp"),
            P("dp", "narrow"),
            P("dp"),
            P("dp", "narrow"),
            P("dp"),
            P("dp"),
            P("dp"),
        ),
        check_vma=False,
    )
```

time: 464 us -> 300 us (0.65); the launches traced: 456 us -> 297 us
  matrix products: 152 us -> 0 us
  Pallas kernels: 198 us -> 251 us
  local copies, waits for them, and re-layouts: 59.2 us -> 24.2 us
  other arithmetic: 23.9 us -> 0 us
    dot_general x24 -> x0, matrix products: 152 us -> none  [the longest x6 61.9 us: product(): return jnp.dot(left, right, preferred_element_type=jnp.float32)]
    pallas_call x2, Pallas kernels: 173 us -> 225 us  [the longest x1 113 us: backward_step(): pl.pallas_call(functools.partial(backward_kernel, direct), name='backward...]
    convert_element_type x2 -> x0, other arithmetic: 17.4 us -> none  [the longest x1 12.7 us: per_device(): d_scores = (probability * (d_probability - jnp.sum(probability * d_probab...]
    unnamed x135 -> x28, local copies, waits for them, and re-layouts: 25.7 us -> 15.4 us
    reshape x11 -> x1, local copies, waits for them, and re-layouts: 11.3 us -> 1.26 us  [per_device(): vecs = [vec[i, :BLOCK] for i in range(8)] + [vec[8:11].reshape(FF // dp)]]
    convert_element_type x5 -> x0, local copies, waits for them, and re-layouts: 8.08 us -> none  [the longest x1 2.78 us: per_device(): d_values = jnp.einsum('phlm,plhe->pmhe', prob_again, d_context, preferred...]
    reduce_sum x4 -> x0, other arithmetic: 5.38 us -> none  [the longest x1 3.24 us: per_device(): denominator = jnp.sum(shifted, axis=-1, keepdims=True)]
  transfers between devices with their start and end apart: 1 -> 1, of which waited for: 0 -> 0; matrix products, arithmetic and copies ran while one was open for 26% -> 2% of each run, Pallas kernels for 25% -> 47%
where the time goes in v2:
time: 300 us; the launch traced here: 297 us
  Pallas kernels  251 us (84%)
  local copies, waits for them, and re-layouts  24.2 us (8%)
  between operations  15.2 us (5%)
  blocking collectives  6.37 us (2%)
    pallas_call x1, Pallas kernels, backward_step(): pl.pallas_call(functools.partial(backward_kernel, direct), name='backward...  113 us
    pallas_call x1, Pallas kernels, forward_step(): pl.pallas_call(functools.partial(forward_kernel, direct), name='forward',...  112 us
    pallas_call x1, Pallas kernels, transport_step(): pl.pallas_call(transport_kernel, name='transport', out_shape=(jax.ShapeDt...  25.4 us
    unnamed x28, local copies, waits for them, and re-layouts  15.4 us
    all_gather x1, blocking collectives, per_device(): lax.all_gather(partial_value[:, 0], 'narrow', axis=0, tiled=True)  6.37 us
  transfers between devices with their start and end apart: 1, of which 0 were waited for; matrix products, arithmetic and copies ran while one was open for 2% of the time, Pallas kernels for 47%

profile of v2, /device:TPU:0, one launch (start us, length us, event | category | flops | bytes accessed | tf_op | source)
XLA Modules:
  0.0 296.7 jit_solution(16992019093173486481)
XLA Ops:
  7.2 0.0 all-gather.3.cloned.1.call-start
  7.2 1.7 copy.40.refs_5_
  9.0 0.7 pad_bitcast_fusion
  9.6 0.7 pad_bitcast_fusion.2
  10.3 0.7 pad_bitcast_fusion.4
  11.0 0.7 pad_bitcast_fusion.6
  11.7 1.9 concatenate.3.refs_6_
  13.5 112.3 %forward.1 = (bf16[3072,768]{1,0:T(8,128)(2,1)}, bf16[8,96,3072]{2,1,0:T(8,128)(2,1)}, bf16[3072,768]{1,0:T(8,128)(2,1)}, f32[16,896]{1,0:T(8,128)}, bf16[1024,2...) custom-call(bf16[96,192]{1,0:T(8,128)(2,1)} %refs_0_.1, ...), custom_call_target="tpu_custom_call" | custom-call | tf_op jit(solution)/shard_map/forward/pallas_call | solution.py:481
  125.9 0.0 all-gather.3.cloned.1.call-update
  125.9 1.3 slice.33.gain_ref
  127.2 25.4 %transport.1 = (f32[4,128]{1,0:T(4,128)}, f32[1024,768]{1,0:T(8,128)}, bf16[1024,768]{1,0:T(8,128)(2,1)}, f32[8,768]{1,0:T(8,128)}) custom-call(bf16[1024,768]{1,0:T(8,128)(2,1)} %get-tuple-element.44.mixed_ref, s32[16,256]{1,0:T(8,128)} %seg_ref.1, s32[16,256]{1,0:T(8,128)} %kind_ref.1, f32[16]{0:T(128)} %weight_ref.1, bf16[1024,768]{1,0:T(8,128)(2,1)} %cot_ref.1, ...), custom_call_target="tpu_custom_call" | custom-call | tf_op jit(solution)/shard_map/transport/pallas_call | solution.py:641
  152.6 0.0 copy-start.7
  152.6 0.0 copy-start.6
  152.6 113.1 %backward.1 = (f32[1024,768]{1,0:T(8,128)}, f32[96,192]{1,0:T(8,128)}, f32[96,192]{1,0:T(8,128)}, f32[96,192]{1,0:T(8,128)}, f32[96,192]{1,0:T(8,128)}, /*index=...) custom-call(bf16[3072,1024]{1,0:T(8,128)(2,1)} %get-tuple-element.49.refs_0_, ...), custom_call_target="tpu_custom_call" | custom-call | tf_op jit(solution)/shard_map/backward/pallas_call | solution.py:1060
  265.7 1.9 copy.41
  267.6 0.0 copy-done.7
  267.6 0.6 dynamic-slice
  268.8 0.0 copy-done.6
  268.8 0.1 slice_reduce_fusion
  268.9 0.2 dynamic-update-slice
  269.2 6.4 %all-reduce.8 = f32[16]{0:T(128)} all-reduce(f32[16]{0:T(128)S(1)} %dynamic-update-slice), channel_id=2, replica_groups=mesh['dp'=8,'narrow'=4] {'narrow'}, use_global_device_ids=true, to_apply=%add.8 | all-reduce | flops 16 | bytes 128 | tf_op jit(solution)/shard_map/all_gather | solution.py:1127
  275.5 1.3 slice_bitcast_fusion
  276.8 1.5 slice_bitcast_fusion.1
  278.3 0.0 all-gather.3.cloned.1.call-done
  278.3 0.0 copy-start
  278.3 6.0 %copy.50 = bf16[4096,768]{1,0:T(8,128)(2,1)} copy(bf16[4096,768]{1,0:T(8,128)(2,1)} %all-gather.3.cloned.1.call-done) | data formatting | bytes 12582912
  284.4 0.0 copy-done
  284.4 0.0 copy-start.5
  284.4 0.0 copy-start.4
  284.4 0.0 copy-start.3
  284.4 0.0 copy-start.2
  284.4 0.0 copy-start.1
  284.4 1.7 copy.51
  286.1 0.0 copy-done.5
  286.1 0.6 copy.52
  286.7 0.0 copy-done.4
  286.7 0.6 copy.53
  287.4 0.0 copy-done.3
  287.4 0.6 copy.54
  288.0 0.0 copy-done.2
  288.0 0.6 copy.55
  288.7 0.0 copy-done.1
  288.7 0.7 copy.56
  (2 shorter events, 0.0 us)
Async XLA Ops:
  7.2 271.1 %all-gather.3.cloned.1.call-start = ((), (), s32[]{:S(2)}) async-start(), calls=%async_computation | async-start | bytes 7864320 | tf_op jit(solution)/shard_map/all_gather | solution.py:1123
  152.6 115.0 %copy-start.7 = (u32[32]{0:T(128)S(1)}, u32[32]{0:T(128)}, u32[]{:S(2)}) copy-start(u32[32]{0:T(128)} %constant.22) | copy-start | bytes 388
  152.6 116.2 %copy-start.6 = (f32[4,128]{1,0:T(4,128)S(1)}, f32[4,128]{1,0:T(4,128)}, u32[]{:S(2)}) copy-start(f32[4,128]{1,0:T(4,128)} %get-tuple-element.48) | copy-start | bytes 6148
  278.3 6.1 %copy-start = (f32[1024,768]{1,0:T(8,128)S(1)}, f32[1024,768]{1,0:T(8,128)}, u32[]{:S(2)}) copy-start(f32[1024,768]{1,0:T(8,128)} %get-tuple-element.142) | copy-start | bytes 9437188
  284.4 1.7 copy-start.5
  284.4 2.3 copy-start.4
  284.4 3.0 %copy-start.3 = (f32[96,192]{1,0:T(8,128)S(1)}, f32[96,192]{1,0:T(8,128)}, u32[]{:S(2)}) copy-start(f32[96,192]{1,0:T(8,128)} %get-tuple-element.146) | copy-start | bytes 221188
  284.4 3.6 %copy-start.2 = (f32[96,192]{1,0:T(8,128)S(1)}, f32[96,192]{1,0:T(8,128)}, u32[]{:S(2)}) copy-start(f32[96,192]{1,0:T(8,128)} %get-tuple-element.148) | copy-start | bytes 221188
  284.4 4.3 %copy-start.1 = (f32[96,768]{1,0:T(8,128)S(1)}, f32[96,768]{1,0:T(8,128)}, u32[]{:S(2)}) copy-start(f32[96,768]{1,0:T(8,128)} %get-tuple-element.152) | copy-start | bytes 884740
Sparse Core Ops, SparseCore 0:
  126.0 50.5 all-gather.2

commit v3 on v2

v3 whole, which is shorter than its diff:
```python
import functools

import jax
import jax.numpy as jnp
from jax import lax
from jax.experimental import pallas as pl
from jax.experimental.pallas import tpu as pltpu
from jax.sharding import PartitionSpec as P

D = 768
HEADS = 12
HEAD_DIM = 64
LEN = 256
ITERS = 20
ROWS = 32
VMEM_LIMIT = 62 * 1024 * 1024

EPS_NORM = 1e-06
BETA = 0.5
MASKED = -1e30


def product(left, right):
    return jnp.dot(left, right, preferred_element_type=jnp.float32)


def product_left(left, right):
    return lax.dot_general(
        left, right, (((0,), (0,)), ((), ())), preferred_element_type=jnp.float32
    )


def product_right(left, right):
    return lax.dot_general(
        left, right, (((1,), (1,)), ((), ())), preferred_element_type=jnp.float32
    )


def fetch_weights(matrices, vectors):
    wide = [lax.all_gather(item, "narrow", axis=1, tiled=True) for item in matrices]
    query, keys, values, output, up, down = [lax.all_gather(item, "dp", axis=0, tiled=True) for item in wide]
    vecs = [lax.all_gather(item, "dp", axis=0, tiled=True).astype(jnp.float32) for item in vectors]
    up = up.reshape(GRID[0], BLOCK, GRID[1], 6, 128).transpose(0, 2, 3, 1, 4)
    up = up.reshape(GRID[0] // 2, 2, GRID[1] // 2, 2, 6 * BLOCK, 128)
    small = jnp.pad(jnp.stack(vecs[:8]), ((0, 8), (0, 128)))
    tiles = jnp.pad(vecs[8].reshape(24, 128), ((0, 8), (0, 0)))
    return (jnp.concatenate([query, keys, values, output], axis=1), up, down.T, small, tiles)


def reduce_grads(matrices, vectors):
    reduced = [lax.psum_scatter(item, "dp", scatter_dimension=0, tiled=True) for item in matrices]
    sums = [lax.psum_scatter(item, "dp", scatter_dimension=0, tiled=True) for item in vectors]
    return (
        [
            lax.psum_scatter(
                item.astype(jnp.bfloat16), "narrow", scatter_dimension=1, tiled=True
            ).astype(jnp.float32)
            for item in reduced
        ],
        lax.psum(sums, "narrow"),
    )


MESH = pl.DeviceIdType.MESH
FF = 4 * D
VEC, SQUARE, UP, DOWN, TOTAL = 0, 16, 592, 1168, 1744
PART = 144
CHUNK_ROWS = (80, 64) * 3 + (144,) * 9
CHUNKS = len(CHUNK_ROWS) + 1
SINGLES = (0, 1, 2, 3, 4, 5, CHUNKS - 1)
GRID = (8, 4)
BLOCK, SIDE = D // GRID[0], D // GRID[1]


def hops():
    dp, narrow = lax.axis_index("dp"), lax.axis_index("narrow")
    return (dp // 2, lax.rem(dp, 2), narrow // 2, lax.rem(narrow, 2))


def place(me, depth, item):
    s, a, b, c = item
    z, x, y, core = me
    z = z if s == 0 else lax.rem(z + s + depth, depth)
    x = 1 - x if a else x
    y = 1 - y if b else y
    core = 1 - core if c else core
    return (2 * z + x, 2 * y + core)


def greet(me, depth):
    peers = [place(me, depth, (s, 0, 0, 0)) for s in range(1, depth)]
    peers += [place(me, depth, (0, *bits)) for bits in ((1, 0, 0), (0, 1, 0), (0, 0, 1))]
    barrier = pltpu.get_barrier_semaphore()
    for peer in peers:
        pl.semaphore_signal(barrier, inc=1, device_id=peer, device_id_type=MESH)
    pl.semaphore_wait(barrier, len(peers))


def number(item):
    s, a, b, c = item
    return ((s * 2 + a) * 2 + b) * 2 + c


GATHER_AXES = (
    "zxy", "zxy", "zyx", "zyx", "zxy", "zxy", "zyx", "zxy", "zxy", "yxz", "zxy", "zyx", "zyx", "zxy", "yxz", "zxy",
)
FORWARD_ORDER = (
    "s1", "s15", "s5", "s2", "s14", "s3", "s4", "11", "115", "s9", "15", "s7", "s0", "12", "13", "14", "s6", "22",
    "s8", "25", "s12", "21", "215", "24", "114", "23", "17", "10", "31", "315", "s11", "19", "s10", "16", "s13", "20",
    "33", "27", "32", "18", "112", "c1", "c15", "34", "35", "30", "c3", "26", "c0", "111", "c2", "c4", "Q0", "29",
    "37", "28", "c5", "Q1", "Q2", "110", "36", "c7", "212", "A0", "214", "A1", "210", "113", "A2", "A3", "211", "c6",
    "39", "38", "O", "c8", "310", "213", "W0", "W1", "c10", "c9", "311", "312", "W2", "W3", "W4", "c11", "313", "W5",
    "c12", "c13", "314", "G", "c14", "F",
)


def split_order(order):
    after, mark = {"": []}, ""
    for word in order:
        if word[0] in "s123c":
            after[mark].append((word[0], int(word[1:])))
        else:
            mark = word
            after[mark] = []
    return after


def chunk_of(k, axes):
    if k == CHUNKS - 1:
        return (k, VEC, SQUARE - VEC, axes[k])
    return (k, SQUARE + sum(CHUNK_ROWS[:k]), CHUNK_ROWS[k], axes[k])


def arrivals(order, depth):
    have, stages = [(0, 0, 0)], []
    for axis in order:
        if axis == "z":
            new = [(far, a, b) for s, a, b in have for far in range(1, depth)]
        else:
            new = [(s, 1, b) if axis == "x" else (s, a, 1) for s, a, b in have]
        stages.append(new)
        have = have + new
    return stages


class Gather:
    def __init__(self, land, pad, send_sem, recv_sem):
        self.land, self.pad, self.send_sem, self.recv_sem = land, pad, send_sem, recv_sem
        self.me = hops()
        self.depth = land.shape[0]

    def block(self, chunk, z, x, y, core):
        return self.land.at[z, x, y, core, pl.ds(chunk[1], chunk[2]), :]

    def copy(self, chunk, block, hop, mark):
        return pltpu.make_async_remote_copy(
            src_ref=block,
            dst_ref=block,
            send_sem=self.send_sem.at[chunk[0]],
            recv_sem=self.recv_sem.at[chunk[0], mark],
            device_id=place(self.me, self.depth, hop),
            device_id_type=MESH,
        )

    def wait(self, chunk, block, mark):
        self.copy(chunk, block, (0, 0, 0, 1), mark).wait_recv()

    def single(self, chunk, item):
        s, a, b = item
        z, x, y, core = self.me
        source = lax.rem(z - s + self.depth, self.depth) if s else z
        return self.block(chunk, source, 1 - x if a else x, 1 - y if b else y, core)

    def send(self, chunk, item, axes):
        s, a, b = item
        block = self.single(chunk, item)
        for axis in axes:
            if axis == "z":
                for far in range(1, self.depth):
                    self.copy(chunk, block, (far, 0, 0, 0), number((far, a, b, 0))).start()
            elif axis == "x":
                self.copy(chunk, block, (0, 1, 0, 0), number((s, 1, b, 0))).start()
            elif axis == "y":
                self.copy(chunk, block, (0, 0, 1, 0), number((s, a, 1, 0))).start()
            else:
                self.copy(chunk, block, (0, 0, 0, 1), 1).start()

    def do(self, kind, k):
        chunk = chunk_of(k, GATHER_AXES)
        order = chunk[3]
        every = slice(None)
        z, x, y, core = self.me
        hop = {"x": (0, 1, 0, 0), "y": (0, 0, 1, 0), "c": (0, 0, 0, 1)}
        if kind == "c":
            self.wait(chunk, self.block(chunk, every, every, every, 1 - core), 1)
        elif k in SINGLES:
            if kind == "s":
                self.send(chunk, (0, 0, 0), order + "c")
            else:
                for item in arrivals(order, self.depth)[int(kind) - 1]:
                    self.wait(chunk, self.single(chunk, item), number((*item, 0)))
                    self.send(chunk, item, order[int(kind) :] + "c")
        elif order[0] == "z":
            column = self.block(chunk, every, x, y, core)
            if order[1] == "x":
                beside, behind = self.block(chunk, every, 1 - x, y, core), self.block(chunk, every, every, 1 - y, core)
            else:
                beside, behind = self.block(chunk, every, x, 1 - y, core), self.block(chunk, every, 1 - x, every, core)
            if kind == "s":
                for far in range(1, self.depth):
                    self.copy(chunk, self.single(chunk, (0, 0, 0)), (far, 0, 0, 0), 2 + far).start()
            elif kind == "1":
                for far in range(1, self.depth):
                    self.wait(chunk, self.single(chunk, (far, 0, 0)), 2 + far)
                for axis, mark in ((order[1], 6), (order[2], 7), ("c", 1)):
                    self.copy(chunk, column, hop[axis], mark).start()
            elif kind == "2":
                self.wait(chunk, beside, 6)
                for axis, mark in ((order[2], 7), ("c", 1)):
                    self.copy(chunk, beside, hop[axis], mark).start()
            else:
                self.wait(chunk, behind, 7)
                self.copy(chunk, behind, hop["c"], 1).start()
        else:
            own = self.single(chunk, (0, 0, 0))
            beside = self.single(chunk, (0, 1, 0) if order[0] == "x" else (0, 0, 1))
            behind = self.block(chunk, z, every, 1 - y, core) if order[0] == "x" else self.block(chunk, z, 1 - x, every, core)
            if kind == "s":
                for axis, mark in ((order[0], 6), (order[1], 7), ("c", 1)):
                    self.copy(chunk, own, hop[axis], mark).start()
            elif kind == "1":
                self.wait(chunk, beside, 6)
                for axis, mark in ((order[1], 7), ("c", 1)):
                    self.copy(chunk, beside, hop[axis], mark).start()
            elif kind == "2":
                self.wait(chunk, behind, 7)
                for far in range(1, self.depth):
                    self.copy(chunk, self.block(chunk, z, every, every, core), (far, 0, 0, 0), 2 + far).start()
                self.copy(chunk, behind, hop["c"], 1).start()
            else:
                for far in range(1, self.depth):
                    layer = self.block(chunk, lax.rem(z - far + self.depth, self.depth), every, every, core)
                    self.wait(chunk, layer, 2 + far)
                    self.copy(chunk, layer, hop["c"], 1).start()

    def drain(self, k):
        chunk = chunk_of(k, GATHER_AXES)
        size = self.pad.at[pl.ds(0, 16 * (8 * self.depth - 1)), pl.ds(0, 128 * chunk[2] // 16)]
        pltpu.make_async_remote_copy(
            src_ref=size,
            dst_ref=size,
            send_sem=self.send_sem.at[k],
            recv_sem=self.recv_sem.at[k, 0],
            device_id=place(self.me, self.depth, (0, 0, 0, 1)),
            device_id_type=MESH,
        ).wait_send()


def swap(half):
    return pltpu.roll(half, 64, 1)


def left_half(shape):
    return lax.broadcasted_iota(jnp.int32, shape, 1) < 64


def pack_block(wide, odd):
    rows = wide.shape[0]
    turned = pltpu.roll(wide, 192, 1)
    main = jnp.where(odd, turned[:, :128], wide[:, :128])
    rest = jnp.where(left_half((rows, 128)), jnp.where(odd, wide[:, :128], wide[:, 128:]), 0.0)
    top, low = rest[: rows // 2], rest[rows // 2 :]
    return main, jnp.where(odd, swap(top) + low, top + swap(low))


def middle_of(even, odd):
    left = left_half(even.shape)
    return jnp.where(left, even, odd), swap(jnp.where(left, odd, even))


def put_main(land, d, at, rows, ref, row, column):
    for pair in range(GRID[1] // 2):
        even, other = land.at[d // 2, d % 2, pair, 0], land.at[d // 2, d % 2, pair, 1]
        left = column + 384 * pair
        ref[pl.ds(row, rows), left : left + 128] = even[at : at + rows, :]
        ref[pl.ds(row, rows), left + 256 : left + 384] = other[at : at + rows, :]


def put_rest(land, d, at, rows, ref, row, column):
    half = rows // 2
    span = slice(at + rows, at + rows + half)
    for pair in range(GRID[1] // 2):
        even, other = land.at[d // 2, d % 2, pair, 0], land.at[d // 2, d % 2, pair, 1]
        top, low = middle_of(even[span, :].astype(jnp.float32), other[span, :].astype(jnp.float32))
        left = column + 384 * pair + 128
        ref[pl.ds(row, half), left : left + 128] = top.astype(jnp.bfloat16)
        ref[pl.ds(row + half, half), left : left + 128] = low.astype(jnp.bfloat16)


def norm_parts(values):
    centre = values - jnp.mean(values, axis=1, keepdims=True)
    spread = jnp.mean(centre * centre, axis=1, keepdims=True)
    recip = lax.rsqrt(spread + EPS_NORM)
    return centre * recip, recip


def gelu_parts(z):
    base = 1.0 + 0.2316419 * jnp.abs(z)
    t = pl.reciprocal(base, approx=True)
    t = t * (2.0 - base * t)
    density = jnp.exp2(z * z * (-0.5 * 1.4426950408889634))
    scale = 0.3989422804014327
    poly = 1.781477937 * scale + t * (-1.821255978 * scale + t * (1.330274429 * scale))
    tail = density * (t * (0.319381530 * scale + t * (-0.356563782 * scale + t * poly)))
    cdf = jnp.where(z < 0.0, tail, 1.0 - tail)
    return z * cdf, cdf + z * density * scale


def forward_kernel(direct, *refs):
    if direct:
        q_ref, k_ref, v_ref, o_ref, upw_ref, downw_ref = refs[:6]
        small_refs = refs[6:15]
        refs = refs[15:]
    else:
        square_in, up_in, down_in, vec_in, bup_in = refs[:5]
        refs = refs[5:]
    in_ref, seg_ref = refs[:2]
    (square_out, up_out, down_out, vec_ref, qkv_out, prob_out, turned_out, norm1_out, recip1_out,
     act_out, slope_out, mixed_out, norm2_out, recip2_out) = refs[2:16]
    (land, square, down, bup, qkv, qkv_turned, prob, turned, ctx, first, flow, norm, recip, act, slope, mixed,
     out_sem, pack_sem, tile_sem) = refs[16:35]
    packs = in_ref.shape[0] // LEN
    base = lax.axis_index("narrow") * packs
    pending = {}

    def save(name, src, dst):
        pending[name] = pltpu.make_async_copy(src, dst, out_sem.at[len(pending)])
        pending[name].start()

    if direct:
        send_sem, recv_sem = refs[35:37]
        dp, narrow = lax.axis_index("dp"), lax.axis_index("narrow")
        odd = lax.rem(narrow, 2) == 1
        own = land.at[dp // 2, lax.rem(dp, 2), narrow // 2, lax.rem(narrow, 2)]
        row = lambda ref: jnp.concatenate(
            [ref[...].astype(jnp.float32), jnp.zeros((1, 128 - BLOCK), jnp.float32)], axis=1
        )
        small = [row(ref) for ref in small_refs[:8]] + [small_refs[8][...].astype(jnp.float32)]
        own[0:16, :] = jnp.concatenate([*small, jnp.zeros((5, 128), jnp.float32)]).astype(jnp.bfloat16)
        for i, ref in enumerate((q_ref, k_ref, v_ref, o_ref)):
            main, rest = pack_block(
                jnp.concatenate([ref[...].astype(jnp.float32), jnp.zeros((BLOCK, 64), jnp.float32)], axis=1), odd
            )
            at = SQUARE + PART * i
            own[at : at + BLOCK, :] = main.astype(jnp.bfloat16)
            own[at + BLOCK : at + PART, :] = rest.astype(jnp.bfloat16)
        g = Gather(land, act, send_sem, recv_sem)
        greet(g.me, g.depth)
        after = split_order(FORWARD_ORDER)
        early = [piece for piece in after[""] if piece[1] < 7 or piece[1] == CHUNKS - 1]
        early = early[: next(i for i, piece in enumerate(early) if piece[0] != "s")]
        for piece in early:
            g.do(*piece)
        for t in range(6):
            own[UP + BLOCK * t : UP + BLOCK * (t + 1), :] = upw_ref[:, 128 * t : 128 * (t + 1)]
        for t in range(3):
            own[DOWN + SIDE * t : DOWN + SIDE * (t + 1), :] = downw_ref[:, 128 * t : 128 * (t + 1)]
        for piece in after[""]:
            if piece not in early:
                g.do(*piece)
        vec_ref[...] = jnp.zeros_like(vec_ref)
        for d in range(GRID[0]):
            tile = land[d // 2, d % 2, 0, 0, 0:16, :].astype(jnp.float32)
            wide = jnp.concatenate([tile, jnp.zeros((16, 128), jnp.float32)], axis=1)
            at, shift = divmod(BLOCK * d, 128)
            wide = pltpu.roll(wide, shift, 1) if shift else wide
            vec_ref[:, 128 * at : 128 * at + 256] += wide
            bup[3 * d : 3 * d + 3, :] = tile[8:11]

        def unpack(i):
            for d in range(GRID[0]):
                put_main(land, d, SQUARE + PART * i, BLOCK, square, BLOCK * d, D * i)
                put_rest(land, d, SQUARE + PART * i, BLOCK, square, BLOCK * d, D * i)

        def pieces_after(mark):
            for piece in after[mark]:
                g.do(*piece)

        def tick(mark, index):
            for name, pieces in after.items():
                if name[:1] == mark and pieces:

                    @pl.when(index == int(name[1:]))
                    def _():
                        for piece in pieces:
                            g.do(*piece)
    else:
        fills = [
            pltpu.make_async_copy(src, dst, out_sem.at[i])
            for i, (src, dst) in enumerate(
                ((square_in, square), (down_in, down), (up_in, land.at[:, :, :, :, pl.ds(UP, DOWN - UP), :]))
            )
        ]
        for copy in fills:
            copy.start()
        vec_ref[...] = vec_in[...]
        bup[...] = bup_in[...]
        for copy in fills:
            copy.wait()
        tick = lambda mark, index: None
        unpack = pieces_after = lambda mark: None

    for i in range(3):
        unpack(i)
        for j in range(3):
            columns = slice(256 * j, 256 * (j + 1))
            part = product(in_ref[...], square[:, D * i + 256 * j : D * i + 256 * (j + 1)])
            if i != 1:
                part = part + vec_ref[i // 2 : i // 2 + 1, columns]
            part = part.astype(jnp.bfloat16)
            qkv[:, D * i + 256 * j : D * i + 256 * (j + 1)] = part
            qkv_turned[D * i + 256 * j : D * i + 256 * (j + 1), :] = jnp.transpose(part)
        pieces_after(f"Q{i}")
    save("qkv", qkv_turned, qkv_out)

    def prob_copy(p):
        return pltpu.make_async_copy(prob.at[p % 2], prob_out.at[p], pack_sem.at[0, p % 2])

    def turned_copy(p):
        at = pl.ds(pl.multiple_of(p * LEN, LEN), LEN)
        return pltpu.make_async_copy(turned.at[p % 2], turned_out.at[:, :, at], pack_sem.at[1, p % 2])

    def attend(p, carry):
        rows = pl.ds(pl.multiple_of(p * LEN, LEN), LEN)
        k = p % 2

        pl.when(p >= 2)(lambda: prob_copy(p - 2).wait())
        seg_row = seg_ref[pl.ds(base + p, 1), :].astype(jnp.float32)
        seg_col = jnp.transpose(jnp.broadcast_to(seg_row, (128, LEN)))
        same = jnp.concatenate([seg_col, seg_col], axis=1) == seg_row
        left = left_half((LEN, 128))
        for h in range(HEADS // 2):
            columns = slice(128 * h, 128 * (h + 1))
            query = qkv[rows, columns] * jnp.asarray(HEAD_DIM**-0.5, jnp.bfloat16)
            keys = qkv[rows, D + 128 * h : D + 128 * (h + 1)]
            values = qkv[rows, 2 * D + 128 * h : 2 * D + 128 * (h + 1)]
            mixes = []
            for side in range(2):
                mine = left if side == 0 else jnp.logical_not(left)
                scores = product_right(jnp.where(mine, query, jnp.zeros_like(query)), keys)
                scores = jnp.where(same, scores, MASKED)
                shifted = jnp.exp(scores - jnp.max(scores, axis=1, keepdims=True))
                total = jnp.sum(shifted, axis=1, keepdims=True)
                low = (shifted * (1.0 / total)).astype(jnp.bfloat16)
                prob[k, 2 * h + side] = low
                mixes.append(product(low, values))
            ctx[rows, columns] = jnp.where(left, mixes[0], mixes[1]).astype(jnp.bfloat16)
        prob_copy(p).start()
        tick("A", p)
        return carry

    lax.fori_loop(0, packs, attend, 0)
    unpack(3)
    save("square", square, square_out)
    prob_copy(packs - 2).wait()
    prob_copy(packs - 1).wait()

    def project(p, carry):
        rows = pl.ds(pl.multiple_of(p * LEN, LEN), LEN)
        k = p % 2

        @pl.when(p >= 2)
        def _():
            turned_copy(p - 2).wait()

        x = in_ref[rows, :]
        context = ctx[rows, :]
        total = x.astype(jnp.float32) + (product(context, square[:, 3 * D :]) + vec_ref[2:3, :D])
        normed, scale = norm_parts(total)
        value = normed * vec_ref[3:4, :D] + vec_ref[4:5, :D]
        first[rows, :] = value
        low = value.astype(jnp.bfloat16)
        flow[rows, :] = low
        norm[rows, :] = normed
        recip[rows, :] = jnp.broadcast_to(scale, (LEN, 128))
        turned[k, 0] = jnp.transpose(x)
        turned[k, 1] = jnp.transpose(context)
        turned[k, 2] = jnp.transpose(low)
        turned_copy(p).start()
        return carry

    lax.fori_loop(0, packs, project, 0)
    pieces_after("O")
    save("norm", norm, norm1_out)
    save("recip", recip, recip1_out)
    turned_copy(packs - 2).wait()
    turned_copy(packs - 1).wait()

    def tile_copies(t):
        k = t % 2
        copies = []
        for n in range(GRID[1]):
            columns = pl.ds(pl.multiple_of(D * n + 128 * t, 128), 128)
            first_row = pl.multiple_of(UP + BLOCK * t, 16)
            copies += [
                pltpu.make_async_copy(slope.at[k, n], slope_out.at[:, columns], tile_sem.at[0, k, n]),
                pltpu.make_async_copy(act.at[:, columns], act_out.at[:, columns], tile_sem.at[1, k, n]),
                pltpu.make_async_copy(
                    land.at[:, :, n // 2, n % 2, pl.ds(first_row, BLOCK), :], up_out.at[:, :, :, columns], tile_sem.at[2, k, n]
                ),
            ]
        return copies

    def widen(t, carry):
        k = t % 2

        @pl.when(t >= 2)
        def _():
            for copy in tile_copies(t - 2):
                copy.wait()

        first_row = pl.multiple_of(UP + BLOCK * t, 16)
        for pair in range(2):
            weight = jnp.concatenate(
                [land[:, :, pair, i, pl.ds(first_row, BLOCK), :].reshape(D, 128) for i in range(2)], axis=1
            )
            bias = jnp.concatenate([bup[pl.ds(6 * (2 * pair + i) + t, 1), :] for i in range(2)], axis=1)
            for r in range(packs):
                rows = slice(LEN * r, LEN * (r + 1))
                value, turn = gelu_parts(product(flow[rows, :], weight) + bias)
                value, turn = value.astype(jnp.bfloat16), turn.astype(jnp.bfloat16)
                for i in range(2):
                    n = 2 * pair + i
                    columns = pl.ds(pl.multiple_of(D * n + 128 * t, 128), 128)
                    act[rows, columns] = value[:, 128 * i : 128 * (i + 1)]
                    slope[k, n, rows, :] = turn[:, 128 * i : 128 * (i + 1)]
        for copy in tile_copies(t):
            copy.start()
        tick("W", t)
        return carry

    lax.fori_loop(0, 6, widen, 0)
    def down_part(*tiles):
        if direct:
            for d in range(GRID[0]):
                for n in range(GRID[1]):
                    for t in tiles:
                        at = 384 * d + 128 * t
                        down[SIDE * n : SIDE * (n + 1), at : at + 128] = land[
                            d // 2, d % 2, n // 2, n % 2, DOWN + SIDE * t : DOWN + SIDE * (t + 1), :
                        ]
        spans = [slice(384 * d + 128 * t, 384 * d + 128 * (t + 1)) for d in range(GRID[0]) for t in tiles]
        for j in range(3):
            columns = slice(256 * j, 256 * (j + 1))
            weight = jnp.concatenate([down[columns, span] for span in spans], axis=1)
            for r in range(packs):
                rows = slice(LEN * r, LEN * (r + 1))
                hidden = jnp.concatenate([act[rows, span] for span in spans], axis=1)
                first[rows, columns] = first[rows, columns] + product_right(hidden, weight)

    down_part(0, 1)
    pieces_after("G")
    down_part(2)
    save("down", down, down_out)
    pending["norm"].wait()
    pending["recip"].wait()

    def finish(p, carry):
        rows = pl.ds(pl.multiple_of(p * LEN, LEN), LEN)
        normed, scale = norm_parts(first[rows, :] + vec_ref[5:6, :D])
        norm[rows, :] = normed
        recip[rows, :] = jnp.broadcast_to(scale, (LEN, 128))
        mixed[rows, :] = (normed * vec_ref[6:7, :D] + vec_ref[7:8, :D]).astype(jnp.bfloat16)
        return carry

    lax.fori_loop(0, packs, finish, 0)
    save("mixed", mixed, mixed_out)
    save("norm2", norm, norm2_out)
    save("recip2", recip, recip2_out)
    for t in (4, 5):
        for copy in tile_copies(t):
            copy.wait()
    if direct:
        for k in range(CHUNKS):
            g.drain(k)
    for name, copy in pending.items():
        if name not in ("norm", "recip"):
            copy.wait()


def forward_step(direct, weights, inputs, segments, dp, narrow):
    rows = inputs.shape[0]
    packs = rows // LEN
    vmem = pl.BlockSpec(memory_space=pltpu.VMEM)
    anywhere = pl.BlockSpec(memory_space=pl.ANY)
    low = lambda *shape: jax.ShapeDtypeStruct(shape, jnp.bfloat16)
    full = lambda *shape: jax.ShapeDtypeStruct(shape, jnp.float32)
    room = lambda *shape: pltpu.VMEM(shape, jnp.bfloat16)
    wide = lambda *shape: pltpu.VMEM(shape, jnp.float32)
    sems = [pltpu.SemaphoreType.DMA((CHUNKS,)), pltpu.SemaphoreType.DMA((CHUNKS, 32))] if direct else []
    return pl.pallas_call(
        functools.partial(forward_kernel, direct),
        name="forward",
        out_shape=(
            low(D, FF), low(GRID[0] // 2, 2, BLOCK, FF), low(D, FF), full(16, 896),
            low(3 * D, rows), low(packs, HEADS, LEN, LEN), low(3, D, rows), full(rows, D), full(rows, 128),
            low(rows, FF), low(rows, FF), low(rows, D), full(rows, D), full(rows, 128),
        ),
        in_specs=([vmem] * 15 if direct else [anywhere] * 3 + [vmem] * 2) + [vmem] * 2,
        out_specs=(anywhere,) * 3 + (vmem,) + (anywhere,) * 10,
        scratch_shapes=[
            room(GRID[0] // 2, 2, GRID[1] // 2, 2, TOTAL, 128), room(D, FF), room(D, FF), wide(32, 128),
            room(rows, 3 * D), room(3 * D, rows), room(2, HEADS, LEN, LEN), room(2, 3, D, LEN), room(rows, D), wide(rows, D), room(rows, D),
            wide(rows, D), wide(rows, 128), room(rows, FF), room(2, 4, rows, 128), room(rows, D),
            pltpu.SemaphoreType.DMA((12,)), pltpu.SemaphoreType.DMA((2, 2)), pltpu.SemaphoreType.DMA((3, 2, 4)),
            *sems,
        ],
        compiler_params=pltpu.CompilerParams(
            vmem_limit_bytes=VMEM_LIMIT, **(dict(collective_id=0, has_side_effects=True) if direct else {})
        ),
    )(*weights, inputs, segments)


def transport_kernel(
    mixed_ref, seg_ref, kind_ref, weight_ref, cot_in, normed_in, recip_in, gain_ref,
    value_ref, second_out, branch_out, turned_out, sums_ref,
    kern_ref, prod_ref, flow_ref, acc_ref, left_ref, sigma_ref,
    cot_ref, normed_ref, recip_ref, second_ref, branch_ref, turned_ref, load_sem, save_sem,
):
    loads = [
        pltpu.make_async_copy(src, dst, load_sem.at[i])
        for i, (src, dst) in enumerate(((cot_in, cot_ref), (normed_in, normed_ref), (recip_in, recip_ref)))
    ]
    for copy in loads:
        copy.start()
    packs = mixed_ref.shape[0] // LEN
    base = lax.axis_index("narrow") * packs
    blocks = LEN // ROWS
    lanes = lambda col: jnp.concatenate([col, col], axis=1)
    fold = lambda wide: wide[:, :128] + wide[:, 128:]
    eight = lambda wide: jnp.sum(wide.reshape(ROWS // 8, 8, LEN), axis=0)
    replicate = lambda col: jnp.broadcast_to(col, (ROWS, 128))

    def turned(row):
        return jnp.transpose(jnp.broadcast_to(row, (128, LEN)))

    for p in range(packs):
        rows = pl.ds(p * LEN, LEN)
        feats = mixed_ref[rows, :].astype(jnp.float32)
        recip = lax.rsqrt(jnp.sum(feats * feats, axis=1, keepdims=True) + EPS_NORM)
        unit = (feats * recip).astype(jnp.bfloat16)
        cosine = product_right(unit, unit)
        seg_row = seg_ref[pl.ds(base + p, 1), :].astype(jnp.float32)
        region_row = jnp.where(kind_ref[pl.ds(base + p, 1), :] == 0, 0.0, 1.0)
        seg_col = turned(seg_row)
        word_col = 1.0 - turned(region_row)
        same = jnp.where(lanes(seg_col) == seg_row, 1.0, 0.0)
        word_count = jnp.sum(same * (1.0 - region_row), axis=1, keepdims=True)
        region_count = jnp.sum(same * lanes(1.0 - word_col), axis=0, keepdims=True)
        kern_ref[p] = jnp.exp((cosine - 1.0) * (1.0 / BETA)) * same * lanes(word_col) * region_row
        left_ref[p, 0] = word_col
        left_ref[p, 1] = jnp.broadcast_to(word_count, (LEN, 128))
        left_ref[p, 2] = 1.0 - word_col
        prod_ref[0, p] = jnp.ones((LEN, LEN), jnp.float32)
        sigma_ref[0, p, 0:1] = region_row / region_count
        sigma_ref[0, p, 1:2] = region_row
        sigma_ref[0, p, 2:3] = region_count

    def advance(t, carry):
        for p in range(packs):
            sigma = sigma_ref[t, p, 0:1]
            scale = jnp.where(t == 0, 1.0, sigma)
            region = sigma_ref[0, p, 1:2]
            count = sigma_ref[0, p, 2:3]
            total = jnp.zeros((8, LEN), jnp.float32)
            for b in range(blocks):
                rows = pl.ds(b * ROWS, ROWS)
                weighted = kern_ref[p, rows, :] * (prod_ref[t, p, rows, :] * scale)
                row_sum = jnp.sum(fold(weighted * sigma), axis=1, keepdims=True)
                word = left_ref[p, 0, rows, :]
                base = left_ref[p, 1, rows, :] * replicate(row_sum) + left_ref[p, 2, rows, :]
                delta = pl.reciprocal(base, approx=True)
                delta = word * delta * (2.0 - base * delta)
                scaled = weighted * lanes(delta)
                prod_ref[t + 1, p, rows, :] = scaled
                total = total + eight(scaled)
            col_sum = jnp.sum(total, axis=0, keepdims=True)
            sigma_ref[t + 1, p, 0:1] = region / (count * col_sum + 1.0 - region)
        return carry

    lax.fori_loop(0, ITERS, advance, 0)

    starts = []
    for p in range(packs):
        rows = pl.ds(p * LEN, LEN)
        weight = weight_ref[base + p]
        feats = mixed_ref[rows, :].astype(jnp.float32)
        recip = lax.rsqrt(jnp.sum(feats * feats, axis=1, keepdims=True) + EPS_NORM)
        unit = (feats * recip).astype(jnp.bfloat16)
        cosine = product_right(unit, unit)
        moved = (prod_ref[ITERS, p] * sigma_ref[ITERS, p, 0:1]) * (1.0 - cosine)
        value_ref[p : p + 1, :] = jnp.broadcast_to(jnp.sum(moved), (1, 128))
        moved = moved * weight
        flow_ref[p] = moved
        acc_ref[p] = jnp.zeros((LEN, LEN), jnp.float32)
        starts += [jnp.sum(moved, axis=0, keepdims=True), jnp.zeros((1, LEN), jnp.float32)]

    def retreat(step, carry):
        t = ITERS - 1 - step
        out = []
        for p in range(packs):
            flow_sum, spread = carry[2 * p : 2 * p + 2]
            before = sigma_ref[t, p, 0:1]
            d_col = -sigma_ref[0, p, 2:3] * sigma_ref[t + 1, p, 0:1] * (spread + flow_sum)
            total = jnp.zeros((8, LEN), jnp.float32)
            shift = jnp.zeros((8, LEN), jnp.float32)
            for b in range(blocks):
                rows = pl.ds(b * ROWS, ROWS)
                scaled = prod_ref[t + 1, p, rows, :]
                flow = flow_ref[p, rows, :] + scaled * d_col
                d_row = replicate(jnp.sum(fold(flow), axis=1, keepdims=True))
                d_row = -left_ref[p, 1, rows, :] * d_row
                moved = scaled * lanes(d_row)
                flow = flow + moved * before
                flow_ref[p, rows, :] = flow
                acc_ref[p, rows, :] = acc_ref[p, rows, :] + flow
                total = total + eight(flow)
                shift = shift + eight(moved)
            out += [
                jnp.sum(total, axis=0, keepdims=True),
                before * jnp.sum(shift, axis=0, keepdims=True),
            ]
        return tuple(out)

    lax.fori_loop(0, ITERS, retreat, tuple(starts))

    for copy in loads:
        copy.wait()
    saves = []
    sums = [jnp.zeros((1, D), jnp.float32)] * 3
    for p in range(packs):
        rows = pl.ds(p * LEN, LEN)
        coupling = prod_ref[ITERS, p] * sigma_ref[ITERS, p, 0:1]
        d_cost = weight_ref[base + p] * coupling - acc_ref[p] * (1.0 / BETA)
        d_cosine = (-d_cost).astype(jnp.bfloat16)
        feats = mixed_ref[rows, :].astype(jnp.float32)
        recip = lax.rsqrt(jnp.sum(feats * feats, axis=1, keepdims=True) + EPS_NORM)
        unit = feats * recip
        unit_low = unit.astype(jnp.bfloat16)
        d_unit = product(d_cosine, unit_low) + product_left(d_cosine, unit_low)
        d_mixed = cot_ref[rows, :].astype(jnp.float32) + recip * (
            d_unit - unit * jnp.sum(d_unit * unit, axis=1, keepdims=True)
        )
        normed = normed_ref[rows, :]
        scaled = d_mixed * gain_ref[6:7, :D]
        inner_mean = jnp.mean(scaled, axis=1, keepdims=True)
        cross_mean = jnp.mean(scaled * normed, axis=1, keepdims=True)
        d_second = recip_ref[rows, 0:1] * (scaled - inner_mean - normed * cross_mean)
        d_branch = d_second.astype(jnp.bfloat16)
        second_ref[rows, :] = d_second
        branch_ref[rows, :] = d_branch
        turned_ref[:, rows] = jnp.transpose(d_branch)
        for src, dst in (
            (second_ref.at[rows, :], second_out.at[rows, :]),
            (branch_ref.at[rows, :], branch_out.at[rows, :]),
            (turned_ref.at[:, rows], turned_out.at[:, rows]),
        ):
            copy = pltpu.make_async_copy(src, dst, save_sem.at[len(saves)])
            copy.start()
            saves.append(copy)
        sums[0] = sums[0] + jnp.sum(d_mixed * normed, axis=0, keepdims=True)
        sums[1] = sums[1] + jnp.sum(d_mixed, axis=0, keepdims=True)
        sums[2] = sums[2] + jnp.sum(d_branch.astype(jnp.float32), axis=0, keepdims=True)
    for k in range(3):
        sums_ref[k : k + 1, :] = sums[k]
    for copy in saves:
        copy.wait()


def transport_step(mixed, segments, row_kind, weight, cotangent, normed, recip, gain):
    rows = mixed.shape[0]
    packs = rows // LEN
    vmem = pl.BlockSpec(memory_space=pltpu.VMEM)
    anywhere = pl.BlockSpec(memory_space=pl.ANY)
    square = (packs, LEN, LEN)
    return pl.pallas_call(
        transport_kernel,
        name="transport",
        out_shape=(
            jax.ShapeDtypeStruct((packs, 128), jnp.float32),
            jax.ShapeDtypeStruct((rows, D), jnp.float32),
            jax.ShapeDtypeStruct((rows, D), jnp.bfloat16),
            jax.ShapeDtypeStruct((D, rows), jnp.bfloat16),
            jax.ShapeDtypeStruct((8, D), jnp.float32),
        ),
        in_specs=[vmem, vmem, vmem, pl.BlockSpec(memory_space=pltpu.SMEM), anywhere, anywhere, anywhere, vmem],
        out_specs=(vmem, anywhere, anywhere, anywhere, vmem),
        scratch_shapes=[
            pltpu.VMEM(square, jnp.float32),
            pltpu.VMEM((ITERS + 1, *square), jnp.float32),
            pltpu.VMEM(square, jnp.float32),
            pltpu.VMEM(square, jnp.float32),
            pltpu.VMEM((packs, 3, LEN, 128), jnp.float32),
            pltpu.VMEM((ITERS + 1, packs, 8, LEN), jnp.float32),
            pltpu.VMEM((rows, D), jnp.bfloat16),
            pltpu.VMEM((rows, D), jnp.float32),
            pltpu.VMEM((rows, 128), jnp.float32),
            pltpu.VMEM((rows, D), jnp.float32),
            pltpu.VMEM((rows, D), jnp.bfloat16),
            pltpu.VMEM((D, rows), jnp.bfloat16),
            pltpu.SemaphoreType.DMA((3,)),
            pltpu.SemaphoreType.DMA((3 * packs,)),
        ],
        compiler_params=pltpu.CompilerParams(vmem_limit_bytes=VMEM_LIMIT),
    )(mixed, segments, row_kind, weight, cotangent, normed, recip, gain)


REST, OUT, MAIN = 16, 160, 304
SCATTER_ROWS = (80, 80, 80, 64, 80, 64, 80, 64) + (144,) * 4 + (96,) * 6
SCATTER_AXES = (
    "zyx", "yxz", "xyz", "xyz", "yxz", "xyz", "xyz", "xyz", "zxy", "xyz", "yxz", "xyz", "xyz", "yxz", "yxz", "zyx",
    "xyz", "yxz",
)
BACKWARD_ORDER = (
    "D0", "s12", "s13", "D1", "s14", "s15", "D2", "s16", "s17", "c12", "c13", "N0", "c14", "N1", "c15", "c16", "N2",
    "c17", "N3", "U0", "U1", "s8", "U2", "s9", "312", "313", "U3", "U4", "s10", "c8", "c9", "U5", "s11", "316", "314",
    "B0", "c10", "213", "c11", "B1", "315", "B2", "317", "B3", "212", "O", "s2", "s3", "39", "216", "T0", "c2", "214",
    "T1", "c3", "T2", "T3", "38", "310", "215", "T4", "311", "113", "T5", "29", "217", "T6", "112", "T7", "32", "116",
    "M", "s4", "s5", "s6", "s7", "211", "114", "X0", "c4", "33", "X1", "c5", "c6", "c7", "22", "28", "19", "X2",
    "210", "117", "X3", "115", "R", "s0", "s1", "34", "35", "23", "12", "111", "W0", "c0", "c1", "18", "W1", "36",
    "110", "W2", "25", "13", "37", "W3", "24", "31", "26", "27", "30", "21", "15", "14", "20", "16", "17", "10", "11",
)


class Scatter:
    def __init__(self, part, lands, send_sem, recv_sem, total):
        self.part, self.lands, self.send_sem, self.recv_sem, self.total = part, lands, send_sem, recv_sem, total
        self.me = hops()
        self.depth = part.shape[0]

    def copies(self, k):
        first, order = sum(SCATTER_ROWS[:k]), SCATTER_AXES[k]
        span = pl.ds(first, SCATTER_ROWS[k])
        every = slice(None)
        z, x, y, core = self.me
        part = lambda *at: self.part.at[*at, span, :]
        land_c, land_q, land_p, land_z = self.lands
        land = lambda ref, *at: ref.at[*at, span, :]
        to_x, to_y = (0, 1, 0, 0), (0, 0, 1, 0)
        stages = {"c": [], "3": [], "2": [], "1": []}
        ahead = lambda far: lax.rem(z + far, self.depth)
        if order[0] == "y":
            stages["c"] = [
                (part(every, every, 1 - y, 1 - core), land(land_c, every, every, 1 - y), None, part(every, every, 1 - y, core)),
                (part(every, every, y, 1 - core), land(land_c, every, every, y), None, part(every, every, y, core)),
            ]
        elif order[0] == "x":
            stages["c"] = [
                (part(every, 1 - x, every, 1 - core), land(land_c, every, 1 - x, every), None, part(every, 1 - x, every, core)),
                (part(every, x, every, 1 - core), land(land_c, every, x, every), None, part(every, x, every, core)),
            ]
        else:
            stages["c"] = [(part(every, every, every, 1 - core), land(land_c, every, every, every), None, part(every, every, every, core))]
        if order == "yxz":
            stages["3"] = [(part(every, every, 1 - y, core), land(land_q, every, every), to_y, part(every, every, y, core))]
            stages["2"] = [(part(every, 1 - x, y, core), land(land_p, every), to_x, part(every, x, y, core))]
        elif order == "xyz":
            stages["3"] = [(part(every, 1 - x, every, core), land(land_q, every, every), to_x, part(every, x, every, core))]
            stages["2"] = [(part(every, x, 1 - y, core), land(land_p, every), to_y, part(every, x, y, core))]
        else:
            for far in range(1, self.depth):
                for i in range(2):
                    slot = 2 * (far - 1) + i
                    where = land(land_q, slot, every) if slot < 4 else land(land_p, slice(2 * slot - 8, 2 * slot - 6))
                    stages["3"].append((part(ahead(far), i, every, core), where, (far, 0, 0, 0), part(z, i, every, core)))
            pair, last = land(land_z, slice(0, 2)), land(land_z, 2)
            if order[1] == "y":
                stages["2"] = [(part(z, every, 1 - y, core), pair, to_y, part(z, every, y, core))]
                stages["1"] = [(part(z, 1 - x, y, core), last, to_x, part(z, x, y, core))]
            else:
                stages["2"] = [(part(z, 1 - x, every, core), pair, to_x, part(z, x, every, core))]
                stages["1"] = [(part(z, x, 1 - y, core), last, to_y, part(z, x, y, core))]
        if order[2] == "z":
            stages["1"] = [
                (part(ahead(far), x, y, core), land(land_z, far - 1), (far, 0, 0, 0), part(z, x, y, core))
                for far in range(1, self.depth)
            ]
        made, mark = {}, 0
        for stage, items in stages.items():
            made[stage] = []
            for src, dst, hop, into in items:
                if stage != "c":
                    copy = functools.partial(self.copy, k, mark, src, dst, hop)
                    made[stage].append((copy, dst, into))
                    mark += 1
                else:
                    made[stage].append((None, dst, into))
        whole = functools.partial(
            self.copy, k, mark, part(every, every, every, 1 - core), land(land_c, every, every, every), (0, 0, 0, 1)
        )
        return whole, made

    def copy(self, k, mark, src, dst, hop):
        return pltpu.make_async_remote_copy(
            src_ref=src,
            dst_ref=dst,
            send_sem=self.send_sem.at[k, mark],
            recv_sem=self.recv_sem.at[k, mark],
            device_id=place(self.me, self.depth, hop),
            device_id_type=MESH,
        )

    def do(self, kind, k):
        whole, made = self.copies(k)
        if kind == "s":
            whole().start()
            return
        if kind == "c":
            whole().wait_recv()
        following = {"c": "3", "3": "2", "2": "1"}.get(kind)
        first, rows = sum(SCATTER_ROWS[:k]), SCATTER_ROWS[k]
        for i, (copy, land, into) in enumerate(made[kind]):
            if kind != "c":
                copy().wait_recv()
            if kind != "1":
                into[...] = into[...] + land[...]
            if kind == "c" and i == 0 and len(made["c"]) == 2:
                made["3"][0][0]().start()
        if kind == "1":
            value = made["1"][0][2][...].astype(jnp.float32)
            for copy, land, into in made["1"]:
                value = value + land[...].astype(jnp.float32)
            self.total[pl.ds(first, rows), :] = value
        elif not (kind == "c" and len(made["c"]) == 2):
            for copy, land, into in made[following]:
                copy().start()

    def drain(self, k):
        whole, made = self.copies(k)
        whole().wait_send()
        for stage in "321":
            for copy, land, into in made[stage]:
                copy().wait_send()


def fold_middle(top, low):
    left = left_half(top.shape)
    return jnp.where(left, top, swap(low)), jnp.where(left, swap(low), top)


def take_main(part, d, pair, at, even, other):
    rows = even.shape[0]
    part[d // 2, d % 2, pair, 0, at : at + rows, :] = even.astype(jnp.bfloat16)
    part[d // 2, d % 2, pair, 1, at : at + rows, :] = other.astype(jnp.bfloat16)


def take_rest(part, d, pair, at, block):
    half = block.shape[0] // 2
    one, two = fold_middle(block[:half], block[half:])
    take_main(part, d, pair, at, one, two)


def unpack_block(main, rest, odd):
    other = swap(rest)
    top, low = jnp.where(odd, other, rest), jnp.where(odd, rest, other)
    piece = jnp.concatenate([top, low], axis=0)
    left = left_half(piece.shape)
    swapped = swap(main)
    first = jnp.where(odd, jnp.where(left, piece, swapped), main)
    second = jnp.where(odd, swapped, piece)
    return jnp.concatenate([first, second], axis=1)


def backward_kernel(direct, *refs):
    (act_in, slope_in, branch_in, branch_turned_in, second_in, sums_in, turned_in, norm_in, recip_in, qkv_in, prob_in,
     square_in, up_in, down_in, vec_ref, value_ref) = refs[:16]
    refs = refs[16:]
    if direct:
        grad_in_out, total = refs[:2]
        refs = refs[2:]
    else:
        grad_in_out, gsquare_ref, gup_ref, gdown_ref, gvec_ref, gbup_ref = refs[:6]
        refs = refs[6:]
    (turned, slope, square, up, flow, norm, recip, branch, branch_turned, prob, sums, bup, load_sem, prob_sem,
     out_sem) = refs[:15]
    rows_all = slope.shape[0]
    packs = rows_all // LEN
    if direct:
        part, land_c, land_q, land_p, land_z, send_sem, recv_sem = refs[15:22]
        g = Scatter(part, (land_c, land_q, land_p, land_z), send_sem, recv_sem, total)
        dp, narrow = lax.axis_index("dp"), lax.axis_index("narrow")
    else:
        (stage,) = refs[15:16]

    loads, waited = {}, set()

    def load(name, *pairs):
        loads[name] = []
        for src, dst in pairs:
            copy = pltpu.make_async_copy(src, dst, load_sem.at[sum(map(len, loads.values()))])
            copy.start()
            loads[name].append(copy)

    def need(*names):
        for name in names:
            if name not in waited:
                waited.add(name)
                for copy in loads[name]:
                    copy.wait()

    blocks = [pl.ds(rows_all * i, rows_all) for i in range(3)]
    load("turned branch", (branch_turned_in, branch_turned))
    load("act", *[(act_in.at[:, span], turned.at[span, :]) for span in blocks])
    if direct:
        greet(g.me, g.depth)
    sums[...] = jnp.zeros_like(sums)
    bup[...] = jnp.zeros_like(bup)
    sums[5:6, :D] = sums_in[2:3, :]
    sums[6:7, :D] = sums_in[0:1, :]
    sums[7:8, :D] = sums_in[1:2, :]

    def put(src, dst):
        copy = pltpu.make_async_copy(src, dst, out_sem.at[0])
        copy.start()
        copy.wait()

    def put_down(t):
        at = pl.ds(pl.multiple_of(DOWN + SIDE * t, 16), SIDE)

        def two(i, carry):
            tiles = []
            for j in range(2):
                tile = 3 * (2 * i + j) + t
                rows = pl.ds(pl.multiple_of(tile // 8 * rows_all, 128), rows_all)
                tiles.append(turned[rows, pl.ds(pl.multiple_of(tile % 8 * 128, 128), 128)])
            grad = product(branch_turned[...], jnp.concatenate(tiles, axis=1))
            for j in range(2):
                block = grad[:, 128 * j : 128 * (j + 1)]
                if direct:
                    for n in range(GRID[1]):
                        part[i, j, n // 2, n % 2, at, :] = block[SIDE * n : SIDE * (n + 1)].astype(jnp.bfloat16)
                else:
                    stage[:, :128] = block
                    columns = pl.ds(pl.multiple_of(384 * (2 * i + j) + 128 * t, 128), 128)
                    put(stage.at[:, pl.ds(0, 128)], gdown_ref.at[:, columns])
            return carry

        lax.fori_loop(0, 4, two, 0)

    def narrow_down(c):
        at = pl.multiple_of(256 * c, 128)
        columns = pl.ds(at, 256)
        weight = square[:, columns]
        column_sum = jnp.zeros((1, 256), jnp.float32)
        for r in range(packs):
            rows = slice(LEN * r, LEN * (r + 1))
            value = product(branch[rows, :], weight) * slope[rows, columns].astype(jnp.float32)
            low = value.astype(jnp.bfloat16)
            slope[rows, columns] = low
            column_sum = column_sum + jnp.sum(low.astype(jnp.float32), axis=0, keepdims=True)
        bup[pl.ds(2 * c, 1), :] = column_sum[:, :128]
        bup[pl.ds(2 * c + 1, 1), :] = column_sum[:, 128:]

    def put_up(t, pair):
        first_row = pl.multiple_of(UP + BLOCK * t, 16)
        at = [pl.multiple_of(D * (2 * pair + j) + 128 * t, 128) for j in range(2)]
        columns = jnp.concatenate([slope[:, pl.ds(at[j], 128)] for j in range(2)], axis=1)
        grad = product(turned[2 * D : 3 * D, :], columns)
        for j in range(2):
            block = grad[:, 128 * j : 128 * (j + 1)]
            if direct:
                part[:, :, pair, j, pl.ds(first_row, BLOCK), :] = block.astype(jnp.bfloat16).reshape(
                    GRID[0] // 2, 2, BLOCK, 128
                )
            else:
                stage[:, :128] = block
                put(stage.at[:, pl.ds(0, 128)], gup_ref.at[:, pl.ds(at[j], 128)])

    def norm_back(r):
        rows = pl.ds(pl.multiple_of(r * LEN, LEN), LEN)
        d_first = flow[rows, :]
        for i in range(3):
            d_first = d_first + product_right(slope[rows, rows_all * i : rows_all * (i + 1)], up[D * i : D * (i + 1), :])
        normed = norm[rows, :]
        scaled = d_first * vec_ref[3:4, :D]
        inner_mean = jnp.mean(scaled, axis=1, keepdims=True)
        cross_mean = jnp.mean(scaled * normed, axis=1, keepdims=True)
        d_sum = recip[rows, 0:1] * (scaled - inner_mean - normed * cross_mean)
        flow[rows, :] = d_sum
        low = d_sum.astype(jnp.bfloat16)
        branch[rows, :] = low
        sums[3:4, :D] += jnp.sum(d_first * normed, axis=0, keepdims=True)
        sums[4:5, :D] += jnp.sum(d_first, axis=0, keepdims=True)
        sums[2:3, :D] += jnp.sum(low.astype(jnp.float32), axis=0, keepdims=True)

    def put_out():
        for pair in range(2):
            grad = product(turned[D : 2 * D, :], branch[:, 384 * pair : 384 * (pair + 1)])
            if direct:
                for d in range(GRID[0]):
                    block = grad[BLOCK * d : BLOCK * (d + 1)]
                    take_main(part, d, pair, OUT, block[:, :128], block[:, 256:])
                    take_rest(part, d, pair, OUT + BLOCK, block[:, 128:256])
            else:
                stage[:, :384] = grad
                put(stage.at[:, pl.ds(0, 384)], gsquare_ref.at[pl.ds(3 * D, D), pl.ds(384 * pair, 384)])

    def context_back():
        for r in range(packs):
            rows = slice(LEN * r, LEN * (r + 1))
            turned[3 * D :, rows] = product_right(square[:, 3 * D :], branch[rows, :]).astype(jnp.bfloat16)
        for r in range(packs):
            rows = slice(LEN * r, LEN * (r + 1))
            branch[rows, :] = product_right(branch[rows, :], square[:, 3 * D :]).astype(jnp.bfloat16)

    def unit_of(j, step):
        i, p = j // (packs // 2), 2 * (j % (packs // 2))
        return (i + (i + 1) // 2 if step == "T" else 3 * i + 1), p

    def prob_copy(j, step):
        h, p = unit_of(j, step)
        return pltpu.make_async_copy(prob_in.at[pl.ds(p, 2), pl.ds(2 * h, 2)], prob.at[j % 3], prob_sem.at[j % 3])

    def attend(j, step, count):
        h, p = unit_of(j, step)
        pl.when(j + 2 < count)(lambda: prob_copy(j + 2, step).start())
        prob_copy(j, step).wait()
        tile = pl.multiple_of(128 * h, 128)
        left = left_half((LEN, 128))
        at = [[pl.ds(pl.multiple_of(D * i + tile + 64 * side, 64), 64) for i in range(4)] for side in range(2)]
        parts = []
        for q in range(2):
            rows = pl.ds(pl.multiple_of((p + q) * LEN, LEN), LEN)
            context = branch[rows, pl.ds(tile, 128)]
            all_values = up[pl.ds(pl.multiple_of(2 * D + tile, 128), 128), rows]
            for side in range(2):
                mine = left if side == 0 else jnp.logical_not(left)
                d_prob = product(jnp.where(mine, context, jnp.zeros_like(context)), all_values)
                low = prob[j % 3, q, side]
                share = low.astype(jnp.float32)
                moved = share * d_prob
                d_scores = (moved - share * jnp.sum(moved, axis=1, keepdims=True)).astype(jnp.bfloat16)
                d_values = product(turned[at[side][3], rows], low)
                d_query = product_right(up[at[side][1], rows], d_scores) * HEAD_DIM**-0.5
                d_keys = product(up[at[side][0], rows], d_scores) * HEAD_DIM**-0.5
                parts.append((side, rows, [item.astype(jnp.bfloat16) for item in (d_query, d_keys, d_values)]))
        for side, rows, items in parts:
            for i in range(3):
                up[at[side][i], rows] = items[i]

    def put_tiles(tiles, at):
        for i in range(3):
            for one, two in tiles:
                right = jnp.concatenate(
                    [up[D * i + 128 * one : D * i + 128 * (one + 1), :], up[D * i + 128 * two : D * i + 128 * (two + 1), :]]
                )
                grad = product_right(turned[0:D, :], right)
                if direct:
                    for d in range(GRID[0]):
                        block = grad[BLOCK * d : BLOCK * (d + 1)]
                        if len(tiles) == 2:
                            take_main(part, d, one // 3, at + BLOCK * i, block[:, :128], block[:, 128:])
                        else:
                            take_rest(part, d, 0, at + BLOCK // 2 * i, block[:, :128])
                            take_rest(part, d, 1, at + BLOCK // 2 * i, block[:, 128:])
                else:
                    for k, tile in enumerate((one, two)):
                        stage[:, :128] = grad[:, 128 * k : 128 * (k + 1)]
                        put(stage.at[:, pl.ds(0, 128)], gsquare_ref.at[pl.ds(D * i, D), pl.ds(128 * tile, 128)])

    def put_vectors():
        ones = jnp.ones((8, rows_all), jnp.bfloat16)
        sums[0:1, :D] = product_right(ones, up[0:D, :])[0:1]
        sums[1:2, :D] = product_right(ones, up[2 * D : 3 * D, :])[0:1]
        if direct:
            lane = lax.broadcasted_iota(jnp.int32, (1, 128), 1)
            value = jnp.zeros((1, 128), jnp.float32)
            for p in range(packs):
                value = jnp.where(lane == narrow * packs + p, value_ref[p : p + 1, :], value)
            high = value.astype(jnp.bfloat16).astype(jnp.float32)
            zeros = jnp.zeros((3, 128), jnp.float32)
            for d in range(GRID[0]):
                at, shift = divmod(BLOCK * d, 128)
                wide = sums[:, 128 * at : 128 * at + 256]
                wide = pltpu.roll(wide, 256 - shift, 1) if shift else wide
                mine = lax.broadcasted_iota(jnp.int32, (8, 128), 1) < BLOCK
                own = jnp.where(dp == d, 1.0, 0.0)
                tile = jnp.concatenate(
                    [jnp.where(mine, wide[:8, :128], 0.0), bup[3 * d : 3 * d + 3, :], high * own, (value - high) * own, zeros]
                )
                for n in range(GRID[1]):
                    part[d // 2, d % 2, n // 2, n % 2, 0:16, :] = tile.astype(jnp.bfloat16)

    def widen_back(r):
        rows = pl.ds(pl.multiple_of(r * LEN, LEN), LEN)
        value = product(square[:, :D], up[:D, rows])
        for i in (1, 2):
            value = value + product(square[:, D * i : D * (i + 1)], up[D * i : D * (i + 1), rows])
        norm[rows, :] = flow[rows, :] + jnp.transpose(value)

    after = split_order(BACKWARD_ORDER)

    def tick(mark, index=None):
        if not direct:
            return
        for name, pieces in after.items():
            if name[:1] == mark and pieces:
                if index is None:
                    for piece in pieces:
                        g.do(*piece)
                else:

                    @pl.when(index == int(name[1:]))
                    def _():
                        for piece in pieces:
                            g.do(*piece)

    def repeat(mark, first, last, body):
        def step(i, carry):
            body(i)
            tick(mark, i)
            return carry

        lax.fori_loop(first, last, step, 0)

    def up_pair(t):
        put_up(t, 0)
        put_up(t, 1)

    def down_three(i):
        for j in range(3):
            narrow_down(3 * i + j)

    groups = []
    for name in [name for name in after if name]:
        if groups and groups[-1][0] == name[0]:
            groups[-1][1].append(int(name[1:]))
        else:
            groups.append((name[0], [int(name[1:] or 0)]))
    for mark, span in groups:
        first, last = span[0], span[-1] + 1
        if mark == "D":
            need("turned branch", "act")
            load("branch", (branch_in, branch))
            load("down", (down_in, square))
            load("slope", (slope_in, slope))
            load("up", *[(up_in.at[:, pl.ds(rows_all * i, rows_all)], up.at[pl.ds(D * i, D), :]) for i in range(3)])
            load("flow", (second_in, flow))
            load("norm", (norm_in, norm))
            load("recip", (recip_in, recip))
            repeat("D", first, last, put_down)
            load("turned", (turned_in, turned.at[pl.ds(0, 3 * D), :]))
        elif mark == "N":
            need("branch", "down", "slope")
            repeat("N", first, last, down_three)
            load("square", (square_in, square))
        elif mark == "U":
            need("turned")
            repeat("U", first, last, up_pair)
        elif mark == "B":
            need("up", "flow", "norm", "recip")
            repeat("B", first, last, norm_back)
            load("qkv", (qkv_in, up))
            for j in range(2):
                prob_copy(j, "T").start()
        elif mark == "O":
            need("turned", "square")
            put_out()
            context_back()
            tick("O")
        elif mark == "T":
            need("qkv")
            repeat("T", first, last, lambda j: attend(j, "T", 2 * packs))
            for j in range(2):
                prob_copy(j, "X").start()
        elif mark == "M":
            put_tiles(((0, 2), (3, 5)), MAIN)
            tick("M")
        elif mark == "X":
            repeat("X", first, last, lambda j: attend(j, "X", packs))
        elif mark == "R":
            put_tiles(((1, 4),), REST)
            put_vectors()
            tick("R")
        elif mark == "W":
            repeat("W", first, last, widen_back)
            result = pltpu.make_async_copy(norm, grad_in_out, out_sem.at[1])
            result.start()
    if direct:
        for k in range(len(SCATTER_ROWS)):
            g.drain(k)
    else:
        gvec_ref[...] = sums[...]
        gbup_ref[...] = bup[...]
    result.wait()


def backward_step(direct, operands, dp, narrow):
    rows = operands[1].shape[0]
    vmem = pl.BlockSpec(memory_space=pltpu.VMEM)
    anywhere = pl.BlockSpec(memory_space=pl.ANY)
    full = lambda *shape: jax.ShapeDtypeStruct(shape, jnp.float32)
    room = lambda *shape: pltpu.VMEM(shape, jnp.bfloat16)
    wide = lambda *shape: pltpu.VMEM(shape, jnp.float32)
    if direct:
        outs, places = [full(TOTAL, 128)], [vmem]
        depth = dp // 2
        count = len(SCATTER_ROWS)
        extra = [
            room(depth, 2, 2, 2, TOTAL, 128), room(depth, 2, 2, TOTAL, 128), room(depth, 2, TOTAL, 128),
            room(depth, TOTAL, 128), room(depth - 1, TOTAL, 128),
            pltpu.SemaphoreType.DMA((count, 12)), pltpu.SemaphoreType.DMA((count, 12)),
        ]
    else:
        outs = [full(FF, D), full(D, FF), full(D, FF), full(16, 896), full(32, 128)]
        places = [anywhere] * 3 + [vmem] * 2
        extra = [wide(D, D)]
    return pl.pallas_call(
        functools.partial(backward_kernel, direct),
        name="backward",
        out_shape=(full(rows, D), *outs),
        in_specs=[anywhere] * 5 + [vmem] + [anywhere] * 8 + [vmem] * 2,
        out_specs=(anywhere, *places),
        scratch_shapes=[
            room(FF, rows), room(rows, FF), room(D, FF), room(3 * D, rows), wide(rows, D), wide(rows, D), wide(rows, 128),
            room(rows, D), room(D, rows), room(3, 2, 2, LEN, LEN), wide(16, 896), wide(32, 128),
            pltpu.SemaphoreType.DMA((20,)), pltpu.SemaphoreType.DMA((3,)), pltpu.SemaphoreType.DMA((2,)),
            *extra,
        ],
        compiler_params=pltpu.CompilerParams(
            vmem_limit_bytes=VMEM_LIMIT, **(dict(collective_id=1, has_side_effects=True) if direct else {})
        ),
    )(*operands)


def collect_kernel(packs_all, total, group_in, grad_in, *refs):
    (group_out, loss, grad_out, gq, gqb, gk, gv, gvb, go, gob, gfg, gfs, gup, gupb, gdown, gdownb, gsg, gss, group, grad, in_sem, out_sem) = refs
    parts = [(group_in, group, group_out, i) for i in range(group.shape[0] // LEN)]
    parts += [(grad_in, grad, grad_out, i) for i in range(grad.shape[0] // LEN)]
    ins, outs = [], []
    for k, (src, via, dst, i) in enumerate(parts):
        rows = pl.ds(LEN * i, LEN)
        ins.append(pltpu.make_async_copy(src.at[rows, :], via.at[rows, :], in_sem.at[k]))
        outs.append(pltpu.make_async_copy(via.at[rows, :], dst.at[rows, :], out_sem.at[k]))
        ins[-1].start()
    odd = lax.rem(lax.axis_index("narrow"), 2) == 1
    for one, two in zip(ins, outs):
        one.wait()
        two.start()
    for i, ref in enumerate((gqb, gvb, gob, gfg, gfs, gdownb, gsg, gss)):
        ref[...] = total[i : i + 1, :BLOCK]
    gupb[...] = total[8:11, :]
    loss[...] = (total[11:12, :] + total[12:13, :])[:, :packs_all]
    for t in range(6):
        gup[:, 128 * t : 128 * (t + 1)] = total[UP + BLOCK * t : UP + BLOCK * (t + 1), :]
    for ref, main, rest in (
        (gq, MAIN, REST), (gk, MAIN + BLOCK, REST + BLOCK // 2), (gv, MAIN + 2 * BLOCK, REST + BLOCK), (go, OUT, OUT + BLOCK),
    ):
        block = unpack_block(total[main : main + BLOCK, :], total[rest : rest + BLOCK // 2, :], odd)
        ref[...] = block[:, :192]
    for t in range(3):
        gdown[:, 128 * t : 128 * (t + 1)] = total[DOWN + SIDE * t : DOWN + SIDE * (t + 1), :]
    for copy in outs:
        copy.wait()


def collect_step(total, group, grad_inputs, dp, narrow):
    packs_all = group.shape[0] // LEN
    vmem = pl.BlockSpec(memory_space=pltpu.VMEM)
    anywhere = pl.BlockSpec(memory_space=pl.ANY)
    full = lambda *shape: jax.ShapeDtypeStruct(shape, jnp.float32)
    square, vector = full(D // dp, D // narrow), full(1, D // dp)
    count = (group.shape[0] + grad_inputs.shape[0]) // LEN
    out = pl.pallas_call(
        functools.partial(collect_kernel, packs_all),
        name="collect",
        out_shape=(
            jax.ShapeDtypeStruct(group.shape, group.dtype), full(1, packs_all), full(*grad_inputs.shape),
            square, vector, square, square, vector, square, vector, vector, vector,
            full(D // dp, FF // narrow), full(FF // dp // 128, 128), full(D // narrow, FF // dp), vector, vector, vector,
        ),
        in_specs=[vmem, anywhere, anywhere],
        out_specs=(anywhere, vmem, anywhere) + (vmem,) * 15,
        scratch_shapes=[
            pltpu.VMEM(group.shape, group.dtype), pltpu.VMEM(grad_inputs.shape, jnp.float32),
            pltpu.SemaphoreType.DMA((count,)), pltpu.SemaphoreType.DMA((count,)),
        ],
        compiler_params=pltpu.CompilerParams(vmem_limit_bytes=VMEM_LIMIT),
    )(total, group, grad_inputs)
    out = [item.reshape(-1) if item.shape[0] in (1, 3) else item for item in out]
    out[14] = out[14].T
    return tuple(out)


def per_device(
    inputs,
    segments,
    row_kind,
    query_weight,
    query_bias,
    key_weight,
    value_weight,
    value_bias,
    output_weight,
    output_bias,
    first_gain,
    first_shift,
    up_weight,
    up_bias,
    down_weight,
    down_bias,
    second_gain,
    second_shift,
    out_cotangent,
    loss_cotangent,
):
    row_count = inputs.shape[0]
    matrices = (query_weight, key_weight, value_weight, output_weight, up_weight, down_weight)
    vectors = (
        query_bias,
        value_bias,
        output_bias,
        first_gain,
        first_shift,
        down_bias,
        second_gain,
        second_shift,
        up_bias,
    )
    dp, narrow = lax.axis_size("dp"), lax.axis_size("narrow")
    direct = (dp, narrow, row_count) == (*GRID, 4 * LEN)
    if direct:
        weights = (*matrices[:5], down_weight.T, *[item.reshape(1, -1) for item in vectors[:8]], up_bias.reshape(-1, 128))
    else:
        weights = fetch_weights(matrices, vectors)
    (square, up, down, vecs, qkv, prob, turned, norm_first, recip_first, active, slope, output_low, norm_second,
     recip_second) = forward_step(direct, weights, inputs, segments, dp, narrow)
    group_out = lax.all_gather(output_low, "narrow", axis=0, tiled=True)
    partial_value, d_second, d_branch, branch_turned, sums_second = transport_step(
        output_low, segments, row_kind, loss_cotangent, out_cotangent, norm_second, recip_second, vecs
    )
    grad_inputs, *grads = backward_step(
        direct,
        (active, slope, d_branch, branch_turned, d_second, sums_second, turned.reshape(3 * D, row_count), norm_first, recip_first, qkv, prob, square,
         up.reshape(D, FF), down, vecs, partial_value),
        dp,
        narrow,
    )
    if direct:
        return collect_step(grads[0], group_out, grad_inputs, dp, narrow)
    transport_loss = lax.all_gather(partial_value[:, 0], "narrow", axis=0, tiled=True)
    squares, g_up, g_down, small, tiles = grads
    mats, vecs = reduce_grads([*squares.reshape(4, D, D), g_up, g_down.T], [*small[:8, :D], tiles[:24].reshape(FF)])
    return (
        group_out,
        transport_loss,
        grad_inputs,
        mats[0],
        vecs[0],
        mats[1],
        mats[2],
        vecs[1],
        mats[3],
        vecs[2],
        vecs[3],
        vecs[4],
        mats[4],
        vecs[8],
        mats[5],
        vecs[5],
        vecs[6],
        vecs[7],
    )


def solution(mesh):
    return jax.shard_map(
        per_device,
        mesh=mesh,
        in_specs=(
            P(("dp", "narrow"), None),
            P("dp", None),
            P("dp", None),
            P("dp", "narrow"),
            P("dp"),
            P("dp", "narrow"),
            P("dp", "narrow"),
            P("dp"),
            P("dp", "narrow"),
            P("dp"),
            P("dp"),
            P("dp"),
            P("dp", "narrow"),
            P("dp"),
            P("dp", "narrow"),
            P("dp"),
            P("dp"),
            P("dp"),
            P(("dp", "narrow"), None),
            P("dp"),
        ),
        out_specs=(
            P("dp", None),
            P("dp"),
            P(("dp", "narrow"), None),
            P("dp", "narrow"),
            P("dp"),
            P("dp", "narrow"),
            P("dp", "narrow"),
            P("dp"),
            P("dp", "narrow"),
            P("dp"),
            P("dp"),
            P("dp"),
            P("dp", "narrow"),
            P("dp"),
            P("dp", "narrow"),
            P("dp"),
            P("dp"),
            P("dp"),
        ),
        check_vma=False,
    )
```

time: 300 us -> 241 us (0.80)
  Pallas kernels: 251 us -> 222 us
  local copies, waits for them, and re-layouts: 24.2 us -> 0 us
  blocking collectives: 6.37 us -> 0 us
    pallas_call x1, Pallas kernels: 112 us -> 93.1 us  [forward_step(): pl.pallas_call(functools.partial(forward_kernel, direct), name='forward',...]
    pallas_call x1, Pallas kernels: 113 us -> 94.3 us  [backward_step(): pl.pallas_call(functools.partial(backward_kernel, direct), name='backward...]
    unnamed x28 -> x0, local copies, waits for them, and re-layouts: 15.4 us -> none
    pallas_call x0 -> x1, Pallas kernels: none -> 9.61 us  [collect_step(): pl.pallas_call(functools.partial(collect_kernel, packs_all), name='collec...]
    all_gather x1 -> x0, blocking collectives: 6.37 us -> none  [per_device(): lax.all_gather(partial_value[:, 0], 'narrow', axis=0, tiled=True)]
  transfers between devices with their start and end apart: 1 -> 1, of which waited for: 0 -> 0; matrix products, arithmetic and copies ran while one was open for 2% -> 0% of each run, Pallas kernels for 47% -> 50%
where the time goes in v3:
time: 241 us; the launch traced here: 236 us
  Pallas kernels  222 us (92%)
  between operations  14.3 us (6%)
    pallas_call x1, Pallas kernels, backward_step(): pl.pallas_call(functools.partial(backward_kernel, direct), name='backward...  94.3 us
    pallas_call x1, Pallas kernels, forward_step(): pl.pallas_call(functools.partial(forward_kernel, direct), name='forward',...  93.1 us
    pallas_call x1, Pallas kernels, transport_step(): pl.pallas_call(transport_kernel, name='transport', out_shape=(jax.ShapeDt...  24.7 us
    pallas_call x1, Pallas kernels, collect_step(): pl.pallas_call(functools.partial(collect_kernel, packs_all), name='collec...  9.61 us
  transfers between devices with their start and end apart: 1, of which 0 were waited for; matrix products, arithmetic and copies ran while one was open for 0% of the time, Pallas kernels for 50%

profile of v3, /device:TPU:0, one launch (start us, length us, event | category | flops | bytes accessed | tf_op | source)
XLA Modules:
  0.0 236.1 jit_solution(38663074363505549)
XLA Ops:
  7.2 0.0 all-gather.2.cloned.1.call-start
  7.2 93.1 %forward.1 = (bf16[768,3072]{1,0:T(8,128)(2,1)}, bf16[4,2,96,3072]{3,2,1,0:T(8,128)(2,1)}, bf16[768,3072]{1,0:T(8,128)(2,1)}, f32[16,896]{1,0:T(8,128)}, bf16[23...) custom-call(bf16[96,192]{1,0:T(8,128)(2,1)} %refs_0_.1, ...), custom_call_target="tpu_custom_call" | custom-call | tf_op jit(solution)/shard_map/forward/pallas_call | solution.py:601
  100.4 0.0 all-gather.2.cloned.1.call-update
  100.4 24.7 %transport.1 = (f32[4,128]{1,0:T(4,128)}, f32[1024,768]{1,0:T(8,128)}, bf16[1024,768]{1,0:T(8,128)(2,1)}, bf16[768,1024]{1,0:T(8,128)(2,1)}, f32[8,768]{1,0:T(8,128)}) custom-call(bf16[1024,768]{1,0:T(8,128)(2,1)} %get-tuple-element.59.mixed_ref, s32[16,256]{1,0:T(8,128)} %seg_ref.1, s32[16,256]{1,0:T(8,128)} %kind_ref.1, f32[16]{0:T(128)} %weight_ref.1, ...), custom_call_target="tpu_custom_call" | custom-call | tf_op jit(solution)/shard_map/transport/pallas_call | solution.py:786
  125.1 94.3 %backward.1 = (f32[1024,768]{1,0:T(8,128)}, f32[1744,128]{1,0:T(8,128)}) custom-call(bf16[1024,3072]{1,0:T(8,128)(2,1)} %get-tuple-element.57.refs_0_, bf16[1024,3072]{1,0:T(8,128)(2,1)} %get-tuple-element.58.refs_1_, bf16[1024,768]{1,0:T(8,128)(2,1)} %get-tuple-element.63.refs_2_, bf16[768,1024]{1,0:T(8,128)(2,1)} %get-tuple-element.64.refs_3_, ...), custom_call_target="tpu_custom_call" | custom-call | tf_op jit(solution)/shard_map/backward/pallas_call | solution.py:1318
  219.4 0.0 all-gather.2.cloned.1.call-done.group_in
  219.4 9.6 %collect.1 = (bf16[4096,768]{1,0:T(8,128)(2,1)}, f32[1,16]{1,0:T(1,128)}, f32[1024,768]{1,0:T(8,128)}, f32[96,192]{1,0:T(8,128)}, f32[1,96]{1,0:T(1,128)}, /*ind...) custom-call(f32[1744,128]{1,0:T(8,128)} %get-tuple-element.76.total,, ...), custom_call_target="tpu_custom_call" | custom-call | tf_op jit(solution)/shard_map/collect/pallas_call | solution.py:1374
Async XLA Ops:
  7.2 212.2 %all-gather.2.cloned.1.call-start = ((), (), s32[]{:S(2)}) async-start(), calls=%async_computation | async-start | bytes 7864320 | tf_op jit(solution)/shard_map/all_gather | solution.py:1438
Sparse Core Ops, SparseCore 0:
  100.5 57.0 all-gather.1
